TPU v7x, 32 devices: a whole 2x2x4 slice. The times are simulated.
32 devices in a mesh: tile: 8 (over y, x, core), chan: 4 (over z).
Axes of the slice: x: 2, y: 2, z: 4, core: 2. Of those that a mesh axis runs over, the one named last changes fastest.
Arguments:
- features: bfloat16 [64, 1536, 128], P('tile', 'chan'), may hold values from -8 to 8
- dw_weight: float32 [1536, 49], P('chan'), may hold values from -2.5 to 2.5
- dw_bias: float32 [1536], P('chan'), may hold values from -3 to 3
- ln_gain: float32 [1536], replicated, may hold values from 0.5 to 1.5
- ln_bias: float32 [1536], replicated, may hold values from -2 to 2
- w_in: bfloat16 [1536, 6144], P('tile', 'chan'), may hold values from -0.15625 to 0.15625
- b_in: float32 [6144], P('chan'), may hold values from -3 to 3
- w_out: bfloat16 [6144, 1536], P('chan', 'tile'), may hold values from -0.109375 to 0.109375
- b_out: float32 [1536], P('chan'), may hold values from -3 to 3
- gamma: float32 [1536], P('chan'), may hold values from 0.5 to 2
Outputs:
- block_out: bfloat16 [64, 1536, 128], P('tile', 'chan')
All inputs are finite; a program needn't handle non-finite values.
Results may differ from a plain program's by a relative error of at most 0.015.
Values may be sent and summed in bfloat16 or wider, within the bound.
No kernel may reach another device: no remote copies, remote signals or barrier semaphores. Data moves between devices by JAX's collectives and lax.ppermute only.
A program may use at most 64 MiB of HBM per device.

v0:
```python
import jax
import jax.numpy as jnp
from jax import lax
from jax.sharding import PartitionSpec as P


def extended(block, sides, width):
    for axis, dim in sides:
        count = lax.axis_size(axis)
        forward = [(i, i + 1) for i in range(count - 1)]
        backward = [(target, source) for source, target in forward]
        low = lax.ppermute(
            lax.slice_in_dim(block, block.shape[dim] - width, None, axis=dim), axis, forward
        )
        high = lax.ppermute(lax.slice_in_dim(block, 0, width, axis=dim), axis, backward)
        block = jnp.concatenate([low, block, high], axis=dim)
    return block


def local(features, dw_weight, dw_bias, ln_gain, ln_bias, w_in, b_in, w_out, b_out, gamma):
    row_count, slab_width, column_count = features.shape
    chan_count = lax.axis_size("chan")
    total_channels = slab_width * chan_count
    with_rims = extended(features, (("tile", 0),), 3)
    padded = jnp.pad(with_rims.astype(jnp.float32), ((0, 0), (0, 0), (3, 3)))
    convolved = (
        jnp.zeros((row_count, slab_width, column_count), jnp.float32) + dw_bias[None, :, None]
    )
    kernel_side = 7
    for tap_row in range(kernel_side):
        for tap_col in range(kernel_side):
            window = padded[tap_row : tap_row + row_count, :, tap_col : tap_col + column_count]
            convolved = (
                convolved + window * dw_weight[:, tap_row * kernel_side + tap_col][None, :, None]
            )
    conv_out = convolved.astype(jnp.bfloat16)
    values = conv_out.astype(jnp.float32)
    offset = lax.axis_index("chan") * slab_width
    gain_slab = lax.dynamic_slice_in_dim(ln_gain, offset, slab_width)
    shift_slab = lax.dynamic_slice_in_dim(ln_bias, offset, slab_width)
    channel_total = lax.psum(jnp.sum(values, axis=1), "chan")
    centered = values - (channel_total / total_channels)[:, None, :]
    square_total = lax.psum(jnp.sum(centered * centered, axis=1), "chan")
    variance = (square_total / total_channels)[:, None, :]
    normed_slab = (
        centered * lax.rsqrt(variance + 1e-06) * gain_slab[None, :, None]
        + shift_slab[None, :, None]
    ).astype(jnp.bfloat16)
    gathered = lax.all_gather(normed_slab, "chan", axis=1, tiled=True)
    pre_act = jnp.einsum(
        "rcw,cf->rwf",
        gathered,
        lax.all_gather(w_in, "tile", axis=0, tiled=True),
        preferred_element_type=jnp.float32,
    )
    hidden = jax.nn.gelu(pre_act + b_in[None, None, :], approximate=False).astype(jnp.bfloat16)
    partial_out = jnp.einsum(
        "rwf,fc->rwc",
        hidden,
        lax.all_gather(w_out, "tile", axis=1, tiled=True),
        preferred_element_type=jnp.float32,
    )
    summed = lax.psum_scatter(
        partial_out.astype(jnp.bfloat16), "chan", scatter_dimension=2, tiled=True
    ).astype(jnp.float32)
    projected = jnp.transpose(summed + b_out[None, None, :], (0, 2, 1))
    return (features.astype(jnp.float32) + gamma[None, :, None] * projected).astype(jnp.bfloat16)


def solution(mesh):
    placed = (
        P("tile", "chan", None),
        P("chan", None),
        P("chan"),
        P(),
        P(),
        P("tile", "chan"),
        P("chan"),
        P("chan", "tile"),
        P("chan"),
        P("chan"),
    )
    return jax.shard_map(
        local, mesh=mesh, in_specs=placed, out_specs=P("tile", "chan", None), check_vma=False
    )
```

profile of v0, /device:TPU:8, one launch (start us, length us, event | category | flops | bytes accessed | tf_op | source)
XLA Modules:
  0.0 299.4 jit_solution(5800990849390864275)
XLA Ops:
  6.5 1.5 copy.16
  8.1 0.1 fusion.156
  8.2 1.8 collective-permute-start
  9.9 1.3 collective-permute-start.1
  11.2 0.7 slice_reduce_fusion.46
  11.9 1.4 dynamic_slice.6
  13.3 1.4 dynamic_slice.7
  14.6 0.7 slice_reduce_fusion.47
  15.3 0.7 slice_reduce_fusion.48
  16.0 0.7 copy-done.2
  16.7 1.3 maximum_convert_fusion
  18.0 14.0 %convert_reduce_fusion = (f32[8,128]{1,0:T(8,128)S(1)}, bf16[8,384,128]{1,2,0:T(8,128)(2,1)S(1)}) fusion(f32[384]{0:T(512)} %get-tuple-element.54, f32[384]{0:T(512)} %get-tuple-element.55, f32[384]{0:T(512)} %get-tuple-element.8, f32[384]{0:T(512)} %get-tuple-element.9, f32[14,384,128]{1,2,0:T(8,128)S(1)} %maximum_convert_fusion, f32[384]{0:T(512)} %get-tuple-element.10, ...), kind=kLoop, calls=%fused_computation.60 | loop fusion | flops 39713792 | bytes 14631424 | tf_op jit(solution)/shard_map/reduce_sum | solution.py:41
  32.0 9.0 %psum.14 = f32[8,128]{1,0:T(8,128)S(1)} all-reduce(f32[8,128]{1,0:T(8,128)S(1)} %get-tuple-element.56), channel_id=1, replica_groups=mesh['tile'=8,'chan'=4] {'chan'}, use_global_device_ids=true, to_apply=%region_1.2 | all-reduce | flops 1024 | bytes 8192 | tf_op jit(solution)/shard_map/psum | solution.py:41
  41.0 0.5 fusion.50
  41.5 11.7 %psum.15 = f32[8,128]{1,0:T(8,128)S(1)} all-reduce(f32[8,128]{1,0:T(8,128)S(1)} %fusion.50), channel_id=1, replica_groups=mesh['tile'=8,'chan'=4] {'chan'}, use_global_device_ids=true, to_apply=%region_3.4 | all-reduce | flops 1024 | bytes 8192 | tf_op jit(solution)/shard_map/psum | solution.py:43
  53.2 2.0 fusion.53
  55.2 0.0 all-gather.6.cloned.1.call-start
  55.3 0.7 all-gather.6.cloned.1.call-update
  56.0 0.7 all-gather.8.cloned.1.call-update
  56.7 0.2 reduce-scatter.4.cloned.1.call-start
  57.0 61.8 %all-gather.4.cloned.1.call-done = bf16[8,1536,128]{1,2,0:T(8,128)(2,1)} async-done(((bf16[8,384,128]{1,2,0:T(8,128)(2,1)}), bf16[8,1536,128]{1,2,0:T(8,128)(2,1)}) %all-gather.4.cloned.1.call-update) | async-done | bytes 3145744 | tf_op jit(solution)/shard_map/all_gather | solution.py:49
  118.8 41.1 %all-gather.6.cloned.1.call-done = bf16[1536,1536]{1,0:T(8,128)(2,1)} async-done(((bf16[192,1536]{1,0:T(8,128)(2,1)}), bf16[1536,1536]{1,0:T(8,128)(2,1)}) %all-gather.6.cloned.1.call-update) | async-done | bytes 4718608 | tf_op jit(solution)/shard_map/all_gather | solution.py:53
  159.9 11.2 %fusion.121 = (u8[128,1536]{1,0:T(8,128)(4,1)S(1)}, u8[128,1536]{1,0:T(8,128)(4,1)S(1)}, f32[8,128,1536]{2,1,0:T(8,128)}) fusion(f32[1536]{0:T(1024)S(1)} %copy-done.6, bf16[8,1536,128]{1,2,0:T(8,128)(2,1)} %all-gather.4.cloned.1.call-done, bf16[1536,1536]{1,0:T(8,128)(2,1)} %all-gather.6.cloned.1.call-done), kind=kOutput, calls=%fused_computation.157 | convolution fusion | flops 4853465088 | bytes 14555136 | tf_op jit(solution)/shard_map/rcw,cf->rwf/dot_general | solution.py:50
  171.1 29.6 %all-gather.8.cloned.1.call-done = bf16[1536,1536]{0,1:T(8,128)(2,1)} async-done(((bf16[1536,192]{0,1:T(8,128)(2,1)}), bf16[1536,1536]{0,1:T(8,128)(2,1)}) %all-gather.8.cloned.1.call-update) | async-done | bytes 4718608 | tf_op jit(solution)/shard_map/all_gather | solution.py:60
  200.7 22.5 %fusion.13 = bf16[8,128,1536]{2,1,0:T(8,128)(2,1)} fusion(bf16[1536,1536]{0,1:T(8,128)(2,1)} %all-gather.8.cloned.1.call-done, f32[8,128,1536]{2,1,0:T(8,128)} %get-tuple-element.60, f32[1536]{0:T(1024)S(1)} %copy-done.6, u8[128,1536]{1,0:T(8,128)(4,1)S(1)} %get-tuple-element.6, u8[128,1536]{1,0:T(8,128)(4,1)S(1)} %get-tuple-element.5), kind=kOutput, calls=%fused_computation.26 | convolution fusion | flops 4945084416 | bytes 14555136 | tf_op jit(solution)/shard_map/rwf,fc->rwc/dot_general | solution.py:57
  223.2 3.8 %copy.21 = bf16[8,128,1536]{1,0,2:T(8,128)(2,1)S(1)} copy(bf16[8,128,1536]{2,1,0:T(8,128)(2,1)} %fusion.13) | data formatting | bytes 6291456
  227.0 2.5 copy.26
  229.5 59.9 %reduce-scatter.4.cloned.1.call-done = bf16[384,1024]{1,0:T(8,128)(2,1)} async-done(((bf16[1536,1024]{1,0:T(8,128)(2,1)}), bf16[384,1024]{1,0:T(8,128)(2,1)}) %reduce-scatter.4.cloned.1.call-update) | async-done | bytes 786448
  289.5 1.4 copy.24
  290.9 0.6 copy.22
  291.4 0.3 fusion.101
  291.7 1.2 copy.20
  (21 shorter events, 0.1 us)
Async XLA Ops:
  6.5 4.7 %copy-start.3 = (f32[384,49]{0,1:T(8,128)S(1)}, f32[384,49]{0,1:T(8,128)}, u32[]{:S(2)}) copy-start(f32[384,49]{0,1:T(8,128)} %param.11) | copy-start | bytes 225796
  6.5 112.2 %all-gather.4.cloned.1.call-start = ((), (), s32[]{:S(2)}) async-start(), calls=%async_computation.1 | async-start | bytes 3932160 | tf_op jit(solution)/shard_map/all_gather | solution.py:49
  8.1 9.9 %copy-start = (bf16[8,384,128]{1,2,0:T(8,128)(2,1)}, bf16[8,384,128]{1,2,0:T(8,128)(2,1)S(1)}, u32[]{:S(2)}) copy-start(bf16[8,384,128]{1,2,0:T(8,128)(2,1)S(1)} %copy.16) | copy-start | bytes 2359300
  8.2 7.8 %collective-permute-start = (bf16[3,384,128]{1,2,0:T(8,128)(2,1)S(1)}, bf16[3,384,128]{1,2,0:T(8,128)(2,1)S(1)}, u32[]{:S(2)}, u32[]{:S(2)}) collective-permute-start(bf16[3,384,128]{1,2,0:T(8,128)(2,1)S(1)} %get-tuple-element.58), channel_id=1, source_target_pairs={{0,4},{4,8},{8,12},{12,16},{16,20},{20,24},{24,28},{1,5},{5,9},{9,... | collective-permute-start | bytes 884744 | tf_op jit(solution)/shard_map/ppermute | solution.py:12
  9.9 6.8 %collective-permute-start.1 = (bf16[3,384,128]{1,2,0:T(8,128)(2,1)S(1)}, bf16[3,384,128]{1,2,0:T(8,128)(2,1)}, u32[]{:S(2)}, u32[]{:S(2)}) collective-permute-start(bf16[3,384,128]{1,2,0:T(8,128)(2,1)S(1)} %get-tuple-element.59), channel_id=1, source_target_pairs={{4,0},{8,4},{12,8},{16,12},{20,16},{24,20},{28,24},{5,1},{9,5},{13... | collective-permute-start | bytes 884744 | tf_op jit(solution)/shard_map/ppermute | solution.py:15
  16.0 0.7 copy-start.2
  53.2 106.6 %copy-start.6 = (f32[1536]{0:T(1024)S(1)}, f32[1536]{0:T(1024)}, u32[]{:S(2)}) copy-start(f32[1536]{0:T(1024)} %param.16) | copy-start | bytes 18436
  55.2 104.6 %all-gather.6.cloned.1.call-start = ((), (), s32[]{:S(2)}) async-start(), calls=%async_computation.2 | async-start | bytes 5308416 | tf_op jit(solution)/shard_map/all_gather | solution.py:53
  56.0 144.7 %all-gather.8.cloned.1.call-start = ((), (), s32[]{:S(2)}) async-start(), calls=%async_computation.3 | async-start | bytes 5308416 | tf_op jit(solution)/shard_map/all_gather | solution.py:60
  56.7 232.7 %reduce-scatter.4.cloned.1.call-start = ((), (), s32[]{:S(2)}) async-start(), calls=%async_computation.4 | async-start | bytes 3932160
  289.5 2.0 copy-start.1
  289.5 2.0 copy-start.4
  289.5 2.0 copy-start.5
Sparse Core Ops, SparseCore 0:
  55.4 63.3 all-gather.3
  120.7 39.1 all-gather.5
  161.7 38.9 all-gather.7
  229.6 59.7 reduce-scatter.3
where the time goes:
time: 302 us; the launch traced here: 299 us
  waiting for transfers between devices  194 us (64%)
  matrix products  33.7 us (11%)
  blocking collectives  20.7 us (7%)
  other arithmetic  18 us (6%)
  local copies, waits for them, and re-layouts  16.5 us (5%)
  between operations  13.3 us (4%)
  starting transfers between devices  3.35 us (1%)
    all_gather x1, waiting for transfers between devices, local(): gathered = lax.all_gather(normed_slab, 'chan', axis=1, tiled=True)  61.8 us
    unnamed x5, waiting for transfers between devices  61.3 us
    all_gather x1, waiting for transfers between devices, local(): lax.all_gather(w_in, 'tile', axis=0, tiled=True)  41.1 us
    all_gather x1, waiting for transfers between devices, local(): lax.all_gather(w_out, 'tile', axis=1, tiled=True)  29.6 us
    dot_general x1, matrix products, local(): jnp.einsum('rwf,fc->rwc', hidden, lax.all_gather(w_out, 'tile', axis=1, t...  22.5 us
    reduce_sum x1, other arithmetic, local(): channel_total = lax.psum(jnp.sum(values, axis=1), 'chan')  14 us
    psum x1, blocking collectives, local(): square_total = lax.psum(jnp.sum(centered * centered, axis=1), 'chan')  11.7 us
    dot_general x1, matrix products, local(): jnp.einsum('rcw,cf->rwf', gathered, lax.all_gather(w_in, 'tile', axis=0,...  11.2 us
  transfers between devices with their start and end apart: 6, of which 4 were waited for; matrix products, arithmetic and copies ran while one was open for 5% of the time, Pallas kernels for 0%

commit v1 on v0

v1 whole, which is shorter than its diff:
```python
import functools

import jax
import jax.numpy as jnp
from jax import lax
from jax.experimental import pallas as pl
from jax.experimental.pallas import tpu as pltpu
from jax.sharding import PartitionSpec as P

SIDE = 7
REACH = SIDE // 2
CHUNKS = 2
VMEM_LIMIT = 48 * 1024 * 1024
EPSILON = 1e-06


def conv_kernel(plan, *refs):
    sources, taps_ref, out_ref, held = refs[:-3], refs[-3], refs[-2], refs[-1]
    rows, channels, width = held.shape
    group = 16
    column = lax.broadcasted_iota(jnp.int32, (1, group, width), 2)

    def one_group(i, carry):
        at = pl.ds(pl.multiple_of(i * group, group), group)
        image = jnp.stack([sources[s][r, at, :] for s, r in plan]).astype(jnp.float32)
        taps = taps_ref[at, :]
        bias = taps[:, SIDE * SIDE : SIDE * SIDE + 1][None]
        total = jnp.broadcast_to(bias, (rows, group, width))
        for b in range(SIDE):
            part = None
            for a in range(SIDE):
                tap = SIDE * a + b
                term = image[a : a + rows] * taps[:, tap : tap + 1][None]
                part = term if part is None else part + term
            offset = b - REACH
            if offset:
                part = pltpu.roll(part, (-offset) % width, 2)
                inside = column < width - offset if offset > 0 else column >= -offset
                part = jnp.where(inside, part, 0.0)
            total = total + part
        held[:, at, :] = total
        return carry

    lax.fori_loop(0, channels // group, one_group, 0)
    for row in range(rows):
        out_ref[row] = held[row].T.astype(out_ref.dtype)


def conv_chunk(first, rows, low, features, high, taps):
    height, slab, width = features.shape
    names, plan = ["features"], []
    for row in range(first - REACH, first + rows + REACH):
        if row < 0:
            name, index = "low", row + REACH
        elif row < height:
            name, index = "features", row
        else:
            name, index = "high", row - height
        if name not in names:
            names.append(name)
        plan.append((names.index(name), index))
    arrays = [{"features": features, "low": low, "high": high}[name] for name in names]
    block = 128
    return pl.pallas_call(
        functools.partial(conv_kernel, tuple(plan)),
        grid=(slab // block,),
        in_specs=[pl.BlockSpec((a.shape[0], block, width), lambda i: (0, i, 0)) for a in arrays]
        + [pl.BlockSpec((block, taps.shape[1]), lambda i: (i, 0))],
        out_specs=pl.BlockSpec((rows, width, block), lambda i: (0, 0, i)),
        out_shape=jax.ShapeDtypeStruct((rows, width, slab), jnp.bfloat16),
        scratch_shapes=[pltpu.VMEM((rows, block, width), jnp.float32)],
        compiler_params=pltpu.CompilerParams(vmem_limit_bytes=VMEM_LIMIT),
        cost_estimate=pl.CostEstimate(
            flops=2 * SIDE * SIDE * rows * slab * width,
            bytes_accessed=4 * rows * slab * width,
            transcendentals=0,
        ),
        name="depthwise",
    )(*arrays, taps)


def line_places(z):
    low_half = z < 2
    return z ^ 1, jnp.where(low_half, 2, 1), jnp.where(low_half, 3, 0)


def mlp_kernel(*refs):
    own, near, mid_inner, mid_outer, far_inner, far_outer = refs[:6]
    w_in_parts, w_out_parts = refs[6:14], refs[14:22]
    gain_ref, shift_ref, b_in_ref = refs[22:25]
    out_refs = refs[25:29]
    x, w_in, w_out, hidden, x_sem, in_sem, out_sem = refs[29:]
    pixels, channels = x.shape
    slab = own.shape[1]
    units = hidden.shape[1]
    shard = w_in_parts[0].shape[0]
    z, t = lax.axis_index("chan"), lax.axis_index("tile")
    pair, mid, far = line_places(z)
    inner = jnp.logical_or(z == 1, z == 2)

    def slab_copy(part, place, sem):
        at = pl.ds(pl.multiple_of(place * slab, 128), slab)
        return pltpu.make_async_copy(part, x.at[:, at], x_sem.at[sem])

    slab_copy(own, z, 0).start()
    slab_copy(near, pair, 1).start()

    @pl.when(inner)
    def _():
        slab_copy(mid_inner, mid, 2).start()
        slab_copy(far_inner, far, 3).start()

    @pl.when(jnp.logical_not(inner))
    def _():
        slab_copy(mid_outer, mid, 2).start()
        slab_copy(far_outer, far, 3).start()

    def shard_copy(part, target, k, sems):
        at = pl.ds(pl.multiple_of((t ^ k) * shard, 16), shard)
        return pltpu.make_async_copy(part, target.at[at, :], sems.at[k])

    for k, part in enumerate(w_in_parts):
        shard_copy(part, w_in, k, in_sem).start()
    for k, part in enumerate(w_out_parts):
        shard_copy(part, w_out, k, out_sem).start()

    slab_copy(own, z, 0).wait()
    slab_copy(near, pair, 1).wait()
    slab_copy(mid_inner, mid, 2).wait()
    slab_copy(far_inner, far, 3).wait()

    step = 64
    gain, shift = gain_ref[...], shift_ref[...]

    def normalize(i, carry):
        at = pl.ds(pl.multiple_of(i * step, step), step)
        values = x[at, :].astype(jnp.float32)
        average = jnp.sum(values, axis=1, keepdims=True) * (1.0 / channels)
        centered = values - average
        variance = jnp.sum(centered * centered, axis=1, keepdims=True) * (1.0 / channels)
        x[at, :] = (centered * lax.rsqrt(variance + EPSILON) * gain + shift).astype(x.dtype)
        return carry

    lax.fori_loop(0, pixels // step, normalize, 0)

    for k, part in enumerate(w_in_parts):
        shard_copy(part, w_in, k, in_sem).wait()
    block = 256
    for f in range(0, units, block):
        pre_act = jnp.dot(x[...], w_in[:, f : f + block], preferred_element_type=jnp.float32)
        pre_act = pre_act + b_in_ref[:, f : f + block]
        gelu = pre_act * (lax.erf(pre_act * (0.5**0.5)) * 0.5 + 0.5)
        hidden[:, f : f + block] = gelu.astype(hidden.dtype)

    for k, part in enumerate(w_out_parts):
        shard_copy(part, w_out, k, out_sem).wait()
    for out_ref, place in zip(out_refs, (far, mid, pair, z), strict=True):
        rows, _, width = out_ref.shape
        at = pl.ds(pl.multiple_of(place * slab, 16), slab)
        partial = lax.dot_general(
            w_out[at, :], hidden[...], (((1,), (1,)), ((), ())), preferred_element_type=jnp.float32
        )
        for row in range(rows):
            out_ref[row] = partial[:, row * width : (row + 1) * width].astype(out_ref.dtype)


def mlp_chunk(slabs, w_in_parts, w_out_parts, gain, shift, b_in):
    rows, width, slab = slabs[0].shape
    shard, units = w_in_parts[0].shape
    channels = shard * len(w_in_parts)
    pixels = rows * width
    anywhere = pl.BlockSpec(memory_space=pl.ANY)
    whole = pl.BlockSpec(memory_space=pltpu.VMEM)
    return pl.pallas_call(
        mlp_kernel,
        in_specs=[anywhere] * (len(slabs) + len(w_in_parts) + len(w_out_parts)) + [whole] * 3,
        out_specs=[whole] * 4,
        out_shape=[jax.ShapeDtypeStruct((rows, slab, width), jnp.bfloat16)] * 4,
        scratch_shapes=[
            pltpu.VMEM((pixels, channels), jnp.bfloat16),
            pltpu.VMEM((channels, units), jnp.bfloat16),
            pltpu.VMEM((channels, units), jnp.bfloat16),
            pltpu.VMEM((pixels, units), jnp.bfloat16),
            pltpu.SemaphoreType.DMA((4,)),
            pltpu.SemaphoreType.DMA((len(w_in_parts),)),
            pltpu.SemaphoreType.DMA((len(w_out_parts),)),
        ],
        compiler_params=pltpu.CompilerParams(vmem_limit_bytes=VMEM_LIMIT),
        cost_estimate=pl.CostEstimate(
            flops=4 * pixels * channels * units,
            bytes_accessed=4 * channels * units + 4 * pixels * channels,
            transcendentals=pixels * units,
        ),
        name="mlp",
    )(
        *[s.reshape(pixels, slab) for s in slabs],
        *w_in_parts,
        *w_out_parts,
        gain[None],
        shift[None],
        b_in[None],
    )


PAIRS = [(0, 1), (1, 0), (2, 3), (3, 2)]
MIDDLE = [(1, 2), (2, 1)]
OUTWARD = [(1, 0), (2, 3)]
INWARD = [(0, 1), (3, 2)]


def gather_line(slab):
    near = lax.ppermute(slab, "chan", PAIRS)
    mid_inner = lax.ppermute(slab, "chan", MIDDLE)
    far_inner = lax.ppermute(near, "chan", MIDDLE)
    mid_outer = lax.ppermute(mid_inner, "chan", OUTWARD)
    far_outer = lax.ppermute(far_inner, "chan", OUTWARD)
    return slab, near, mid_inner, mid_outer, far_inner, far_outer


def add(a, b):
    return (a.astype(jnp.float32) + b.astype(jnp.float32)).astype(jnp.bfloat16)


def scatter_line(far, mid, near, own):
    far_in = lax.ppermute(far, "chan", INWARD)
    mid_in = lax.ppermute(mid, "chan", INWARD)
    far_across = lax.ppermute(add(far, far_in), "chan", MIDDLE)
    mid_across = lax.ppermute(add(mid, mid_in), "chan", MIDDLE)
    from_pair = lax.ppermute(add(near, far_across), "chan", PAIRS)
    return own.astype(jnp.float32) + mid_across.astype(jnp.float32) + from_pair.astype(jnp.float32)


def flipped(array, bit):
    return lax.ppermute(array, "tile", [(i, i ^ bit) for i in range(8)])


def gather_shards(w_in, w_out):
    in_x, in_y = flipped(w_in, 2), flipped(w_in, 4)
    out_x, out_y = flipped(w_out, 2), flipped(w_out, 4)
    in_xy, out_xy = flipped(in_x, 4), flipped(out_y, 2)
    ins, outs = [w_in, in_x, in_y, in_xy], [w_out, out_x, out_y, out_xy]
    ins = [part for mine in ins for part in (mine, flipped(mine, 1))]
    outs = [part for mine in outs for part in (mine, flipped(mine, 1))]
    return ins, outs


def rims(features):
    count = lax.axis_size("tile")
    forward = [(i, i + 1) for i in range(count - 1)]
    backward = [(b, a) for a, b in forward]
    low = lax.ppermute(features[-REACH:], "tile", forward)
    high = lax.ppermute(features[:REACH], "tile", backward)
    return low, high


def local(features, dw_weight, dw_bias, ln_gain, ln_bias, w_in, b_in, w_out, b_out, gamma):
    height = features.shape[0]
    low, high = rims(features)
    taps = jnp.concatenate([dw_weight, dw_bias[:, None]], axis=1)
    w_in_parts, w_out_parts = gather_shards(w_in, w_out.T)
    rows = height // CHUNKS
    results = []
    for first in range(0, height, rows):
        slab = conv_chunk(first, rows, low, features, high, taps)
        partials = mlp_chunk(gather_line(slab), w_in_parts, w_out_parts, ln_gain, ln_bias, b_in)
        projected = scatter_line(*partials) + b_out[None, :, None]
        block = features[first : first + rows].astype(jnp.float32)
        results.append((block + gamma[None, :, None] * projected).astype(jnp.bfloat16))
    return jnp.concatenate(results, axis=0)


def plain(features, dw_weight, dw_bias, ln_gain, ln_bias, w_in, b_in, w_out, b_out, gamma):
    rows, slab, width = features.shape
    low, high = rims(features)
    image = jnp.concatenate([low, features, high], axis=0).astype(jnp.float32)
    image = jnp.pad(image, ((0, 0), (0, 0), (REACH, REACH)))
    total = jnp.zeros((rows, slab, width), jnp.float32) + dw_bias[None, :, None]
    for a in range(SIDE):
        for b in range(SIDE):
            window = image[a : a + rows, :, b : b + width]
            total = total + window * dw_weight[:, a * SIDE + b][None, :, None]
    conv_out = lax.all_gather(total.astype(jnp.bfloat16), "chan", axis=1, tiled=True)
    values = conv_out.astype(jnp.float32)
    centered = values - jnp.mean(values, axis=1, keepdims=True)
    variance = jnp.mean(centered * centered, axis=1, keepdims=True)
    normed = centered * lax.rsqrt(variance + EPSILON) * ln_gain[None, :, None] + ln_bias[None, :, None]
    pre_act = jnp.einsum(
        "rcw,cf->rwf",
        normed.astype(jnp.bfloat16),
        lax.all_gather(w_in, "tile", axis=0, tiled=True),
        preferred_element_type=jnp.float32,
    )
    hidden = jax.nn.gelu(pre_act + b_in[None, None, :], approximate=False).astype(jnp.bfloat16)
    partial = jnp.einsum(
        "rwf,fc->rwc",
        hidden,
        lax.all_gather(w_out, "tile", axis=1, tiled=True),
        preferred_element_type=jnp.float32,
    )
    summed = lax.psum_scatter(
        partial.astype(jnp.bfloat16), "chan", scatter_dimension=2, tiled=True
    ).astype(jnp.float32)
    projected = jnp.transpose(summed + b_out[None, None, :], (0, 2, 1))
    return (features.astype(jnp.float32) + gamma[None, :, None] * projected).astype(jnp.bfloat16)


def solution(mesh):
    placed = (
        P("tile", "chan", None),
        P("chan", None),
        P("chan"),
        P(),
        P(),
        P("tile", "chan"),
        P("chan"),
        P("chan", "tile"),
        P("chan"),
        P("chan"),
    )
    cube = mesh.shape["tile"] == 8 and mesh.shape["chan"] == 4
    return jax.shard_map(
        local if cube else plain,
        mesh=mesh,
        in_specs=placed,
        out_specs=P("tile", "chan", None),
        check_vma=False,
    )
```

time: 302 us -> 164 us (0.54)
  waiting for transfers between devices: 194 us -> 56.7 us
  starting transfers between devices: 3.35 us -> 53.7 us
  Pallas kernels: 0 us -> 44 us
  matrix products: 33.7 us -> 0 us
  blocking collectives: 20.7 us -> 0 us
  other arithmetic: 18 us -> 4.35 us
  local copies, waits for them, and re-layouts: 16.5 us -> 3.01 us
  between operations: 13.3 us -> 0.51 us
    all_gather x3 -> x0, waiting for transfers between devices: 132 us -> none  [the longest x1 61.8 us: local(): gathered = lax.all_gather(normed_slab, 'chan', axis=1, tiled=True)]
    unnamed x5 -> x0, waiting for transfers between devices: 61.3 us -> none
    ppermute x2 -> x36, waiting for transfers between devices: 0.01 us -> 56.7 us  [the longest x2 10.7 us: gather_line(): far_inner = lax.ppermute(near, 'chan', MIDDLE)]
    ppermute x2 -> x36, starting transfers between devices: 3.05 us -> 53.7 us  [the longest x14 16.8 us: flipped(): return lax.ppermute(array, 'tile', [(i, i ^ bit) for i in range(8)])]
    pallas_call x0 -> x4, Pallas kernels: none -> 44 us  [the longest x2 25.7 us: conv_chunk(): pl.pallas_call(functools.partial(conv_kernel, tuple(plan)), grid=(slab //...]
    dot_general x2 -> x0, matrix products: 33.7 us -> none  [the longest x1 22.5 us: local(): jnp.einsum('rwf,fc->rwc', hidden, lax.all_gather(w_out, 'tile', axis=1, t...]
    psum x2 -> x0, blocking collectives: 20.7 us -> none  [the longest x1 11.7 us: local(): square_total = lax.psum(jnp.sum(centered * centered, axis=1), 'chan')]
    reduce_sum x2 -> x0, other arithmetic: 14.5 us -> none  [the longest x1 14 us: local(): channel_total = lax.psum(jnp.sum(values, axis=1), 'chan')]
  transfers between devices with their start and end apart: 6 -> 36, of which waited for: 4 -> 13; matrix products, arithmetic and copies ran while one was open for 5% -> 2% of each run, Pallas kernels for 0% -> 27%
where the time goes in v1:
time: 164 us; the launch traced here: 162 us
  waiting for transfers between devices  56.7 us (35%)
  starting transfers between devices  53.7 us (33%)
  Pallas kernels  44 us (27%)
  other arithmetic  4.35 us (3%)
  local copies, waits for them, and re-layouts  3.01 us (2%)
    pallas_call x2, Pallas kernels, conv_chunk(): pl.pallas_call(functools.partial(conv_kernel, tuple(plan)), grid=(slab //...  25.7 us
    pallas_call x2, Pallas kernels, mlp_chunk(): pl.pallas_call(mlp_kernel, in_specs=[anywhere] * (len(slabs) + len(w_in_p...  18.3 us
    ppermute x14, starting transfers between devices, flipped(): return lax.ppermute(array, 'tile', [(i, i ^ bit) for i in range(8)])  16.8 us
    ppermute x2, waiting for transfers between devices, gather_line(): far_inner = lax.ppermute(near, 'chan', MIDDLE)  10.7 us
    ppermute x2, waiting for transfers between devices, gather_line(): far_outer = lax.ppermute(far_inner, 'chan', OUTWARD)  9.52 us
    ppermute x2, waiting for transfers between devices, scatter_line(): far_across = lax.ppermute(add(far, far_in), 'chan', MIDDLE)  7.4 us
    ppermute x2, waiting for transfers between devices, scatter_line(): mid_across = lax.ppermute(add(mid, mid_in), 'chan', MIDDLE)  6.08 us
    ppermute x2, waiting for transfers between devices, scatter_line(): mid_in = lax.ppermute(mid, 'chan', INWARD)  6.05 us
  transfers between devices with their start and end apart: 36, of which 13 were waited for; matrix products, arithmetic and copies ran while one was open for 2% of the time, Pallas kernels for 27%

profile of v1, /device:TPU:8, one launch (start us, length us, event | category | flops | bytes accessed | tf_op | source)
XLA Modules:
  0.0 162.2 jit_solution(13188769274620461324)
XLA Ops:
  1.2 1.8 %collective-permute-start = (bf16[3,384,128]{2,1,0:T(8,128)(2,1)S(1)}, bf16[3,384,128]{2,1,0:T(8,128)(2,1)S(1)}, u32[]{:S(2)}, u32[]{:S(2)}) collective-permute-start(bf16[3,384,128]{2,1,0:T(8,128)(2,1)S(1)} %get-tuple-element.23), channel_id=1, source_target_pairs={{0,4},{4,8},{8,12},{12,16},{16,20},{20,24},{24,28},{1,5},{5,9},{9,... | collective-permute-start | bytes 884744 | tf_op jit(solution)/shard_map/ppermute | solution.py:251
  4.3 2.5 %collective-permute-start.6 = (bf16[192,1536]{1,0:T(8,128)(2,1)}, bf16[192,1536]{1,0:T(8,128)(2,1)S(1)}, u32[]{:S(2)}, u32[]{:S(2)}) collective-permute-start(bf16[192,1536]{1,0:T(8,128)(2,1)} %refs_6_.3), channel_id=1, source_target_pairs={{0,4},{4,0},{8,12},{12,8},{16,20},{20,16},{24,28},{28,24},{1,5},{5... | collective-permute-start | bytes 1769480 | tf_op jit(solution)/shard_map/ppermute | solution.py:234
  6.7 1.7 %collective-permute-start.7 = (bf16[192,1536]{1,0:T(8,128)(2,1)}, bf16[192,1536]{1,0:T(8,128)(2,1)S(1)}, u32[]{:S(2)}, u32[]{:S(2)}) collective-permute-start(bf16[192,1536]{1,0:T(8,128)(2,1)} %refs_6_.3), channel_id=1, source_target_pairs={{0,8},{4,12},{8,0},{12,4},{16,24},{20,28},{24,16},{28,20},{1,9},{5... | collective-permute-start | bytes 1769480 | tf_op jit(solution)/shard_map/ppermute | solution.py:234
  8.4 1.5 collective-permute-start.9
  9.9 5.8 %collective-permute-start.14 = (bf16[192,1536]{1,0:T(8,128)(2,1)}, bf16[192,1536]{1,0:T(8,128)(2,1)}, u32[]{:S(2)}, u32[]{:S(2)}) collective-permute-start(bf16[192,1536]{1,0:T(8,128)(2,1)} %bitcast.26), channel_id=1, source_target_pairs={{0,8},{4,12},{8,0},{12,4},{16,24},{20,28},{24,16},{28,20},{1,9},{5... | collective-permute-start | bytes 1769480 | tf_op jit(solution)/shard_map/ppermute | solution.py:234
  15.9 12.8 %depthwise.2 = bf16[4,128,384]{2,1,0:T(8,128)(2,1)S(1)} custom-call(bf16[8,384,128]{2,1,0:T(8,128)(2,1)S(1)} %copy-done, bf16[3,384,128]{2,1,0:T(8,128)(2,1)S(1)} %collective-permute-done.refs_1_, f32[384,50]{1,0:T(8,128)S(1)} %copy.14.refs_2_), custom_call_target="tpu_custom_call" | custom-call | flops 19267584 | bytes 786432 | tf_op jit(solution)/shard_map/depthwise/pallas_call | solution.py:64
  28.8 3.6 %collective-permute-start.2 = (bf16[4,128,384]{2,1,0:T(8,128)(2,1)S(1)}, bf16[4,128,384]{2,1,0:T(8,128)(2,1)S(1)}, u32[]{:S(2)}, u32[]{:S(2)}) collective-permute-start(bf16[4,128,384]{2,1,0:T(8,128)(2,1)S(1)} %depthwise.2), channel_id=1, source_target_pairs={{1,2},{2,1},{5,6},{6,5},{9,10},{10,9},{13,14},{14,13},{17,18},{18,... | collective-permute-start | bytes 1179656 | tf_op jit(solution)/shard_map/ppermute | solution.py:213
  33.0 12.8 %depthwise.3 = bf16[4,128,384]{2,1,0:T(8,128)(2,1)S(1)} custom-call(bf16[8,384,128]{2,1,0:T(8,128)(2,1)S(1)} %copy-done, bf16[3,384,128]{2,1,0:T(8,128)(2,1)S(1)} %collective-permute-done.25.refs_1_, f32[384,50]{1,0:T(8,128)S(1)} %copy.14.refs_2_), custom_call_target="tpu_custom_call" | custom-call | flops 19267584 | bytes 786432 | tf_op jit(solution)/shard_map/depthwise/pallas_call | solution.py:64
  45.9 2.1 %collective-permute-start.26 = (bf16[4,128,384]{2,1,0:T(8,128)(2,1)S(1)}, bf16[4,128,384]{2,1,0:T(8,128)(2,1)S(1)}, u32[]{:S(2)}, u32[]{:S(2)}) collective-permute-start(bf16[4,128,384]{2,1,0:T(8,128)(2,1)S(1)} %depthwise.3), channel_id=1, source_target_pairs={{0,1},{1,0},{2,3},{3,2},{4,5},{5,4},{6,7},{7,6},{8,9},{9,8},{10,11... | collective-permute-start | bytes 1179656 | tf_op jit(solution)/shard_map/ppermute | solution.py:212
  48.0 2.3 %collective-permute-start.27 = (bf16[4,128,384]{2,1,0:T(8,128)(2,1)S(1)}, bf16[4,128,384]{2,1,0:T(8,128)(2,1)S(1)}, u32[]{:S(2)}, u32[]{:S(2)}) collective-permute-start(bf16[4,128,384]{2,1,0:T(8,128)(2,1)S(1)} %depthwise.3), channel_id=1, source_target_pairs={{1,2},{2,1},{5,6},{6,5},{9,10},{10,9},{13,14},{14,13},{17,18},{18,... | collective-permute-start | bytes 1179656 | tf_op jit(solution)/shard_map/ppermute | solution.py:213
  51.7 3.5 %collective-permute-start.4 = (bf16[4,128,384]{2,1,0:T(8,128)(2,1)S(1)}, bf16[4,128,384]{2,1,0:T(8,128)(2,1)S(1)}, u32[]{:S(2)}, u32[]{:S(2)}) collective-permute-start(bf16[4,128,384]{2,1,0:T(8,128)(2,1)S(1)} %collective-permute-done.1), channel_id=1, source_target_pairs={{1,2},{2,1},{5,6},{6,5},{9,10},{10,9},{13,14},{14,13},{17,18},{18,... | collective-permute-start | bytes 1179656 | tf_op jit(solution)/shard_map/ppermute | solution.py:214
  55.4 2.2 %collective-permute-done.26 = bf16[4,128,384]{2,1,0:T(8,128)(2,1)S(1)} collective-permute-done((bf16[4,128,384]{2,1,0:T(8,128)(2,1)S(1)}, bf16[4,128,384]{2,1,0:T(8,128)(2,1)S(1)}, u32[]{:S(2)}, u32[]{:S(2)}) %collective-permute-start.26) | collective-permute-done | bytes 393248 | tf_op jit(solution)/shard_map/ppermute | solution.py:212
  57.6 1.5 collective-permute-start.11
  59.1 2.7 %collective-permute-done.27 = bf16[4,128,384]{2,1,0:T(8,128)(2,1)S(1)} collective-permute-done((bf16[4,128,384]{2,1,0:T(8,128)(2,1)S(1)}, bf16[4,128,384]{2,1,0:T(8,128)(2,1)S(1)}, u32[]{:S(2)}, u32[]{:S(2)}) %collective-permute-start.27) | collective-permute-done | bytes 393248 | tf_op jit(solution)/shard_map/ppermute | solution.py:213
  61.8 2.1 %collective-permute-start.18 = (bf16[192,1536]{1,0:T(8,128)(2,1)S(1)}, bf16[192,1536]{1,0:T(8,128)(2,1)S(1)}, u32[]{:S(2)}, u32[]{:S(2)}) collective-permute-start(bf16[192,1536]{1,0:T(8,128)(2,1)S(1)} %collective-permute-done.16.refs_18_), channel_id=1, source_target_pairs={{0,8},{4,12},{8,0},{12,4},{16,24},{20,28},{24,16},{28,20},{1,9},{5... | collective-permute-start | bytes 1769480 | tf_op jit(solution)/shard_map/ppermute | solution.py:234
  63.9 2.0 %collective-permute-done.3 = bf16[4,128,384]{2,1,0:T(8,128)(2,1)S(1)} collective-permute-done((bf16[4,128,384]{2,1,0:T(8,128)(2,1)S(1)}, bf16[4,128,384]{2,1,0:T(8,128)(2,1)S(1)}, u32[]{:S(2)}, u32[]{:S(2)}) %collective-permute-start.3) | collective-permute-done | bytes 393248 | tf_op jit(solution)/shard_map/ppermute | solution.py:215
  65.9 2.3 %collective-permute-start.29 = (bf16[4,128,384]{2,1,0:T(8,128)(2,1)S(1)}, bf16[4,128,384]{2,1,0:T(8,128)(2,1)S(1)}, u32[]{:S(2)}, u32[]{:S(2)}) collective-permute-start(bf16[4,128,384]{2,1,0:T(8,128)(2,1)S(1)} %collective-permute-done.26), channel_id=1, source_target_pairs={{1,2},{2,1},{5,6},{6,5},{9,10},{10,9},{13,14},{14,13},{17,18},{18,... | collective-permute-start | bytes 1179656 | tf_op jit(solution)/shard_map/ppermute | solution.py:214
  68.2 1.8 %collective-permute-done.4 = bf16[4,128,384]{2,1,0:T(8,128)(2,1)S(1)} collective-permute-done((bf16[4,128,384]{2,1,0:T(8,128)(2,1)S(1)}, bf16[4,128,384]{2,1,0:T(8,128)(2,1)S(1)}, u32[]{:S(2)}, u32[]{:S(2)}) %collective-permute-start.4) | collective-permute-done | bytes 393248 | tf_op jit(solution)/shard_map/ppermute | solution.py:214
  70.0 8.9 %collective-permute-done.29 = bf16[4,128,384]{2,1,0:T(8,128)(2,1)S(1)} collective-permute-done((bf16[4,128,384]{2,1,0:T(8,128)(2,1)S(1)}, bf16[4,128,384]{2,1,0:T(8,128)(2,1)S(1)}, u32[]{:S(2)}, u32[]{:S(2)}) %collective-permute-start.29) | collective-permute-done | bytes 393248 | tf_op jit(solution)/shard_map/ppermute | solution.py:214
  84.7 6.0 %collective-permute-done.5 = bf16[4,128,384]{2,1,0:T(8,128)(2,1)S(1)} collective-permute-done((bf16[4,128,384]{2,1,0:T(8,128)(2,1)S(1)}, bf16[4,128,384]{2,1,0:T(8,128)(2,1)S(1)}, u32[]{:S(2)}, u32[]{:S(2)}) %collective-permute-start.5) | collective-permute-done | bytes 393248 | tf_op jit(solution)/shard_map/ppermute | solution.py:216
  91.7 9.1 %mlp.2 = (bf16[4,384,128]{2,1,0:T(8,128)(2,1)S(1)}, bf16[4,384,128]{2,1,0:T(8,128)(2,1)S(1)}, bf16[4,384,128]{2,1,0:T(8,128)(2,1)S(1)}, bf16[4,384,128]{2,1,0:T(8,128)(2,1)S(1)}) custom-call(bf16[512,384]{1,0:T(8,128)(2,1)S(1)} %bitcast.14, bf16[512,384]{1,0:T(8,128)(2,1)S(1)} %bitcast.18, bf16[512,384]{1,0:T(8,128)(2,1)S(1)} %bitcast.17, ...), custom_call_target="tpu_custom_call" | custom-call | flops 4831838208 | bytes 12582912 | tf_op jit(solution)/shard_map/mlp/pallas_call | solution.py:174
  103.5 3.5 %collective-permute-done.30 = bf16[4,128,384]{2,1,0:T(8,128)(2,1)S(1)} collective-permute-done((bf16[4,128,384]{2,1,0:T(8,128)(2,1)S(1)}, bf16[4,128,384]{2,1,0:T(8,128)(2,1)S(1)}, u32[]{:S(2)}, u32[]{:S(2)}) %collective-permute-start.30) | collective-permute-done | bytes 393248 | tf_op jit(solution)/shard_map/ppermute | solution.py:216
  107.0 9.1 %mlp.3 = (bf16[4,384,128]{2,1,0:T(8,128)(2,1)S(1)}, bf16[4,384,128]{2,1,0:T(8,128)(2,1)S(1)}, bf16[4,384,128]{2,1,0:T(8,128)(2,1)S(1)}, bf16[4,384,128]{2,1,0:T(8,128)(2,1)S(1)}) custom-call(bf16[512,384]{1,0:T(8,128)(2,1)S(1)} %bitcast.13, bf16[512,384]{1,0:T(8,128)(2,1)S(1)} %bitcast.15, bf16[512,384]{1,0:T(8,128)(2,1)S(1)} %bitcast.16, ...), custom_call_target="tpu_custom_call" | custom-call | flops 4831838208 | bytes 12582912 | tf_op jit(solution)/shard_map/mlp/pallas_call | solution.py:174
  118.8 2.4 %collective-permute-start.23 = (bf16[4,384,128]{2,1,0:T(8,128)(2,1)S(1)}, bf16[4,384,128]{2,1,0:T(8,128)(2,1)S(1)}, u32[]{:S(2)}, u32[]{:S(2)}) collective-permute-start(bf16[4,384,128]{2,1,0:T(8,128)(2,1)S(1)} %add_convert_fusion.6), channel_id=1, source_target_pairs={{1,2},{2,1},{5,6},{6,5},{9,10},{10,9},{13,14},{14,13},{17,18},{18,... | collective-permute-start | bytes 1179656 | tf_op jit(solution)/shard_map/ppermute | solution.py:227
  122.4 2.4 %collective-permute-start.21 = (bf16[4,384,128]{2,1,0:T(8,128)(2,1)S(1)}, bf16[4,384,128]{2,1,0:T(8,128)(2,1)S(1)}, u32[]{:S(2)}, u32[]{:S(2)}) collective-permute-start(bf16[4,384,128]{2,1,0:T(8,128)(2,1)S(1)} %add_convert_fusion.7), channel_id=1, source_target_pairs={{1,2},{2,1},{5,6},{6,5},{9,10},{10,9},{13,14},{14,13},{17,18},{18,... | collective-permute-start | bytes 1179656 | tf_op jit(solution)/shard_map/ppermute | solution.py:228
  124.8 5.9 %collective-permute-done.33 = bf16[4,384,128]{2,1,0:T(8,128)(2,1)S(1)} collective-permute-done((bf16[4,384,128]{2,1,0:T(8,128)(2,1)S(1)}, bf16[4,384,128]{2,1,0:T(8,128)(2,1)S(1)}, u32[]{:S(2)}, u32[]{:S(2)}) %collective-permute-start.33) | collective-permute-done | bytes 393248 | tf_op jit(solution)/shard_map/ppermute | solution.py:225
  130.8 2.4 %collective-permute-start.34 = (bf16[4,384,128]{2,1,0:T(8,128)(2,1)S(1)}, bf16[4,384,128]{2,1,0:T(8,128)(2,1)S(1)}, u32[]{:S(2)}, u32[]{:S(2)}) collective-permute-start(bf16[4,384,128]{2,1,0:T(8,128)(2,1)S(1)} %add_convert_fusion.2), channel_id=1, source_target_pairs={{1,2},{2,1},{5,6},{6,5},{9,10},{10,9},{13,14},{14,13},{17,18},{18,... | collective-permute-start | bytes 1179656 | tf_op jit(solution)/shard_map/ppermute | solution.py:227
  133.2 5.0 %collective-permute-done.31 = bf16[4,384,128]{2,1,0:T(8,128)(2,1)S(1)} collective-permute-done((bf16[4,384,128]{2,1,0:T(8,128)(2,1)S(1)}, bf16[4,384,128]{2,1,0:T(8,128)(2,1)S(1)}, u32[]{:S(2)}, u32[]{:S(2)}) %collective-permute-start.31) | collective-permute-done | bytes 393248 | tf_op jit(solution)/shard_map/ppermute | solution.py:226
  139.0 2.3 %collective-permute-start.32 = (bf16[4,384,128]{2,1,0:T(8,128)(2,1)}, bf16[4,384,128]{2,1,0:T(8,128)(2,1)S(1)}, u32[]{:S(2)}, u32[]{:S(2)}) collective-permute-start(bf16[4,384,128]{2,1,0:T(8,128)(2,1)} %add_convert_fusion.3), channel_id=1, source_target_pairs={{1,2},{2,1},{5,6},{6,5},{9,10},{10,9},{13,14},{14,13},{17,18},{18,... | collective-permute-start | bytes 1179656 | tf_op jit(solution)/shard_map/ppermute | solution.py:228
  142.2 7.4 %collective-permute-done.34 = bf16[4,384,128]{2,1,0:T(8,128)(2,1)S(1)} collective-permute-done((bf16[4,384,128]{2,1,0:T(8,128)(2,1)S(1)}, bf16[4,384,128]{2,1,0:T(8,128)(2,1)S(1)}, u32[]{:S(2)}, u32[]{:S(2)}) %collective-permute-start.34) | collective-permute-done | bytes 393248 | tf_op jit(solution)/shard_map/ppermute | solution.py:227
  150.5 6.1 %collective-permute-done.32 = bf16[4,384,128]{2,1,0:T(8,128)(2,1)S(1)} collective-permute-done((bf16[4,384,128]{2,1,0:T(8,128)(2,1)}, bf16[4,384,128]{2,1,0:T(8,128)(2,1)S(1)}, u32[]{:S(2)}, u32[]{:S(2)}) %collective-permute-start.32) | collective-permute-done | bytes 393248 | tf_op jit(solution)/shard_map/ppermute | solution.py:228
  156.6 4.2 %collective-permute-done.35 = bf16[4,384,128]{2,1,0:T(8,128)(2,1)S(1)} collective-permute-done((bf16[4,384,128]{2,1,0:T(8,128)(2,1)}, bf16[4,384,128]{2,1,0:T(8,128)(2,1)S(1)}, u32[]{:S(2)}, u32[]{:S(2)}) %collective-permute-start.35) | collective-permute-done | bytes 393248 | tf_op jit(solution)/shard_map/ppermute | solution.py:229
  (99 shorter events, 22.0 us)
Async XLA Ops:
  4.3 24.5 %collective-permute-start.6 = (bf16[192,1536]{1,0:T(8,128)(2,1)}, bf16[192,1536]{1,0:T(8,128)(2,1)S(1)}, u32[]{:S(2)}, u32[]{:S(2)}) collective-permute-start(bf16[192,1536]{1,0:T(8,128)(2,1)} %refs_6_.3), channel_id=1, source_target_pairs={{0,4},{4,0},{8,12},{12,8},{16,20},{20,16},{24,28},{28,24},{1,5},{5... | collective-permute-start | bytes 1769480 | tf_op jit(solution)/shard_map/ppermute | solution.py:234
  6.7 25.7 %collective-permute-start.7 = (bf16[192,1536]{1,0:T(8,128)(2,1)}, bf16[192,1536]{1,0:T(8,128)(2,1)S(1)}, u32[]{:S(2)}, u32[]{:S(2)}) collective-permute-start(bf16[192,1536]{1,0:T(8,128)(2,1)} %refs_6_.3), channel_id=1, source_target_pairs={{0,8},{4,12},{8,0},{12,4},{16,24},{20,28},{24,16},{28,20},{1,9},{5... | collective-permute-start | bytes 1769480 | tf_op jit(solution)/shard_map/ppermute | solution.py:234
  8.4 24.6 %collective-permute-start.9 = (bf16[192,1536]{1,0:T(8,128)(2,1)}, bf16[192,1536]{1,0:T(8,128)(2,1)S(1)}, u32[]{:S(2)}, u32[]{:S(2)}) collective-permute-start(bf16[192,1536]{1,0:T(8,128)(2,1)} %refs_6_.3), channel_id=1, source_target_pairs={{0,16},{4,20},{8,24},{12,28},{16,0},{20,4},{24,8},{28,12},{1,17},{... | collective-permute-start | bytes 1769480 | tf_op jit(solution)/shard_map/ppermute | solution.py:234
  9.9 35.9 %collective-permute-start.13 = (bf16[192,1536]{1,0:T(8,128)(2,1)}, bf16[192,1536]{1,0:T(8,128)(2,1)}, u32[]{:S(2)}, u32[]{:S(2)}) collective-permute-start(bf16[192,1536]{1,0:T(8,128)(2,1)} %bitcast.25), channel_id=1, source_target_pairs={{0,4},{4,0},{8,12},{12,8},{16,20},{20,16},{24,28},{28,24},{1,5},{5... | collective-permute-start | bytes 1769480 | tf_op jit(solution)/shard_map/ppermute | solution.py:234
  9.9 38.0 %collective-permute-start.14 = (bf16[192,1536]{1,0:T(8,128)(2,1)}, bf16[192,1536]{1,0:T(8,128)(2,1)}, u32[]{:S(2)}, u32[]{:S(2)}) collective-permute-start(bf16[192,1536]{1,0:T(8,128)(2,1)} %bitcast.26), channel_id=1, source_target_pairs={{0,8},{4,12},{8,0},{12,4},{16,24},{20,28},{24,16},{28,20},{1,9},{5... | collective-permute-start | bytes 1769480 | tf_op jit(solution)/shard_map/ppermute | solution.py:234
  28.8 21.5 %collective-permute-start.2 = (bf16[4,128,384]{2,1,0:T(8,128)(2,1)S(1)}, bf16[4,128,384]{2,1,0:T(8,128)(2,1)S(1)}, u32[]{:S(2)}, u32[]{:S(2)}) collective-permute-start(bf16[4,128,384]{2,1,0:T(8,128)(2,1)S(1)} %depthwise.2), channel_id=1, source_target_pairs={{1,2},{2,1},{5,6},{6,5},{9,10},{10,9},{13,14},{14,13},{17,18},{18,... | collective-permute-start | bytes 1179656 | tf_op jit(solution)/shard_map/ppermute | solution.py:213
  32.4 22.7 %collective-permute-start.16 = (bf16[192,1536]{1,0:T(8,128)(2,1)S(1)}, bf16[192,1536]{1,0:T(8,128)(2,1)S(1)}, u32[]{:S(2)}, u32[]{:S(2)}) collective-permute-start(bf16[192,1536]{1,0:T(8,128)(2,1)S(1)} %bitcast.29), channel_id=1, source_target_pairs={{0,16},{4,20},{8,24},{12,28},{16,0},{20,4},{24,8},{28,12},{1,17},{... | collective-permute-start | bytes 1769480 | tf_op jit(solution)/shard_map/ppermute | solution.py:234
  33.0 18.7 %collective-permute-start.1 = (bf16[4,128,384]{2,1,0:T(8,128)(2,1)S(1)}, bf16[4,128,384]{2,1,0:T(8,128)(2,1)S(1)}, u32[]{:S(2)}, u32[]{:S(2)}) collective-permute-start(bf16[4,128,384]{2,1,0:T(8,128)(2,1)S(1)} %depthwise.2), channel_id=1, source_target_pairs={{0,1},{1,0},{2,3},{3,2},{4,5},{5,4},{6,7},{7,6},{8,9},{9,8},{10,11... | collective-permute-start | bytes 1179656 | tf_op jit(solution)/shard_map/ppermute | solution.py:212
  45.9 11.7 %collective-permute-start.26 = (bf16[4,128,384]{2,1,0:T(8,128)(2,1)S(1)}, bf16[4,128,384]{2,1,0:T(8,128)(2,1)S(1)}, u32[]{:S(2)}, u32[]{:S(2)}) collective-permute-start(bf16[4,128,384]{2,1,0:T(8,128)(2,1)S(1)} %depthwise.3), channel_id=1, source_target_pairs={{0,1},{1,0},{2,3},{3,2},{4,5},{5,4},{6,7},{7,6},{8,9},{9,8},{10,11... | collective-permute-start | bytes 1179656 | tf_op jit(solution)/shard_map/ppermute | solution.py:212
  48.0 13.9 %collective-permute-start.27 = (bf16[4,128,384]{2,1,0:T(8,128)(2,1)S(1)}, bf16[4,128,384]{2,1,0:T(8,128)(2,1)S(1)}, u32[]{:S(2)}, u32[]{:S(2)}) collective-permute-start(bf16[4,128,384]{2,1,0:T(8,128)(2,1)S(1)} %depthwise.3), channel_id=1, source_target_pairs={{1,2},{2,1},{5,6},{6,5},{9,10},{10,9},{13,14},{14,13},{17,18},{18,... | collective-permute-start | bytes 1179656 | tf_op jit(solution)/shard_map/ppermute | solution.py:213
  50.3 15.6 %collective-permute-start.3 = (bf16[4,128,384]{2,1,0:T(8,128)(2,1)S(1)}, bf16[4,128,384]{2,1,0:T(8,128)(2,1)S(1)}, u32[]{:S(2)}, u32[]{:S(2)}) collective-permute-start(bf16[4,128,384]{2,1,0:T(8,128)(2,1)S(1)} %collective-permute-done.2), channel_id=1, source_target_pairs={{1,0},{2,3},{5,4},{6,7},{9,8},{10,11},{13,12},{14,15},{17,16},{18,... | collective-permute-start | bytes 1179656 | tf_op jit(solution)/shard_map/ppermute | solution.py:215
  51.7 18.3 %collective-permute-start.4 = (bf16[4,128,384]{2,1,0:T(8,128)(2,1)S(1)}, bf16[4,128,384]{2,1,0:T(8,128)(2,1)S(1)}, u32[]{:S(2)}, u32[]{:S(2)}) collective-permute-start(bf16[4,128,384]{2,1,0:T(8,128)(2,1)S(1)} %collective-permute-done.1), channel_id=1, source_target_pairs={{1,2},{2,1},{5,6},{6,5},{9,10},{10,9},{13,14},{14,13},{17,18},{18,... | collective-permute-start | bytes 1179656 | tf_op jit(solution)/shard_map/ppermute | solution.py:214
  55.2 23.8 %collective-permute-start.8 = (bf16[192,1536]{1,0:T(8,128)(2,1)S(1)}, bf16[192,1536]{1,0:T(8,128)(2,1)S(1)}, u32[]{:S(2)}, u32[]{:S(2)}) collective-permute-start(bf16[192,1536]{1,0:T(8,128)(2,1)S(1)} %collective-permute-done.7.refs_8_), channel_id=1, source_target_pairs={{0,4},{4,0},{8,12},{12,8},{16,20},{20,16},{24,28},{28,24},{1,5},{5... | collective-permute-start | bytes 1769480 | tf_op jit(solution)/shard_map/ppermute | solution.py:234
  57.6 21.8 %collective-permute-start.11 = (bf16[192,1536]{1,0:T(8,128)(2,1)S(1)}, bf16[192,1536]{1,0:T(8,128)(2,1)S(1)}, u32[]{:S(2)}, u32[]{:S(2)}) collective-permute-start(bf16[192,1536]{1,0:T(8,128)(2,1)S(1)} %collective-permute-done.7.refs_8_), channel_id=1, source_target_pairs={{0,16},{4,20},{8,24},{12,28},{16,0},{20,4},{24,8},{28,12},{1,17},{... | collective-permute-start | bytes 1769480 | tf_op jit(solution)/shard_map/ppermute | solution.py:234
  61.8 17.7 %collective-permute-start.18 = (bf16[192,1536]{1,0:T(8,128)(2,1)S(1)}, bf16[192,1536]{1,0:T(8,128)(2,1)S(1)}, u32[]{:S(2)}, u32[]{:S(2)}) collective-permute-start(bf16[192,1536]{1,0:T(8,128)(2,1)S(1)} %collective-permute-done.16.refs_18_), channel_id=1, source_target_pairs={{0,8},{4,12},{8,0},{12,4},{16,24},{20,28},{24,16},{28,20},{1,9},{5... | collective-permute-start | bytes 1769480 | tf_op jit(solution)/shard_map/ppermute | solution.py:234
  65.9 13.0 %collective-permute-start.29 = (bf16[4,128,384]{2,1,0:T(8,128)(2,1)S(1)}, bf16[4,128,384]{2,1,0:T(8,128)(2,1)S(1)}, u32[]{:S(2)}, u32[]{:S(2)}) collective-permute-start(bf16[4,128,384]{2,1,0:T(8,128)(2,1)S(1)} %collective-permute-done.26), channel_id=1, source_target_pairs={{1,2},{2,1},{5,6},{6,5},{9,10},{10,9},{13,14},{14,13},{17,18},{18,... | collective-permute-start | bytes 1179656 | tf_op jit(solution)/shard_map/ppermute | solution.py:214
  70.0 10.0 %collective-permute-start.10 = (bf16[192,1536]{1,0:T(8,128)(2,1)S(1)}, bf16[192,1536]{1,0:T(8,128)(2,1)S(1)}, u32[]{:S(2)}, u32[]{:S(2)}) collective-permute-start(bf16[192,1536]{1,0:T(8,128)(2,1)S(1)} %collective-permute-done.9.refs_10_), channel_id=1, source_target_pairs={{0,4},{4,0},{8,12},{12,8},{16,20},{20,16},{24,28},{28,24},{1,5},{5... | collective-permute-start | bytes 1769480 | tf_op jit(solution)/shard_map/ppermute | solution.py:234
  79.4 11.2 %collective-permute-start.12 = (bf16[192,1536]{1,0:T(8,128)(2,1)S(1)}, bf16[192,1536]{1,0:T(8,128)(2,1)S(1)}, u32[]{:S(2)}, u32[]{:S(2)}) collective-permute-start(bf16[192,1536]{1,0:T(8,128)(2,1)S(1)} %collective-permute-done.11.refs_12_), channel_id=1, source_target_pairs={{0,4},{4,0},{8,12},{12,8},{16,20},{20,16},{24,28},{28,24},{1,5},{5... | collective-permute-start | bytes 1769480 | tf_op jit(solution)/shard_map/ppermute | solution.py:234
  79.5 11.2 %collective-permute-start.19 = (bf16[192,1536]{1,0:T(8,128)(2,1)S(1)}, bf16[192,1536]{1,0:T(8,128)(2,1)S(1)}, u32[]{:S(2)}, u32[]{:S(2)}) collective-permute-start(bf16[192,1536]{1,0:T(8,128)(2,1)S(1)} %collective-permute-done.18.refs_20_), channel_id=1, source_target_pairs={{0,4},{4,0},{8,12},{12,8},{16,20},{20,16},{24,28},{28,24},{1,5},{5... | collective-permute-start | bytes 1769480 | tf_op jit(solution)/shard_map/ppermute | solution.py:234
  80.0 10.7 %collective-permute-start.5 = (bf16[4,128,384]{2,1,0:T(8,128)(2,1)S(1)}, bf16[4,128,384]{2,1,0:T(8,128)(2,1)S(1)}, u32[]{:S(2)}, u32[]{:S(2)}) collective-permute-start(bf16[4,128,384]{2,1,0:T(8,128)(2,1)S(1)} %collective-permute-done.4), channel_id=1, source_target_pairs={{1,0},{2,3},{5,4},{6,7},{9,8},{10,11},{13,12},{14,15},{17,16},{18,... | collective-permute-start | bytes 1179656 | tf_op jit(solution)/shard_map/ppermute | solution.py:216
  82.0 21.4 %collective-permute-start.28 = (bf16[4,128,384]{2,1,0:T(8,128)(2,1)S(1)}, bf16[4,128,384]{2,1,0:T(8,128)(2,1)S(1)}, u32[]{:S(2)}, u32[]{:S(2)}) collective-permute-start(bf16[4,128,384]{2,1,0:T(8,128)(2,1)S(1)} %collective-permute-done.27), channel_id=1, source_target_pairs={{1,0},{2,3},{5,4},{6,7},{9,8},{10,11},{13,12},{14,15},{17,16},{18,... | collective-permute-start | bytes 1179656 | tf_op jit(solution)/shard_map/ppermute | solution.py:215
  83.4 23.6 %collective-permute-start.30 = (bf16[4,128,384]{2,1,0:T(8,128)(2,1)S(1)}, bf16[4,128,384]{2,1,0:T(8,128)(2,1)S(1)}, u32[]{:S(2)}, u32[]{:S(2)}) collective-permute-start(bf16[4,128,384]{2,1,0:T(8,128)(2,1)S(1)} %collective-permute-done.29), channel_id=1, source_target_pairs={{1,0},{2,3},{5,4},{6,7},{9,8},{10,11},{13,12},{14,15},{17,16},{18,... | collective-permute-start | bytes 1179656 | tf_op jit(solution)/shard_map/ppermute | solution.py:216
  100.8 17.9 %collective-permute-start.22 = (bf16[4,384,128]{2,1,0:T(8,128)(2,1)S(1)}, bf16[4,384,128]{2,1,0:T(8,128)(2,1)S(1)}, u32[]{:S(2)}, u32[]{:S(2)}) collective-permute-start(bf16[4,384,128]{2,1,0:T(8,128)(2,1)S(1)} %get-tuple-element.16), channel_id=1, source_target_pairs={{0,1},{3,2},{4,5},{7,6},{8,9},{11,10},{12,13},{15,14},{16,17},{19,... | collective-permute-start | bytes 1179656 | tf_op jit(solution)/shard_map/ppermute | solution.py:225
  102.1 20.1 %collective-permute-start.20 = (bf16[4,384,128]{2,1,0:T(8,128)(2,1)S(1)}, bf16[4,384,128]{2,1,0:T(8,128)(2,1)S(1)}, u32[]{:S(2)}, u32[]{:S(2)}) collective-permute-start(bf16[4,384,128]{2,1,0:T(8,128)(2,1)S(1)} %get-tuple-element.14), channel_id=1, source_target_pairs={{0,1},{3,2},{4,5},{7,6},{8,9},{11,10},{12,13},{15,14},{16,17},{19,... | collective-permute-start | bytes 1179656 | tf_op jit(solution)/shard_map/ppermute | solution.py:226
  116.1 14.6 %collective-permute-start.33 = (bf16[4,384,128]{2,1,0:T(8,128)(2,1)S(1)}, bf16[4,384,128]{2,1,0:T(8,128)(2,1)S(1)}, u32[]{:S(2)}, u32[]{:S(2)}) collective-permute-start(bf16[4,384,128]{2,1,0:T(8,128)(2,1)S(1)} %get-tuple-element.20), channel_id=1, source_target_pairs={{0,1},{3,2},{4,5},{7,6},{8,9},{11,10},{12,13},{15,14},{16,17},{19,... | collective-permute-start | bytes 1179656 | tf_op jit(solution)/shard_map/ppermute | solution.py:225
  117.4 20.7 %collective-permute-start.31 = (bf16[4,384,128]{2,1,0:T(8,128)(2,1)S(1)}, bf16[4,384,128]{2,1,0:T(8,128)(2,1)S(1)}, u32[]{:S(2)}, u32[]{:S(2)}) collective-permute-start(bf16[4,384,128]{2,1,0:T(8,128)(2,1)S(1)} %get-tuple-element.18), channel_id=1, source_target_pairs={{0,1},{3,2},{4,5},{7,6},{8,9},{11,10},{12,13},{15,14},{16,17},{19,... | collective-permute-start | bytes 1179656 | tf_op jit(solution)/shard_map/ppermute | solution.py:226
  118.8 22.5 %collective-permute-start.23 = (bf16[4,384,128]{2,1,0:T(8,128)(2,1)S(1)}, bf16[4,384,128]{2,1,0:T(8,128)(2,1)S(1)}, u32[]{:S(2)}, u32[]{:S(2)}) collective-permute-start(bf16[4,384,128]{2,1,0:T(8,128)(2,1)S(1)} %add_convert_fusion.6), channel_id=1, source_target_pairs={{1,2},{2,1},{5,6},{6,5},{9,10},{10,9},{13,14},{14,13},{17,18},{18,... | collective-permute-start | bytes 1179656 | tf_op jit(solution)/shard_map/ppermute | solution.py:227
  122.4 28.1 %collective-permute-start.21 = (bf16[4,384,128]{2,1,0:T(8,128)(2,1)S(1)}, bf16[4,384,128]{2,1,0:T(8,128)(2,1)S(1)}, u32[]{:S(2)}, u32[]{:S(2)}) collective-permute-start(bf16[4,384,128]{2,1,0:T(8,128)(2,1)S(1)} %add_convert_fusion.7), channel_id=1, source_target_pairs={{1,2},{2,1},{5,6},{6,5},{9,10},{10,9},{13,14},{14,13},{17,18},{18,... | collective-permute-start | bytes 1179656 | tf_op jit(solution)/shard_map/ppermute | solution.py:228
  130.8 18.8 %collective-permute-start.34 = (bf16[4,384,128]{2,1,0:T(8,128)(2,1)S(1)}, bf16[4,384,128]{2,1,0:T(8,128)(2,1)S(1)}, u32[]{:S(2)}, u32[]{:S(2)}) collective-permute-start(bf16[4,384,128]{2,1,0:T(8,128)(2,1)S(1)} %add_convert_fusion.2), channel_id=1, source_target_pairs={{1,2},{2,1},{5,6},{6,5},{9,10},{10,9},{13,14},{14,13},{17,18},{18,... | collective-permute-start | bytes 1179656 | tf_op jit(solution)/shard_map/ppermute | solution.py:227
  139.0 17.6 %collective-permute-start.32 = (bf16[4,384,128]{2,1,0:T(8,128)(2,1)}, bf16[4,384,128]{2,1,0:T(8,128)(2,1)S(1)}, u32[]{:S(2)}, u32[]{:S(2)}) collective-permute-start(bf16[4,384,128]{2,1,0:T(8,128)(2,1)} %add_convert_fusion.3), channel_id=1, source_target_pairs={{1,2},{2,1},{5,6},{6,5},{9,10},{10,9},{13,14},{14,13},{17,18},{18,... | collective-permute-start | bytes 1179656 | tf_op jit(solution)/shard_map/ppermute | solution.py:228
  142.2 14.4 %collective-permute-start.24 = (bf16[4,384,128]{2,1,0:T(8,128)(2,1)}, bf16[4,384,128]{2,1,0:T(8,128)(2,1)S(1)}, u32[]{:S(2)}, u32[]{:S(2)}) collective-permute-start(bf16[4,384,128]{2,1,0:T(8,128)(2,1)} %add_convert_fusion.5), channel_id=1, source_target_pairs={{0,1},{1,0},{2,3},{3,2},{4,5},{5,4},{6,7},{7,6},{8,9},{9,8},{10,11... | collective-permute-start | bytes 1179656 | tf_op jit(solution)/shard_map/ppermute | solution.py:229
  150.5 10.3 %collective-permute-start.35 = (bf16[4,384,128]{2,1,0:T(8,128)(2,1)}, bf16[4,384,128]{2,1,0:T(8,128)(2,1)S(1)}, u32[]{:S(2)}, u32[]{:S(2)}) collective-permute-start(bf16[4,384,128]{2,1,0:T(8,128)(2,1)} %add_convert_fusion.1), channel_id=1, source_target_pairs={{0,1},{1,0},{2,3},{3,2},{4,5},{5,4},{6,7},{7,6},{8,9},{9,8},{10,11... | collective-permute-start | bytes 1179656 | tf_op jit(solution)/shard_map/ppermute | solution.py:229
  (24 other events, 393.6 us)

commit v2 on v1

--- a/solution.py
+++ b/solution.py
@@ -15,38 +15,36 @@
 
 
 def conv_kernel(plan, *refs):
-    sources, taps_ref, out_ref, held = refs[:-3], refs[-3], refs[-2], refs[-1]
-    rows, channels, width = held.shape
-    group = 16
-    column = lax.broadcasted_iota(jnp.int32, (1, group, width), 2)
-
-    def one_group(i, carry):
-        at = pl.ds(pl.multiple_of(i * group, group), group)
-        image = jnp.stack([sources[s][r, at, :] for s, r in plan]).astype(jnp.float32)
-        taps = taps_ref[at, :]
-        bias = taps[:, SIDE * SIDE : SIDE * SIDE + 1][None]
-        total = jnp.broadcast_to(bias, (rows, group, width))
+    sources, taps_ref, bias_ref, out_ref, image = refs[:-4], *refs[-4:]
+    rows, width, channels = out_ref.shape
+    edge = (image.shape[1] - width) // 2
+    blank = jnp.zeros((edge, channels), jnp.float32)
+    for i, (source, row) in enumerate(plan):
+        image[i, :edge, :] = blank
+        image[i, edge + width :, :] = blank
+        image[i, edge : edge + width, :] = sources[source][row].astype(jnp.float32).T
+    bias = bias_ref[...]
+    tile = 16
+
+    def one_tile(i, carry):
+        start = pl.multiple_of(i * tile, tile)
+        totals = [jnp.broadcast_to(bias, (tile, channels)) for _ in range(rows)]
         for b in range(SIDE):
-            part = None
-            for a in range(SIDE):
-                tap = SIDE * a + b
-                term = image[a : a + rows] * taps[:, tap : tap + 1][None]
-                part = term if part is None else part + term
-            offset = b - REACH
-            if offset:
-                part = pltpu.roll(part, (-offset) % width, 2)
-                inside = column < width - offset if offset > 0 else column >= -offset
-                part = jnp.where(inside, part, 0.0)
-            total = total + part
-        held[:, at, :] = total
+            for j in range(len(plan)):
+                pixels = image[j, pl.ds(start + (edge - REACH + b), tile), :]
+                for row in range(rows):
+                    a = j - row
+                    if 0 <= a < SIDE:
+                        tap = SIDE * a + b
+                        totals[row] = totals[row] + pixels * taps_ref[tap : tap + 1, :]
+        for row in range(rows):
+            out_ref[row, pl.ds(start, tile), :] = totals[row].astype(out_ref.dtype)
         return carry
 
-    lax.fori_loop(0, channels // group, one_group, 0)
-    for row in range(rows):
-        out_ref[row] = held[row].T.astype(out_ref.dtype)
-
-
-def conv_chunk(first, rows, low, features, high, taps):
+    lax.fori_loop(0, width // tile, one_tile, 0)
+
+
+def conv_chunk(first, rows, low, features, high, taps, bias):
     height, slab, width = features.shape
     names, plan = ["features"], []
     for row in range(first - REACH, first + rows + REACH):
@@ -65,10 +63,10 @@
         functools.partial(conv_kernel, tuple(plan)),
         grid=(slab // block,),
         in_specs=[pl.BlockSpec((a.shape[0], block, width), lambda i: (0, i, 0)) for a in arrays]
-        + [pl.BlockSpec((block, taps.shape[1]), lambda i: (i, 0))],
+        + [pl.BlockSpec((t.shape[0], block), lambda i: (0, i)) for t in (taps, bias)],
         out_specs=pl.BlockSpec((rows, width, block), lambda i: (0, 0, i)),
         out_shape=jax.ShapeDtypeStruct((rows, width, slab), jnp.bfloat16),
-        scratch_shapes=[pltpu.VMEM((rows, block, width), jnp.float32)],
+        scratch_shapes=[pltpu.VMEM((len(plan), width + 16, block), jnp.float32)],
         compiler_params=pltpu.CompilerParams(vmem_limit_bytes=VMEM_LIMIT),
         cost_estimate=pl.CostEstimate(
             flops=2 * SIDE * SIDE * rows * slab * width,
@@ -76,7 +74,7 @@
             transcendentals=0,
         ),
         name="depthwise",
-    )(*arrays, taps)
+    )(*arrays, taps, bias)
 
 
 def line_places(z):
@@ -256,12 +254,11 @@
 def local(features, dw_weight, dw_bias, ln_gain, ln_bias, w_in, b_in, w_out, b_out, gamma):
     height = features.shape[0]
     low, high = rims(features)
-    taps = jnp.concatenate([dw_weight, dw_bias[:, None]], axis=1)
     w_in_parts, w_out_parts = gather_shards(w_in, w_out.T)
     rows = height // CHUNKS
     results = []
     for first in range(0, height, rows):
-        slab = conv_chunk(first, rows, low, features, high, taps)
+        slab = conv_chunk(first, rows, low, features, high, dw_weight.T, dw_bias[None])
         partials = mlp_chunk(gather_line(slab), w_in_parts, w_out_parts, ln_gain, ln_bias, b_in)
         projected = scatter_line(*partials) + b_out[None, :, None]
         block = features[first : first + rows].astype(jnp.float32)

time: 164 us -> 152 us (0.927)
  Pallas kernels: 44 us -> 27.1 us
  starting transfers between devices: 53.7 us -> 56.7 us
  waiting for transfers between devices: 56.7 us -> 58.6 us
    pallas_call x2, Pallas kernels: 25.7 us -> 8.87 us  [conv_chunk(): pl.pallas_call(functools.partial(conv_kernel, tuple(plan)), grid=(slab //...]
    ppermute x14, waiting for transfers between devices: 0.04 us -> 8.1 us  [flipped(): return lax.ppermute(array, 'tile', [(i, i ^ bit) for i in range(8)])]
    ppermute x14, starting transfers between devices: 16.8 us -> 13.8 us  [flipped(): return lax.ppermute(array, 'tile', [(i, i ^ bit) for i in range(8)])]
    ppermute x2, starting transfers between devices: 4.72 us -> 6.97 us  [scatter_line(): far_across = lax.ppermute(add(far, far_in), 'chan', MIDDLE)]
    ppermute x2, waiting for transfers between devices: 2.24 us -> 0.01 us  [gather_line(): near = lax.ppermute(slab, 'chan', PAIRS)]
    ppermute x2, waiting for transfers between devices: 2.72 us -> 4.95 us  [gather_line(): mid_inner = lax.ppermute(slab, 'chan', MIDDLE)]
    ppermute x2, waiting for transfers between devices: 6.05 us -> 3.89 us  [scatter_line(): mid_in = lax.ppermute(mid, 'chan', INWARD)]
    ppermute x2, starting transfers between devices: 4.79 us -> 6.84 us  [scatter_line(): mid_across = lax.ppermute(add(mid, mid_in), 'chan', MIDDLE)]
  transfers between devices with their start and end apart: 36 -> 36, of which waited for: 13 -> 12; matrix products, arithmetic and copies ran while one was open for 2% -> 2% of each run, Pallas kernels for 27% -> 18%
where the time goes in v2:
time: 152 us; the launch traced here: 150 us
  waiting for transfers between devices  58.6 us (39%)
  starting transfers between devices  56.7 us (37%)
  Pallas kernels  27.1 us (18%)
  other arithmetic  4.33 us (3%)
  local copies, waits for them, and re-layouts  2.88 us (2%)
    pallas_call x2, Pallas kernels, mlp_chunk(): pl.pallas_call(mlp_kernel, in_specs=[anywhere] * (len(slabs) + len(w_in_p...  18.3 us
    ppermute x14, starting transfers between devices, flipped(): return lax.ppermute(array, 'tile', [(i, i ^ bit) for i in range(8)])  13.8 us
    ppermute x2, waiting for transfers between devices, gather_line(): far_inner = lax.ppermute(near, 'chan', MIDDLE)  9.63 us
    ppermute x2, waiting for transfers between devices, gather_line(): far_outer = lax.ppermute(far_inner, 'chan', OUTWARD)  9.54 us
    pallas_call x2, Pallas kernels, conv_chunk(): pl.pallas_call(functools.partial(conv_kernel, tuple(plan)), grid=(slab //...  8.87 us
    ppermute x14, waiting for transfers between devices, flipped(): return lax.ppermute(array, 'tile', [(i, i ^ bit) for i in range(8)])  8.1 us
    ppermute x2, starting transfers between devices, gather_line(): mid_inner = lax.ppermute(slab, 'chan', MIDDLE)  7.09 us
    ppermute x2, starting transfers between devices, scatter_line(): far_across = lax.ppermute(add(far, far_in), 'chan', MIDDLE)  6.97 us
  transfers between devices with their start and end apart: 36, of which 12 were waited for; matrix products, arithmetic and copies ran while one was open for 2% of the time, Pallas kernels for 18%

profile of v2, /device:TPU:8, one launch (start us, length us, event | category | flops | bytes accessed | tf_op | source)
XLA Modules:
  0.0 150.1 jit_solution(1436225441809327477)
XLA Ops:
  1.2 1.8 %collective-permute-start = (bf16[3,384,128]{2,1,0:T(8,128)(2,1)S(1)}, bf16[3,384,128]{2,1,0:T(8,128)(2,1)S(1)}, u32[]{:S(2)}, u32[]{:S(2)}) collective-permute-start(bf16[3,384,128]{2,1,0:T(8,128)(2,1)S(1)} %get-tuple-element.23), channel_id=1, source_target_pairs={{0,4},{4,8},{8,12},{12,16},{16,20},{20,24},{24,28},{1,5},{5,9},{9,... | collective-permute-start | bytes 884744 | tf_op jit(solution)/shard_map/ppermute | solution.py:249
  4.3 2.5 %collective-permute-start.6 = (bf16[192,1536]{1,0:T(8,128)(2,1)}, bf16[192,1536]{1,0:T(8,128)(2,1)S(1)}, u32[]{:S(2)}, u32[]{:S(2)}) collective-permute-start(bf16[192,1536]{1,0:T(8,128)(2,1)} %refs_6_.3), channel_id=1, source_target_pairs={{0,4},{4,0},{8,12},{12,8},{16,20},{20,16},{24,28},{28,24},{1,5},{5... | collective-permute-start | bytes 1769480 | tf_op jit(solution)/shard_map/ppermute | solution.py:232
  6.7 1.7 %collective-permute-start.7 = (bf16[192,1536]{1,0:T(8,128)(2,1)}, bf16[192,1536]{1,0:T(8,128)(2,1)S(1)}, u32[]{:S(2)}, u32[]{:S(2)}) collective-permute-start(bf16[192,1536]{1,0:T(8,128)(2,1)} %refs_6_.3), channel_id=1, source_target_pairs={{0,8},{4,12},{8,0},{12,4},{16,24},{20,28},{24,16},{28,20},{1,9},{5... | collective-permute-start | bytes 1769480 | tf_op jit(solution)/shard_map/ppermute | solution.py:232
  8.4 1.5 %collective-permute-start.9 = (bf16[192,1536]{1,0:T(8,128)(2,1)}, bf16[192,1536]{1,0:T(8,128)(2,1)S(1)}, u32[]{:S(2)}, u32[]{:S(2)}) collective-permute-start(bf16[192,1536]{1,0:T(8,128)(2,1)} %refs_6_.3), channel_id=1, source_target_pairs={{0,16},{4,20},{8,24},{12,28},{16,0},{20,4},{24,8},{28,12},{1,17},{... | collective-permute-start | bytes 1769480 | tf_op jit(solution)/shard_map/ppermute | solution.py:232
  9.9 5.8 %collective-permute-start.14 = (bf16[192,1536]{1,0:T(8,128)(2,1)}, bf16[192,1536]{1,0:T(8,128)(2,1)S(1)}, u32[]{:S(2)}, u32[]{:S(2)}) collective-permute-start(bf16[192,1536]{1,0:T(8,128)(2,1)} %bitcast.29), channel_id=1, source_target_pairs={{0,8},{4,12},{8,0},{12,4},{16,24},{20,28},{24,16},{28,20},{1,9},{5... | collective-permute-start | bytes 1769480 | tf_op jit(solution)/shard_map/ppermute | solution.py:232
  15.7 4.4 %depthwise.2 = bf16[4,128,384]{2,1,0:T(8,128)(2,1)S(1)} custom-call(bf16[8,384,128]{2,1,0:T(8,128)(2,1)S(1)} %copy-done, bf16[3,384,128]{2,1,0:T(8,128)(2,1)S(1)} %collective-permute-done.refs_1_, f32[49,384]{1,0:T(8,128)S(1)} %bitcast.16, f32[1,384]{1,0:T(1,128)S(1)} %broadcast_in_dim.8.refs_3_), custom_call_target="tpu_custom_call" | custom-call | flops 19267584 | bytes 786432 | tf_op jit(solution)/shard_map/depthwise/pallas_call | solution.py:62
  20.2 3.6 %collective-permute-start.2 = (bf16[4,128,384]{2,1,0:T(8,128)(2,1)S(1)}, bf16[4,128,384]{2,1,0:T(8,128)(2,1)S(1)}, u32[]{:S(2)}, u32[]{:S(2)}) collective-permute-start(bf16[4,128,384]{2,1,0:T(8,128)(2,1)S(1)} %depthwise.2), channel_id=1, source_target_pairs={{1,2},{2,1},{5,6},{6,5},{9,10},{10,9},{13,14},{14,13},{17,18},{18,... | collective-permute-start | bytes 1179656 | tf_op jit(solution)/shard_map/ppermute | solution.py:211
  23.8 5.0 %collective-permute-done.7.refs_8_ = bf16[192,1536]{1,0:T(8,128)(2,1)S(1)} collective-permute-done((bf16[192,1536]{1,0:T(8,128)(2,1)}, bf16[192,1536]{1,0:T(8,128)(2,1)S(1)}, u32[]{:S(2)}, u32[]{:S(2)}) %collective-permute-start.7) | collective-permute-done | bytes 589856 | tf_op jit(solution)/shard_map/ppermute | solution.py:232
  29.4 4.4 %depthwise.3 = bf16[4,128,384]{2,1,0:T(8,128)(2,1)S(1)} custom-call(bf16[8,384,128]{2,1,0:T(8,128)(2,1)S(1)} %copy-done, bf16[3,384,128]{2,1,0:T(8,128)(2,1)S(1)} %collective-permute-done.25.refs_1_, f32[49,384]{1,0:T(8,128)S(1)} %bitcast.17, f32[1,384]{1,0:T(1,128)S(1)} %broadcast_in_dim.8.refs_3_), custom_call_target="tpu_custom_call" | custom-call | flops 19267584 | bytes 786432 | tf_op jit(solution)/shard_map/depthwise/pallas_call | solution.py:62
  33.9 1.6 %collective-permute-start.26 = (bf16[4,128,384]{2,1,0:T(8,128)(2,1)S(1)}, bf16[4,128,384]{2,1,0:T(8,128)(2,1)S(1)}, u32[]{:S(2)}, u32[]{:S(2)}) collective-permute-start(bf16[4,128,384]{2,1,0:T(8,128)(2,1)S(1)} %depthwise.3), channel_id=1, source_target_pairs={{0,1},{1,0},{2,3},{3,2},{4,5},{5,4},{6,7},{7,6},{8,9},{9,8},{10,11... | collective-permute-start | bytes 1179656 | tf_op jit(solution)/shard_map/ppermute | solution.py:210
  35.5 3.1 %collective-permute-done.14.refs_16_ = bf16[192,1536]{1,0:T(8,128)(2,1)S(1)} collective-permute-done((bf16[192,1536]{1,0:T(8,128)(2,1)}, bf16[192,1536]{1,0:T(8,128)(2,1)S(1)}, u32[]{:S(2)}, u32[]{:S(2)}) %collective-permute-start.14) | collective-permute-done | bytes 589856 | tf_op jit(solution)/shard_map/ppermute | solution.py:232
  38.6 3.5 %collective-permute-start.27 = (bf16[4,128,384]{2,1,0:T(8,128)(2,1)S(1)}, bf16[4,128,384]{2,1,0:T(8,128)(2,1)S(1)}, u32[]{:S(2)}, u32[]{:S(2)}) collective-permute-start(bf16[4,128,384]{2,1,0:T(8,128)(2,1)S(1)} %depthwise.3), channel_id=1, source_target_pairs={{1,2},{2,1},{5,6},{6,5},{9,10},{10,9},{13,14},{14,13},{17,18},{18,... | collective-permute-start | bytes 1179656 | tf_op jit(solution)/shard_map/ppermute | solution.py:211
  42.1 1.3 collective-permute-start.3
  43.5 2.9 %collective-permute-start.4 = (bf16[4,128,384]{2,1,0:T(8,128)(2,1)S(1)}, bf16[4,128,384]{2,1,0:T(8,128)(2,1)S(1)}, u32[]{:S(2)}, u32[]{:S(2)}) collective-permute-start(bf16[4,128,384]{2,1,0:T(8,128)(2,1)S(1)} %collective-permute-done.1), channel_id=1, source_target_pairs={{1,2},{2,1},{5,6},{6,5},{9,10},{10,9},{13,14},{14,13},{17,18},{18,... | collective-permute-start | bytes 1179656 | tf_op jit(solution)/shard_map/ppermute | solution.py:212
  47.6 4.9 %collective-permute-done.27 = bf16[4,128,384]{2,1,0:T(8,128)(2,1)S(1)} collective-permute-done((bf16[4,128,384]{2,1,0:T(8,128)(2,1)S(1)}, bf16[4,128,384]{2,1,0:T(8,128)(2,1)S(1)}, u32[]{:S(2)}, u32[]{:S(2)}) %collective-permute-start.27) | collective-permute-done | bytes 393248 | tf_op jit(solution)/shard_map/ppermute | solution.py:211
  52.6 3.5 %collective-permute-start.29 = (bf16[4,128,384]{2,1,0:T(8,128)(2,1)S(1)}, bf16[4,128,384]{2,1,0:T(8,128)(2,1)S(1)}, u32[]{:S(2)}, u32[]{:S(2)}) collective-permute-start(bf16[4,128,384]{2,1,0:T(8,128)(2,1)S(1)} %collective-permute-done.26), channel_id=1, source_target_pairs={{1,2},{2,1},{5,6},{6,5},{9,10},{10,9},{13,14},{14,13},{17,18},{18,... | collective-permute-start | bytes 1179656 | tf_op jit(solution)/shard_map/ppermute | solution.py:212
  56.1 4.5 %collective-permute-done.4 = bf16[4,128,384]{2,1,0:T(8,128)(2,1)S(1)} collective-permute-done((bf16[4,128,384]{2,1,0:T(8,128)(2,1)S(1)}, bf16[4,128,384]{2,1,0:T(8,128)(2,1)S(1)}, u32[]{:S(2)}, u32[]{:S(2)}) %collective-permute-start.4) | collective-permute-done | bytes 393248 | tf_op jit(solution)/shard_map/ppermute | solution.py:212
  60.6 5.1 %collective-permute-done.29 = bf16[4,128,384]{2,1,0:T(8,128)(2,1)S(1)} collective-permute-done((bf16[4,128,384]{2,1,0:T(8,128)(2,1)S(1)}, bf16[4,128,384]{2,1,0:T(8,128)(2,1)S(1)}, u32[]{:S(2)}, u32[]{:S(2)}) %collective-permute-start.29) | collective-permute-done | bytes 393248 | tf_op jit(solution)/shard_map/ppermute | solution.py:212
  71.5 6.0 %collective-permute-done.5 = bf16[4,128,384]{2,1,0:T(8,128)(2,1)S(1)} collective-permute-done((bf16[4,128,384]{2,1,0:T(8,128)(2,1)S(1)}, bf16[4,128,384]{2,1,0:T(8,128)(2,1)S(1)}, u32[]{:S(2)}, u32[]{:S(2)}) %collective-permute-start.5) | collective-permute-done | bytes 393248 | tf_op jit(solution)/shard_map/ppermute | solution.py:214
  78.5 9.1 %mlp.2 = (bf16[4,384,128]{2,1,0:T(8,128)(2,1)S(1)}, bf16[4,384,128]{2,1,0:T(8,128)(2,1)S(1)}, bf16[4,384,128]{2,1,0:T(8,128)(2,1)S(1)}, bf16[4,384,128]{2,1,0:T(8,128)(2,1)S(1)}) custom-call(bf16[512,384]{1,0:T(8,128)(2,1)S(1)} %bitcast.15, bf16[512,384]{1,0:T(8,128)(2,1)S(1)} %bitcast.21, bf16[512,384]{1,0:T(8,128)(2,1)S(1)} %bitcast.20, ...), custom_call_target="tpu_custom_call" | custom-call | flops 4831838208 | bytes 12582912 | tf_op jit(solution)/shard_map/mlp/pallas_call | solution.py:172
  90.2 3.5 %collective-permute-done.30 = bf16[4,128,384]{2,1,0:T(8,128)(2,1)S(1)} collective-permute-done((bf16[4,128,384]{2,1,0:T(8,128)(2,1)S(1)}, bf16[4,128,384]{2,1,0:T(8,128)(2,1)S(1)}, u32[]{:S(2)}, u32[]{:S(2)}) %collective-permute-start.30) | collective-permute-done | bytes 393248 | tf_op jit(solution)/shard_map/ppermute | solution.py:214
  93.8 9.1 %mlp.3 = (bf16[4,384,128]{2,1,0:T(8,128)(2,1)S(1)}, bf16[4,384,128]{2,1,0:T(8,128)(2,1)S(1)}, bf16[4,384,128]{2,1,0:T(8,128)(2,1)S(1)}, bf16[4,384,128]{2,1,0:T(8,128)(2,1)S(1)}) custom-call(bf16[512,384]{1,0:T(8,128)(2,1)S(1)} %bitcast.14, bf16[512,384]{1,0:T(8,128)(2,1)S(1)} %bitcast.18, bf16[512,384]{1,0:T(8,128)(2,1)S(1)} %bitcast.19, ...), custom_call_target="tpu_custom_call" | custom-call | flops 4831838208 | bytes 12582912 | tf_op jit(solution)/shard_map/mlp/pallas_call | solution.py:172
  105.6 3.5 %collective-permute-start.23 = (bf16[4,384,128]{2,1,0:T(8,128)(2,1)S(1)}, bf16[4,384,128]{2,1,0:T(8,128)(2,1)S(1)}, u32[]{:S(2)}, u32[]{:S(2)}) collective-permute-start(bf16[4,384,128]{2,1,0:T(8,128)(2,1)S(1)} %add_convert_fusion.6), channel_id=1, source_target_pairs={{1,2},{2,1},{5,6},{6,5},{9,10},{10,9},{13,14},{14,13},{17,18},{18,... | collective-permute-start | bytes 1179656 | tf_op jit(solution)/shard_map/ppermute | solution.py:225
  109.2 3.4 %collective-permute-start.21 = (bf16[4,384,128]{2,1,0:T(8,128)(2,1)S(1)}, bf16[4,384,128]{2,1,0:T(8,128)(2,1)S(1)}, u32[]{:S(2)}, u32[]{:S(2)}) collective-permute-start(bf16[4,384,128]{2,1,0:T(8,128)(2,1)S(1)} %add_convert_fusion.7), channel_id=1, source_target_pairs={{1,2},{2,1},{5,6},{6,5},{9,10},{10,9},{13,14},{14,13},{17,18},{18,... | collective-permute-start | bytes 1179656 | tf_op jit(solution)/shard_map/ppermute | solution.py:226
  112.6 4.8 %collective-permute-done.33 = bf16[4,384,128]{2,1,0:T(8,128)(2,1)S(1)} collective-permute-done((bf16[4,384,128]{2,1,0:T(8,128)(2,1)S(1)}, bf16[4,384,128]{2,1,0:T(8,128)(2,1)S(1)}, u32[]{:S(2)}, u32[]{:S(2)}) %collective-permute-start.33) | collective-permute-done | bytes 393248 | tf_op jit(solution)/shard_map/ppermute | solution.py:223
  117.5 3.5 %collective-permute-start.34 = (bf16[4,384,128]{2,1,0:T(8,128)(2,1)S(1)}, bf16[4,384,128]{2,1,0:T(8,128)(2,1)S(1)}, u32[]{:S(2)}, u32[]{:S(2)}) collective-permute-start(bf16[4,384,128]{2,1,0:T(8,128)(2,1)S(1)} %add_convert_fusion.2), channel_id=1, source_target_pairs={{1,2},{2,1},{5,6},{6,5},{9,10},{10,9},{13,14},{14,13},{17,18},{18,... | collective-permute-start | bytes 1179656 | tf_op jit(solution)/shard_map/ppermute | solution.py:225
  121.0 3.9 %collective-permute-done.31 = bf16[4,384,128]{2,1,0:T(8,128)(2,1)S(1)} collective-permute-done((bf16[4,384,128]{2,1,0:T(8,128)(2,1)S(1)}, bf16[4,384,128]{2,1,0:T(8,128)(2,1)S(1)}, u32[]{:S(2)}, u32[]{:S(2)}) %collective-permute-start.31) | collective-permute-done | bytes 393248 | tf_op jit(solution)/shard_map/ppermute | solution.py:224
  125.8 3.5 %collective-permute-start.32 = (bf16[4,384,128]{2,1,0:T(8,128)(2,1)}, bf16[4,384,128]{2,1,0:T(8,128)(2,1)S(1)}, u32[]{:S(2)}, u32[]{:S(2)}) collective-permute-start(bf16[4,384,128]{2,1,0:T(8,128)(2,1)} %add_convert_fusion.3), channel_id=1, source_target_pairs={{1,2},{2,1},{5,6},{6,5},{9,10},{10,9},{13,14},{14,13},{17,18},{18,... | collective-permute-start | bytes 1179656 | tf_op jit(solution)/shard_map/ppermute | solution.py:226
  130.1 6.3 %collective-permute-done.34 = bf16[4,384,128]{2,1,0:T(8,128)(2,1)S(1)} collective-permute-done((bf16[4,384,128]{2,1,0:T(8,128)(2,1)S(1)}, bf16[4,384,128]{2,1,0:T(8,128)(2,1)S(1)}, u32[]{:S(2)}, u32[]{:S(2)}) %collective-permute-start.34) | collective-permute-done | bytes 393248 | tf_op jit(solution)/shard_map/ppermute | solution.py:225
  137.3 6.1 %collective-permute-done.32 = bf16[4,384,128]{2,1,0:T(8,128)(2,1)S(1)} collective-permute-done((bf16[4,384,128]{2,1,0:T(8,128)(2,1)}, bf16[4,384,128]{2,1,0:T(8,128)(2,1)S(1)}, u32[]{:S(2)}, u32[]{:S(2)}) %collective-permute-start.32) | collective-permute-done | bytes 393248 | tf_op jit(solution)/shard_map/ppermute | solution.py:226
  143.4 5.3 %collective-permute-done.35 = bf16[4,384,128]{2,1,0:T(8,128)(2,1)S(1)} collective-permute-done((bf16[4,384,128]{2,1,0:T(8,128)(2,1)}, bf16[4,384,128]{2,1,0:T(8,128)(2,1)S(1)}, u32[]{:S(2)}, u32[]{:S(2)}) %collective-permute-start.35) | collective-permute-done | bytes 393248 | tf_op jit(solution)/shard_map/ppermute | solution.py:227
  148.7 1.4 add_convert_fusion.4
  (101 shorter events, 19.1 us)
Async XLA Ops:
  1.2 8.7 %collective-permute-start = (bf16[3,384,128]{2,1,0:T(8,128)(2,1)S(1)}, bf16[3,384,128]{2,1,0:T(8,128)(2,1)S(1)}, u32[]{:S(2)}, u32[]{:S(2)}) collective-permute-start(bf16[3,384,128]{2,1,0:T(8,128)(2,1)S(1)} %get-tuple-element.23), channel_id=1, source_target_pairs={{0,4},{4,8},{8,12},{12,16},{16,20},{20,24},{24,28},{1,5},{5,9},{9,... | collective-permute-start | bytes 884744 | tf_op jit(solution)/shard_map/ppermute | solution.py:249
  4.3 16.0 %collective-permute-start.6 = (bf16[192,1536]{1,0:T(8,128)(2,1)}, bf16[192,1536]{1,0:T(8,128)(2,1)S(1)}, u32[]{:S(2)}, u32[]{:S(2)}) collective-permute-start(bf16[192,1536]{1,0:T(8,128)(2,1)} %refs_6_.3), channel_id=1, source_target_pairs={{0,4},{4,0},{8,12},{12,8},{16,20},{20,16},{24,28},{28,24},{1,5},{5... | collective-permute-start | bytes 1769480 | tf_op jit(solution)/shard_map/ppermute | solution.py:232
  6.7 22.1 %collective-permute-start.7 = (bf16[192,1536]{1,0:T(8,128)(2,1)}, bf16[192,1536]{1,0:T(8,128)(2,1)S(1)}, u32[]{:S(2)}, u32[]{:S(2)}) collective-permute-start(bf16[192,1536]{1,0:T(8,128)(2,1)} %refs_6_.3), channel_id=1, source_target_pairs={{0,8},{4,12},{8,0},{12,4},{16,24},{20,28},{24,16},{28,20},{1,9},{5... | collective-permute-start | bytes 1769480 | tf_op jit(solution)/shard_map/ppermute | solution.py:232
  8.4 20.5 %collective-permute-start.9 = (bf16[192,1536]{1,0:T(8,128)(2,1)}, bf16[192,1536]{1,0:T(8,128)(2,1)S(1)}, u32[]{:S(2)}, u32[]{:S(2)}) collective-permute-start(bf16[192,1536]{1,0:T(8,128)(2,1)} %refs_6_.3), channel_id=1, source_target_pairs={{0,16},{4,20},{8,24},{12,28},{16,0},{20,4},{24,8},{28,12},{1,17},{... | collective-permute-start | bytes 1769480 | tf_op jit(solution)/shard_map/ppermute | solution.py:232
  9.9 23.9 %collective-permute-start.13 = (bf16[192,1536]{1,0:T(8,128)(2,1)}, bf16[192,1536]{1,0:T(8,128)(2,1)S(1)}, u32[]{:S(2)}, u32[]{:S(2)}) collective-permute-start(bf16[192,1536]{1,0:T(8,128)(2,1)} %bitcast.28), channel_id=1, source_target_pairs={{0,4},{4,0},{8,12},{12,8},{16,20},{20,16},{24,28},{28,24},{1,5},{5... | collective-permute-start | bytes 1769480 | tf_op jit(solution)/shard_map/ppermute | solution.py:232
  9.9 28.7 %collective-permute-start.14 = (bf16[192,1536]{1,0:T(8,128)(2,1)}, bf16[192,1536]{1,0:T(8,128)(2,1)S(1)}, u32[]{:S(2)}, u32[]{:S(2)}) collective-permute-start(bf16[192,1536]{1,0:T(8,128)(2,1)} %bitcast.29), channel_id=1, source_target_pairs={{0,8},{4,12},{8,0},{12,4},{16,24},{20,28},{24,16},{28,20},{1,9},{5... | collective-permute-start | bytes 1769480 | tf_op jit(solution)/shard_map/ppermute | solution.py:232
  20.2 21.9 %collective-permute-start.2 = (bf16[4,128,384]{2,1,0:T(8,128)(2,1)S(1)}, bf16[4,128,384]{2,1,0:T(8,128)(2,1)S(1)}, u32[]{:S(2)}, u32[]{:S(2)}) collective-permute-start(bf16[4,128,384]{2,1,0:T(8,128)(2,1)S(1)} %depthwise.2), channel_id=1, source_target_pairs={{1,2},{2,1},{5,6},{6,5},{9,10},{10,9},{13,14},{14,13},{17,18},{18,... | collective-permute-start | bytes 1179656 | tf_op jit(solution)/shard_map/ppermute | solution.py:211
  28.8 17.5 %collective-permute-start.16 = (bf16[192,1536]{1,0:T(8,128)(2,1)S(1)}, bf16[192,1536]{1,0:T(8,128)(2,1)S(1)}, u32[]{:S(2)}, u32[]{:S(2)}) collective-permute-start(bf16[192,1536]{1,0:T(8,128)(2,1)S(1)} %bitcast.32), channel_id=1, source_target_pairs={{0,16},{4,20},{8,24},{12,28},{16,0},{20,4},{24,8},{28,12},{1,17},{... | collective-permute-start | bytes 1769480 | tf_op jit(solution)/shard_map/ppermute | solution.py:232
  29.0 14.5 %collective-permute-start.1 = (bf16[4,128,384]{2,1,0:T(8,128)(2,1)S(1)}, bf16[4,128,384]{2,1,0:T(8,128)(2,1)S(1)}, u32[]{:S(2)}, u32[]{:S(2)}) collective-permute-start(bf16[4,128,384]{2,1,0:T(8,128)(2,1)S(1)} %depthwise.2), channel_id=1, source_target_pairs={{0,1},{1,0},{2,3},{3,2},{4,5},{5,4},{6,7},{7,6},{8,9},{9,8},{10,11... | collective-permute-start | bytes 1179656 | tf_op jit(solution)/shard_map/ppermute | solution.py:210
  33.9 12.6 %collective-permute-start.26 = (bf16[4,128,384]{2,1,0:T(8,128)(2,1)S(1)}, bf16[4,128,384]{2,1,0:T(8,128)(2,1)S(1)}, u32[]{:S(2)}, u32[]{:S(2)}) collective-permute-start(bf16[4,128,384]{2,1,0:T(8,128)(2,1)S(1)} %depthwise.3), channel_id=1, source_target_pairs={{0,1},{1,0},{2,3},{3,2},{4,5},{5,4},{6,7},{7,6},{8,9},{9,8},{10,11... | collective-permute-start | bytes 1179656 | tf_op jit(solution)/shard_map/ppermute | solution.py:210
  38.6 13.9 %collective-permute-start.27 = (bf16[4,128,384]{2,1,0:T(8,128)(2,1)S(1)}, bf16[4,128,384]{2,1,0:T(8,128)(2,1)S(1)}, u32[]{:S(2)}, u32[]{:S(2)}) collective-permute-start(bf16[4,128,384]{2,1,0:T(8,128)(2,1)S(1)} %depthwise.3), channel_id=1, source_target_pairs={{1,2},{2,1},{5,6},{6,5},{9,10},{10,9},{13,14},{14,13},{17,18},{18,... | collective-permute-start | bytes 1179656 | tf_op jit(solution)/shard_map/ppermute | solution.py:211
  42.1 10.4 %collective-permute-start.3 = (bf16[4,128,384]{2,1,0:T(8,128)(2,1)S(1)}, bf16[4,128,384]{2,1,0:T(8,128)(2,1)S(1)}, u32[]{:S(2)}, u32[]{:S(2)}) collective-permute-start(bf16[4,128,384]{2,1,0:T(8,128)(2,1)S(1)} %collective-permute-done.2), channel_id=1, source_target_pairs={{1,0},{2,3},{5,4},{6,7},{9,8},{10,11},{13,12},{14,15},{17,16},{18,... | collective-permute-start | bytes 1179656 | tf_op jit(solution)/shard_map/ppermute | solution.py:213
  43.5 17.1 %collective-permute-start.4 = (bf16[4,128,384]{2,1,0:T(8,128)(2,1)S(1)}, bf16[4,128,384]{2,1,0:T(8,128)(2,1)S(1)}, u32[]{:S(2)}, u32[]{:S(2)}) collective-permute-start(bf16[4,128,384]{2,1,0:T(8,128)(2,1)S(1)} %collective-permute-done.1), channel_id=1, source_target_pairs={{1,2},{2,1},{5,6},{6,5},{9,10},{10,9},{13,14},{14,13},{17,18},{18,... | collective-permute-start | bytes 1179656 | tf_op jit(solution)/shard_map/ppermute | solution.py:212
  46.4 19.3 %collective-permute-start.8 = (bf16[192,1536]{1,0:T(8,128)(2,1)S(1)}, bf16[192,1536]{1,0:T(8,128)(2,1)S(1)}, u32[]{:S(2)}, u32[]{:S(2)}) collective-permute-start(bf16[192,1536]{1,0:T(8,128)(2,1)S(1)} %collective-permute-done.7.refs_8_), channel_id=1, source_target_pairs={{0,4},{4,0},{8,12},{12,8},{16,20},{20,16},{24,28},{28,24},{1,5},{5... | collective-permute-start | bytes 1769480 | tf_op jit(solution)/shard_map/ppermute | solution.py:232
  46.4 19.8 %collective-permute-start.11 = (bf16[192,1536]{1,0:T(8,128)(2,1)S(1)}, bf16[192,1536]{1,0:T(8,128)(2,1)S(1)}, u32[]{:S(2)}, u32[]{:S(2)}) collective-permute-start(bf16[192,1536]{1,0:T(8,128)(2,1)S(1)} %collective-permute-done.7.refs_8_), channel_id=1, source_target_pairs={{0,16},{4,20},{8,24},{12,28},{16,0},{20,4},{24,8},{28,12},{1,17},{... | collective-permute-start | bytes 1769480 | tf_op jit(solution)/shard_map/ppermute | solution.py:232
  52.6 13.7 %collective-permute-start.18 = (bf16[192,1536]{1,0:T(8,128)(2,1)S(1)}, bf16[192,1536]{1,0:T(8,128)(2,1)S(1)}, u32[]{:S(2)}, u32[]{:S(2)}) collective-permute-start(bf16[192,1536]{1,0:T(8,128)(2,1)S(1)} %collective-permute-done.16.refs_18_), channel_id=1, source_target_pairs={{0,8},{4,12},{8,0},{12,4},{16,24},{20,28},{24,16},{28,20},{1,9},{5... | collective-permute-start | bytes 1769480 | tf_op jit(solution)/shard_map/ppermute | solution.py:232
  52.6 13.1 %collective-permute-start.29 = (bf16[4,128,384]{2,1,0:T(8,128)(2,1)S(1)}, bf16[4,128,384]{2,1,0:T(8,128)(2,1)S(1)}, u32[]{:S(2)}, u32[]{:S(2)}) collective-permute-start(bf16[4,128,384]{2,1,0:T(8,128)(2,1)S(1)} %collective-permute-done.26), channel_id=1, source_target_pairs={{1,2},{2,1},{5,6},{6,5},{9,10},{10,9},{13,14},{14,13},{17,18},{18,... | collective-permute-start | bytes 1179656 | tf_op jit(solution)/shard_map/ppermute | solution.py:212
  66.2 11.2 %collective-permute-start.12 = (bf16[192,1536]{1,0:T(8,128)(2,1)S(1)}, bf16[192,1536]{1,0:T(8,128)(2,1)S(1)}, u32[]{:S(2)}, u32[]{:S(2)}) collective-permute-start(bf16[192,1536]{1,0:T(8,128)(2,1)S(1)} %collective-permute-done.11.refs_12_), channel_id=1, source_target_pairs={{0,4},{4,0},{8,12},{12,8},{16,20},{20,16},{24,28},{28,24},{1,5},{5... | collective-permute-start | bytes 1769480 | tf_op jit(solution)/shard_map/ppermute | solution.py:232
  66.3 11.2 %collective-permute-start.19 = (bf16[192,1536]{1,0:T(8,128)(2,1)S(1)}, bf16[192,1536]{1,0:T(8,128)(2,1)S(1)}, u32[]{:S(2)}, u32[]{:S(2)}) collective-permute-start(bf16[192,1536]{1,0:T(8,128)(2,1)S(1)} %collective-permute-done.18.refs_20_), channel_id=1, source_target_pairs={{0,4},{4,0},{8,12},{12,8},{16,20},{20,16},{24,28},{28,24},{1,5},{5... | collective-permute-start | bytes 1769480 | tf_op jit(solution)/shard_map/ppermute | solution.py:232
  66.7 10.7 %collective-permute-start.5 = (bf16[4,128,384]{2,1,0:T(8,128)(2,1)S(1)}, bf16[4,128,384]{2,1,0:T(8,128)(2,1)S(1)}, u32[]{:S(2)}, u32[]{:S(2)}) collective-permute-start(bf16[4,128,384]{2,1,0:T(8,128)(2,1)S(1)} %collective-permute-done.4), channel_id=1, source_target_pairs={{1,0},{2,3},{5,4},{6,7},{9,8},{10,11},{13,12},{14,15},{17,16},{18,... | collective-permute-start | bytes 1179656 | tf_op jit(solution)/shard_map/ppermute | solution.py:214
  68.8 21.4 %collective-permute-start.28 = (bf16[4,128,384]{2,1,0:T(8,128)(2,1)S(1)}, bf16[4,128,384]{2,1,0:T(8,128)(2,1)S(1)}, u32[]{:S(2)}, u32[]{:S(2)}) collective-permute-start(bf16[4,128,384]{2,1,0:T(8,128)(2,1)S(1)} %collective-permute-done.27), channel_id=1, source_target_pairs={{1,0},{2,3},{5,4},{6,7},{9,8},{10,11},{13,12},{14,15},{17,16},{18,... | collective-permute-start | bytes 1179656 | tf_op jit(solution)/shard_map/ppermute | solution.py:213
  70.1 23.6 %collective-permute-start.30 = (bf16[4,128,384]{2,1,0:T(8,128)(2,1)S(1)}, bf16[4,128,384]{2,1,0:T(8,128)(2,1)S(1)}, u32[]{:S(2)}, u32[]{:S(2)}) collective-permute-start(bf16[4,128,384]{2,1,0:T(8,128)(2,1)S(1)} %collective-permute-done.29), channel_id=1, source_target_pairs={{1,0},{2,3},{5,4},{6,7},{9,8},{10,11},{13,12},{14,15},{17,16},{18,... | collective-permute-start | bytes 1179656 | tf_op jit(solution)/shard_map/ppermute | solution.py:214
  87.6 17.9 %collective-permute-start.22 = (bf16[4,384,128]{2,1,0:T(8,128)(2,1)S(1)}, bf16[4,384,128]{2,1,0:T(8,128)(2,1)S(1)}, u32[]{:S(2)}, u32[]{:S(2)}) collective-permute-start(bf16[4,384,128]{2,1,0:T(8,128)(2,1)S(1)} %get-tuple-element.16), channel_id=1, source_target_pairs={{0,1},{3,2},{4,5},{7,6},{8,9},{11,10},{12,13},{15,14},{16,17},{19,... | collective-permute-start | bytes 1179656 | tf_op jit(solution)/shard_map/ppermute | solution.py:223
  88.9 20.2 %collective-permute-start.20 = (bf16[4,384,128]{2,1,0:T(8,128)(2,1)S(1)}, bf16[4,384,128]{2,1,0:T(8,128)(2,1)S(1)}, u32[]{:S(2)}, u32[]{:S(2)}) collective-permute-start(bf16[4,384,128]{2,1,0:T(8,128)(2,1)S(1)} %get-tuple-element.14), channel_id=1, source_target_pairs={{0,1},{3,2},{4,5},{7,6},{8,9},{11,10},{12,13},{15,14},{16,17},{19,... | collective-permute-start | bytes 1179656 | tf_op jit(solution)/shard_map/ppermute | solution.py:224
  102.9 14.5 %collective-permute-start.33 = (bf16[4,384,128]{2,1,0:T(8,128)(2,1)S(1)}, bf16[4,384,128]{2,1,0:T(8,128)(2,1)S(1)}, u32[]{:S(2)}, u32[]{:S(2)}) collective-permute-start(bf16[4,384,128]{2,1,0:T(8,128)(2,1)S(1)} %get-tuple-element.20), channel_id=1, source_target_pairs={{0,1},{3,2},{4,5},{7,6},{8,9},{11,10},{12,13},{15,14},{16,17},{19,... | collective-permute-start | bytes 1179656 | tf_op jit(solution)/shard_map/ppermute | solution.py:223
  104.2 20.7 %collective-permute-start.31 = (bf16[4,384,128]{2,1,0:T(8,128)(2,1)S(1)}, bf16[4,384,128]{2,1,0:T(8,128)(2,1)S(1)}, u32[]{:S(2)}, u32[]{:S(2)}) collective-permute-start(bf16[4,384,128]{2,1,0:T(8,128)(2,1)S(1)} %get-tuple-element.18), channel_id=1, source_target_pairs={{0,1},{3,2},{4,5},{7,6},{8,9},{11,10},{12,13},{15,14},{16,17},{19,... | collective-permute-start | bytes 1179656 | tf_op jit(solution)/shard_map/ppermute | solution.py:224
  105.6 23.6 %collective-permute-start.23 = (bf16[4,384,128]{2,1,0:T(8,128)(2,1)S(1)}, bf16[4,384,128]{2,1,0:T(8,128)(2,1)S(1)}, u32[]{:S(2)}, u32[]{:S(2)}) collective-permute-start(bf16[4,384,128]{2,1,0:T(8,128)(2,1)S(1)} %add_convert_fusion.6), channel_id=1, source_target_pairs={{1,2},{2,1},{5,6},{6,5},{9,10},{10,9},{13,14},{14,13},{17,18},{18,... | collective-permute-start | bytes 1179656 | tf_op jit(solution)/shard_map/ppermute | solution.py:225
  109.2 28.1 %collective-permute-start.21 = (bf16[4,384,128]{2,1,0:T(8,128)(2,1)S(1)}, bf16[4,384,128]{2,1,0:T(8,128)(2,1)S(1)}, u32[]{:S(2)}, u32[]{:S(2)}) collective-permute-start(bf16[4,384,128]{2,1,0:T(8,128)(2,1)S(1)} %add_convert_fusion.7), channel_id=1, source_target_pairs={{1,2},{2,1},{5,6},{6,5},{9,10},{10,9},{13,14},{14,13},{17,18},{18,... | collective-permute-start | bytes 1179656 | tf_op jit(solution)/shard_map/ppermute | solution.py:226
  117.5 18.9 %collective-permute-start.34 = (bf16[4,384,128]{2,1,0:T(8,128)(2,1)S(1)}, bf16[4,384,128]{2,1,0:T(8,128)(2,1)S(1)}, u32[]{:S(2)}, u32[]{:S(2)}) collective-permute-start(bf16[4,384,128]{2,1,0:T(8,128)(2,1)S(1)} %add_convert_fusion.2), channel_id=1, source_target_pairs={{1,2},{2,1},{5,6},{6,5},{9,10},{10,9},{13,14},{14,13},{17,18},{18,... | collective-permute-start | bytes 1179656 | tf_op jit(solution)/shard_map/ppermute | solution.py:225
  125.8 17.6 %collective-permute-start.32 = (bf16[4,384,128]{2,1,0:T(8,128)(2,1)}, bf16[4,384,128]{2,1,0:T(8,128)(2,1)S(1)}, u32[]{:S(2)}, u32[]{:S(2)}) collective-permute-start(bf16[4,384,128]{2,1,0:T(8,128)(2,1)} %add_convert_fusion.3), channel_id=1, source_target_pairs={{1,2},{2,1},{5,6},{6,5},{9,10},{10,9},{13,14},{14,13},{17,18},{18,... | collective-permute-start | bytes 1179656 | tf_op jit(solution)/shard_map/ppermute | solution.py:226
  130.1 13.3 %collective-permute-start.24 = (bf16[4,384,128]{2,1,0:T(8,128)(2,1)}, bf16[4,384,128]{2,1,0:T(8,128)(2,1)S(1)}, u32[]{:S(2)}, u32[]{:S(2)}) collective-permute-start(bf16[4,384,128]{2,1,0:T(8,128)(2,1)} %add_convert_fusion.5), channel_id=1, source_target_pairs={{0,1},{1,0},{2,3},{3,2},{4,5},{5,4},{6,7},{7,6},{8,9},{9,8},{10,11... | collective-permute-start | bytes 1179656 | tf_op jit(solution)/shard_map/ppermute | solution.py:227
  137.3 11.4 %collective-permute-start.35 = (bf16[4,384,128]{2,1,0:T(8,128)(2,1)}, bf16[4,384,128]{2,1,0:T(8,128)(2,1)S(1)}, u32[]{:S(2)}, u32[]{:S(2)}) collective-permute-start(bf16[4,384,128]{2,1,0:T(8,128)(2,1)} %add_convert_fusion.1), channel_id=1, source_target_pairs={{0,1},{1,0},{2,3},{3,2},{4,5},{5,4},{6,7},{7,6},{8,9},{9,8},{10,11... | collective-permute-start | bytes 1179656 | tf_op jit(solution)/shard_map/ppermute | solution.py:227
  (26 other events, 459.3 us)

commit v3 on v2

--- a/solution.py
+++ b/solution.py
@@ -9,7 +9,6 @@
 
 SIDE = 7
 REACH = SIDE // 2
-CHUNKS = 2
 VMEM_LIMIT = 48 * 1024 * 1024
 EPSILON = 1e-06
 
@@ -44,7 +43,7 @@
     lax.fori_loop(0, width // tile, one_tile, 0)
 
 
-def conv_chunk(first, rows, low, features, high, taps, bias):
+def conv_chunk(first, rows, *, low, features, high, taps, bias):
     height, slab, width = features.shape
     names, plan = ["features"], []
     for row in range(first - REACH, first + rows + REACH):
@@ -82,16 +81,29 @@
     return z ^ 1, jnp.where(low_half, 2, 1), jnp.where(low_half, 3, 0)
 
 
+def weight_pieces(parts, shard):
+    own, x, y, in_xy, out_xy, others, other_xy = parts
+    three = [(own, 0), (x, 2), (y, 4)]
+    ins = [(part, 0, k) for part, k in three] + [(in_xy, 0, 6), (other_xy, 0, 7)]
+    outs = [(part, shard, k) for part, k in three] + [(out_xy, 0, 6), (other_xy, shard, 7)]
+    for i, k in enumerate((1, 3, 5)):
+        ins.append((others, 2 * shard * i, k))
+        outs.append((others, 2 * shard * i + shard, k))
+    return ins, outs
+
+
 def mlp_kernel(*refs):
     own, near, mid_inner, mid_outer, far_inner, far_outer = refs[:6]
-    w_in_parts, w_out_parts = refs[6:14], refs[14:22]
-    gain_ref, shift_ref, b_in_ref = refs[22:25]
-    out_refs = refs[25:29]
-    x, w_in, w_out, hidden, x_sem, in_sem, out_sem = refs[29:]
+    refs = refs[6:]
+    parts, refs = refs[: len(refs) - 14], refs[len(refs) - 14 :]
+    shard = parts[0].shape[0] // 2
+    w_in_parts, w_out_parts = weight_pieces(parts, shard)
+    gain_ref, shift_ref, b_in_ref = refs[:3]
+    out_refs = refs[3:7]
+    x, w_in, w_out, hidden, x_sem, in_sem, out_sem = refs[7:]
     pixels, channels = x.shape
     slab = own.shape[1]
     units = hidden.shape[1]
-    shard = w_in_parts[0].shape[0]
     z, t = lax.axis_index("chan"), lax.axis_index("tile")
     pair, mid, far = line_places(z)
     inner = jnp.logical_or(z == 1, z == 2)
@@ -113,14 +125,15 @@
         slab_copy(mid_outer, mid, 2).start()
         slab_copy(far_outer, far, 3).start()
 
-    def shard_copy(part, target, k, sems):
+    def shard_copy(piece, target, sems):
+        part, first, k = piece
         at = pl.ds(pl.multiple_of((t ^ k) * shard, 16), shard)
-        return pltpu.make_async_copy(part, target.at[at, :], sems.at[k])
-
-    for k, part in enumerate(w_in_parts):
-        shard_copy(part, w_in, k, in_sem).start()
-    for k, part in enumerate(w_out_parts):
-        shard_copy(part, w_out, k, out_sem).start()
+        return pltpu.make_async_copy(part.at[first : first + shard, :], target.at[at, :], sems.at[k])
+
+    for piece in w_in_parts:
+        shard_copy(piece, w_in, in_sem).start()
+    for piece in w_out_parts:
+        shard_copy(piece, w_out, out_sem).start()
 
     slab_copy(own, z, 0).wait()
     slab_copy(near, pair, 1).wait()
@@ -141,8 +154,8 @@
 
     lax.fori_loop(0, pixels // step, normalize, 0)
 
-    for k, part in enumerate(w_in_parts):
-        shard_copy(part, w_in, k, in_sem).wait()
+    for piece in w_in_parts:
+        shard_copy(piece, w_in, in_sem).wait()
     block = 256
     for f in range(0, units, block):
         pre_act = jnp.dot(x[...], w_in[:, f : f + block], preferred_element_type=jnp.float32)
@@ -150,8 +163,8 @@
         gelu = pre_act * (lax.erf(pre_act * (0.5**0.5)) * 0.5 + 0.5)
         hidden[:, f : f + block] = gelu.astype(hidden.dtype)
 
-    for k, part in enumerate(w_out_parts):
-        shard_copy(part, w_out, k, out_sem).wait()
+    for piece in w_out_parts:
+        shard_copy(piece, w_out, out_sem).wait()
     for out_ref, place in zip(out_refs, (far, mid, pair, z), strict=True):
         rows, _, width = out_ref.shape
         at = pl.ds(pl.multiple_of(place * slab, 16), slab)
@@ -162,16 +175,17 @@
             out_ref[row] = partial[:, row * width : (row + 1) * width].astype(out_ref.dtype)
 
 
-def mlp_chunk(slabs, w_in_parts, w_out_parts, gain, shift, b_in):
+def mlp_chunk(slabs, weights, gain, shift, b_in):
     rows, width, slab = slabs[0].shape
-    shard, units = w_in_parts[0].shape
-    channels = shard * len(w_in_parts)
+    shards = 8
+    units = weights[0].shape[1]
+    channels = slab * 4
     pixels = rows * width
     anywhere = pl.BlockSpec(memory_space=pl.ANY)
     whole = pl.BlockSpec(memory_space=pltpu.VMEM)
     return pl.pallas_call(
         mlp_kernel,
-        in_specs=[anywhere] * (len(slabs) + len(w_in_parts) + len(w_out_parts)) + [whole] * 3,
+        in_specs=[anywhere] * (len(slabs) + len(weights)) + [whole] * 3,
         out_specs=[whole] * 4,
         out_shape=[jax.ShapeDtypeStruct((rows, slab, width), jnp.bfloat16)] * 4,
         scratch_shapes=[
@@ -180,10 +194,10 @@
             pltpu.VMEM((channels, units), jnp.bfloat16),
             pltpu.VMEM((pixels, units), jnp.bfloat16),
             pltpu.SemaphoreType.DMA((4,)),
-            pltpu.SemaphoreType.DMA((len(w_in_parts),)),
-            pltpu.SemaphoreType.DMA((len(w_out_parts),)),
+            pltpu.SemaphoreType.DMA((shards,)),
+            pltpu.SemaphoreType.DMA((shards,)),
         ],
-        compiler_params=pltpu.CompilerParams(vmem_limit_bytes=VMEM_LIMIT),
+        compiler_params=pltpu.CompilerParams(vmem_limit_bytes=28 * 1024 * 1024),
         cost_estimate=pl.CostEstimate(
             flops=4 * pixels * channels * units,
             bytes_accessed=4 * channels * units + 4 * pixels * channels,
@@ -192,75 +206,101 @@
         name="mlp",
     )(
         *[s.reshape(pixels, slab) for s in slabs],
-        *w_in_parts,
-        *w_out_parts,
+        *weights,
         gain[None],
         shift[None],
         b_in[None],
     )
 
 
-PAIRS = [(0, 1), (1, 0), (2, 3), (3, 2)]
-MIDDLE = [(1, 2), (2, 1)]
-OUTWARD = [(1, 0), (2, 3)]
-INWARD = [(0, 1), (3, 2)]
-
-
-def gather_line(slab):
-    near = lax.ppermute(slab, "chan", PAIRS)
-    mid_inner = lax.ppermute(slab, "chan", MIDDLE)
-    far_inner = lax.ppermute(near, "chan", MIDDLE)
-    mid_outer = lax.ppermute(mid_inner, "chan", OUTWARD)
-    far_outer = lax.ppermute(far_inner, "chan", OUTWARD)
-    return slab, near, mid_inner, mid_outer, far_inner, far_outer
+def to_pair(array):
+    return lax.ppermute(array, "chan", [(0, 1), (1, 0), (2, 3), (3, 2)])
+
+
+def to_middle(array):
+    return lax.ppermute(array, "chan", [(1, 2), (2, 1)])
+
+
+def outward(array):
+    return lax.ppermute(array, "chan", [(1, 0), (2, 3)])
+
+
+def inward(array):
+    return lax.ppermute(array, "chan", [(0, 1), (3, 2)])
+
+
+def after(value, *others):
+    return lax.optimization_barrier((value, *others))[0] if others else value
 
 
 def add(a, b):
     return (a.astype(jnp.float32) + b.astype(jnp.float32)).astype(jnp.bfloat16)
 
 
-def scatter_line(far, mid, near, own):
-    far_in = lax.ppermute(far, "chan", INWARD)
-    mid_in = lax.ppermute(mid, "chan", INWARD)
-    far_across = lax.ppermute(add(far, far_in), "chan", MIDDLE)
-    mid_across = lax.ppermute(add(mid, mid_in), "chan", MIDDLE)
-    from_pair = lax.ppermute(add(near, far_across), "chan", PAIRS)
-    return own.astype(jnp.float32) + mid_across.astype(jnp.float32) + from_pair.astype(jnp.float32)
-
-
 def flipped(array, bit):
     return lax.ppermute(array, "tile", [(i, i ^ bit) for i in range(8)])
 
 
-def gather_shards(w_in, w_out):
-    in_x, in_y = flipped(w_in, 2), flipped(w_in, 4)
-    out_x, out_y = flipped(w_out, 2), flipped(w_out, 4)
-    in_xy, out_xy = flipped(in_x, 4), flipped(out_y, 2)
-    ins, outs = [w_in, in_x, in_y, in_xy], [w_out, out_x, out_y, out_xy]
-    ins = [part for mine in ins for part in (mine, flipped(mine, 1))]
-    outs = [part for mine in outs for part in (mine, flipped(mine, 1))]
-    return ins, outs
-
-
-def rims(features):
+def rims(top, bottom):
     count = lax.axis_size("tile")
     forward = [(i, i + 1) for i in range(count - 1)]
     backward = [(b, a) for a, b in forward]
-    low = lax.ppermute(features[-REACH:], "tile", forward)
-    high = lax.ppermute(features[:REACH], "tile", backward)
-    return low, high
+    return lax.ppermute(bottom, "tile", forward), lax.ppermute(top, "tile", backward)
 
 
 def local(features, dw_weight, dw_bias, ln_gain, ln_bias, w_in, b_in, w_out, b_out, gamma):
     height = features.shape[0]
-    low, high = rims(features)
-    w_in_parts, w_out_parts = gather_shards(w_in, w_out.T)
-    rows = height // CHUNKS
+    rows = height // 2
+    shard = w_in.shape[0]
+    conv = functools.partial(conv_chunk, features=features, taps=dw_weight.T, bias=dw_bias[None])
+    mlp = functools.partial(mlp_chunk, gain=ln_gain, shift=ln_bias, b_in=b_in)
+
+    low, high = rims(features[:REACH], features[-REACH:])
+    slab_0 = conv(0, rows, low=low, high=high)
+    slab_1 = conv(rows, rows, low=low, high=high)
+
+    own = jnp.concatenate([w_in, w_out.T], axis=0)
+    moving = after(own, low, high)
+    own_x, own_y = flipped(moving, 2), flipped(moving, 4)
+
+    near_0, mid_in_0 = to_pair(slab_0), to_middle(slab_0)
+    far_in_0, mid_out_0 = to_middle(near_0), outward(mid_in_0)
+    far_out_0 = outward(far_in_0)
+
+    begun = own_x, own_y, far_in_0, mid_out_0, slab_1
+    in_xy = flipped(after(own_x, *begun)[:shard], 4)
+    out_xy = flipped(after(own_y, *begun)[shard:], 2)
+    near_1, mid_in_1 = to_pair(after(slab_1, *begun)), to_middle(after(slab_1, *begun))
+
+    ready = in_xy, out_xy, far_out_0, near_1, mid_in_1
+    others = flipped(after(jnp.concatenate([own, own_x, own_y], axis=0), *ready), 1)
+    other_xy = flipped(after(jnp.concatenate([in_xy, out_xy], axis=0), *ready), 1)
+    far_in_1, mid_out_1 = to_middle(after(near_1, *ready)), outward(after(mid_in_1, *ready))
+    weights = [own, own_x, own_y, in_xy, out_xy, others, other_xy]
+
+    line_0 = [slab_0, near_0, mid_in_0, mid_out_0, far_in_0, far_out_0]
+    far_0, mid_0, pair_0, home_0 = mlp(line_0, weights)
+    far_out_1 = outward(after(far_in_1, far_0))
+    far_sum_0, mid_from_0 = add(far_0, inward(far_0)), inward(mid_0)
+
+    line_1 = [slab_1, near_1, mid_in_1, mid_out_1, far_in_1, far_out_1]
+    far_1, mid_1, pair_1, home_1 = mlp(line_1, weights)
+
+    far_across_0 = to_middle(far_sum_0)
+    mid_across_0 = to_middle(add(mid_0, mid_from_0))
+    from_pair_0 = to_pair(add(pair_0, far_across_0))
+
+    far_sum_1, mid_from_1 = add(far_1, inward(far_1)), inward(mid_1)
+    far_across_1 = to_middle(far_sum_1)
+    mid_across_1 = to_middle(add(mid_1, mid_from_1))
+    from_pair_1 = to_pair(add(pair_1, far_across_1))
+
     results = []
-    for first in range(0, height, rows):
-        slab = conv_chunk(first, rows, low, features, high, dw_weight.T, dw_bias[None])
-        partials = mlp_chunk(gather_line(slab), w_in_parts, w_out_parts, ln_gain, ln_bias, b_in)
-        projected = scatter_line(*partials) + b_out[None, :, None]
+    for first, parts in (
+        (0, (home_0, mid_across_0, from_pair_0)),
+        (rows, (home_1, mid_across_1, from_pair_1)),
+    ):
+        projected = sum(part.astype(jnp.float32) for part in parts) + b_out[None, :, None]
         block = features[first : first + rows].astype(jnp.float32)
         results.append((block + gamma[None, :, None] * projected).astype(jnp.bfloat16))
     return jnp.concatenate(results, axis=0)
@@ -268,7 +308,7 @@
 
 def plain(features, dw_weight, dw_bias, ln_gain, ln_bias, w_in, b_in, w_out, b_out, gamma):
     rows, slab, width = features.shape
-    low, high = rims(features)
+    low, high = rims(features[:REACH], features[-REACH:])
     image = jnp.concatenate([low, features, high], axis=0).astype(jnp.float32)
     image = jnp.pad(image, ((0, 0), (0, 0), (REACH, REACH)))
     total = jnp.zeros((rows, slab, width), jnp.float32) + dw_bias[None, :, None]

time: 152 us -> 148 us (0.974)
  starting transfers between devices: 56.7 us -> 48.4 us
  waiting for transfers between devices: 58.6 us -> 61.9 us
  other arithmetic: 4.33 us -> 5.98 us
  local copies, waits for them, and re-layouts: 2.88 us -> 1.33 us
    ppermute x14 -> x6, starting transfers between devices: 13.8 us -> 9.1 us  [flipped(): return lax.ppermute(array, 'tile', [(i, i ^ bit) for i in range(8)])]
    ppermute x22, starting transfers between devices: 42.8 us -> 39.3 us  [the longest x8 23.7 us: to_middle(): return lax.ppermute(array, 'chan', [(1, 2), (2, 1)])]
    ppermute x22, waiting for transfers between devices: 50.5 us -> 53.7 us  [the longest x8 16.7 us: to_middle(): return lax.ppermute(array, 'chan', [(1, 2), (2, 1)])]
    concatenate x0 -> x3, other arithmetic: none -> 1.65 us  [the longest x1 1.32 us: local(): own = jnp.concatenate([w_in, w_out.T], axis=0)]
    unnamed x44 -> x20, local copies, waits for them, and re-layouts: 1.69 us -> 0.06 us
    ppermute x14 -> x6, waiting for transfers between devices: 8.1 us -> 8.19 us  [flipped(): return lax.ppermute(array, 'tile', [(i, i ^ bit) for i in range(8)])]
  transfers between devices with their start and end apart: 36 -> 28, of which waited for: 12 -> 14; matrix products, arithmetic and copies ran while one was open for 2% -> 3% of each run, Pallas kernels for 18% -> 19%
where the time goes in v3:
time: 148 us; the launch traced here: 146 us
  waiting for transfers between devices  61.9 us (42%)
  starting transfers between devices  48.4 us (33%)
  Pallas kernels  28.1 us (19%)
  other arithmetic  5.98 us (4%)
    ppermute x8, starting transfers between devices, to_middle(): return lax.ppermute(array, 'chan', [(1, 2), (2, 1)])  23.7 us
    pallas_call x2, Pallas kernels, mlp_chunk(): pl.pallas_call(mlp_kernel, in_specs=[anywhere] * (len(slabs) + len(weight...  19.2 us
    ppermute x8, waiting for transfers between devices, to_middle(): return lax.ppermute(array, 'chan', [(1, 2), (2, 1)])  16.7 us
    ppermute x4, waiting for transfers between devices, to_pair(): return lax.ppermute(array, 'chan', [(0, 1), (1, 0), (2, 3), (3, 2)])  16.1 us
    ppermute x4, waiting for transfers between devices, inward(): return lax.ppermute(array, 'chan', [(0, 1), (3, 2)])  10.4 us
    ppermute x6, starting transfers between devices, flipped(): return lax.ppermute(array, 'tile', [(i, i ^ bit) for i in range(8)])  9.1 us
    pallas_call x2, Pallas kernels, conv_chunk(): pl.pallas_call(functools.partial(conv_kernel, tuple(plan)), grid=(slab //...  8.89 us
    ppermute x4, waiting for transfers between devices, outward(): return lax.ppermute(array, 'chan', [(1, 0), (2, 3)])  8.38 us
  transfers between devices with their start and end apart: 28, of which 14 were waited for; matrix products, arithmetic and copies ran while one was open for 3% of the time, Pallas kernels for 19%

profile of v3, /device:TPU:8, one launch (start us, length us, event | category | flops | bytes accessed | tf_op | source)
XLA Modules:
  0.0 146.1 jit_solution(11806739133102779743)
XLA Ops:
  1.2 1.8 %collective-permute-start = (bf16[3,384,128]{2,1,0:T(8,128)(2,1)S(1)}, bf16[3,384,128]{2,1,0:T(8,128)(2,1)S(1)}, u32[]{:S(2)}, u32[]{:S(2)}) collective-permute-start(bf16[3,384,128]{2,1,0:T(8,128)(2,1)S(1)} %get-tuple-element.41), channel_id=1, source_target_pairs={{0,4},{4,8},{8,12},{12,16},{16,20},{20,24},{24,28},{1,5},{5,9},{9,... | collective-permute-start | bytes 884744 | tf_op jit(solution)/shard_map/ppermute | solution.py:248
  4.2 1.3 pad_maximum_fusion.1.refs_6_
  5.6 2.1 %collective-permute-done.6.refs_1_ = bf16[3,384,128]{2,1,0:T(8,128)(2,1)S(1)} collective-permute-done((bf16[3,384,128]{2,1,0:T(8,128)(2,1)S(1)}, bf16[3,384,128]{2,1,0:T(8,128)(2,1)S(1)}, u32[]{:S(2)}, u32[]{:S(2)}) %collective-permute-start.6) | collective-permute-done | bytes 294944 | tf_op jit(solution)/shard_map/ppermute | solution.py:248
  7.7 5.2 %collective-permute-start.7 = (bf16[384,1536]{1,0:T(8,128)(2,1)S(1)}, bf16[384,1536]{1,0:T(8,128)(2,1)S(1)}, u32[]{:S(2)}, u32[]{:S(2)}) collective-permute-start(bf16[384,1536]{1,0:T(8,128)(2,1)S(1)} %pad_maximum_fusion.1.refs_6_), channel_id=1, source_target_pairs={{0,8},{4,12},{8,0},{12,4},{16,24},{20,28},{24,16},{28,20},{1,9},{5... | collective-permute-start | bytes 3538952 | tf_op jit(solution)/shard_map/ppermute | solution.py:241
  14.0 4.4 %depthwise.2 = bf16[4,128,384]{2,1,0:T(8,128)(2,1)S(1)} custom-call(bf16[8,384,128]{2,1,0:T(8,128)(2,1)S(1)} %copy-done, bf16[3,384,128]{2,1,0:T(8,128)(2,1)S(1)} %collective-permute-done.refs_1_, f32[49,384]{1,0:T(8,128)S(1)} %bitcast.16, f32[1,384]{1,0:T(1,128)S(1)} %broadcast_in_dim.8.refs_3_), custom_call_target="tpu_custom_call" | custom-call | flops 19267584 | bytes 786432 | tf_op jit(solution)/shard_map/depthwise/pallas_call | solution.py:61
  19.0 4.6 %collective-permute-start.2 = (bf16[4,128,384]{2,1,0:T(8,128)(2,1)S(1)}, bf16[4,128,384]{2,1,0:T(8,128)(2,1)S(1)}, u32[]{:S(2)}, u32[]{:S(2)}) collective-permute-start(bf16[4,128,384]{2,1,0:T(8,128)(2,1)S(1)} %depthwise.2), channel_id=1, source_target_pairs={{1,2},{2,1},{5,6},{6,5},{9,10},{10,9},{13,14},{14,13},{17,18},{18,... | collective-permute-start | bytes 1179656 | tf_op jit(solution)/shard_map/ppermute | solution.py:221
  23.6 6.8 %collective-permute-done.1 = bf16[4,128,384]{2,1,0:T(8,128)(2,1)S(1)} collective-permute-done((bf16[4,128,384]{2,1,0:T(8,128)(2,1)S(1)}, bf16[4,128,384]{2,1,0:T(8,128)(2,1)S(1)}, u32[]{:S(2)}, u32[]{:S(2)}) %collective-permute-start.1) | collective-permute-done | bytes 393248 | tf_op jit(solution)/shard_map/ppermute | solution.py:217
  30.5 3.5 %collective-permute-start.4 = (bf16[4,128,384]{2,1,0:T(8,128)(2,1)S(1)}, bf16[4,128,384]{2,1,0:T(8,128)(2,1)S(1)}, u32[]{:S(2)}, u32[]{:S(2)}) collective-permute-start(bf16[4,128,384]{2,1,0:T(8,128)(2,1)S(1)} %collective-permute-done.1), channel_id=1, source_target_pairs={{1,2},{2,1},{5,6},{6,5},{9,10},{10,9},{13,14},{14,13},{17,18},{18,... | collective-permute-start | bytes 1179656 | tf_op jit(solution)/shard_map/ppermute | solution.py:221
  35.3 4.4 %depthwise.3 = bf16[4,128,384]{2,1,0:T(8,128)(2,1)S(1)} custom-call(bf16[8,384,128]{2,1,0:T(8,128)(2,1)S(1)} %copy-done, bf16[3,384,128]{2,1,0:T(8,128)(2,1)S(1)} %collective-permute-done.6.refs_1_, f32[49,384]{1,0:T(8,128)S(1)} %bitcast.17, f32[1,384]{1,0:T(1,128)S(1)} %broadcast_in_dim.8.refs_3_), custom_call_target="tpu_custom_call" | custom-call | flops 19267584 | bytes 786432 | tf_op jit(solution)/shard_map/depthwise/pallas_call | solution.py:61
  39.7 3.7 %collective-permute-done.4 = bf16[4,128,384]{2,1,0:T(8,128)(2,1)S(1)} collective-permute-done((bf16[4,128,384]{2,1,0:T(8,128)(2,1)S(1)}, bf16[4,128,384]{2,1,0:T(8,128)(2,1)S(1)}, u32[]{:S(2)}, u32[]{:S(2)}) %collective-permute-start.4) | collective-permute-done | bytes 393248 | tf_op jit(solution)/shard_map/ppermute | solution.py:221
  44.7 1.6 %collective-permute-start.11 = (bf16[4,128,384]{2,1,0:T(8,128)(2,1)S(1)}, bf16[4,128,384]{2,1,0:T(8,128)(2,1)S(1)}, u32[]{:S(2)}, u32[]{:S(2)}) collective-permute-start(bf16[4,128,384]{2,1,0:T(8,128)(2,1)S(1)} %depthwise.3), channel_id=1, source_target_pairs={{0,1},{1,0},{2,3},{3,2},{4,5},{5,4},{6,7},{7,6},{8,9},{9,8},{10,11... | collective-permute-start | bytes 1179656 | tf_op jit(solution)/shard_map/ppermute | solution.py:217
  46.3 3.2 %collective-permute-start.12 = (bf16[4,128,384]{2,1,0:T(8,128)(2,1)S(1)}, bf16[4,128,384]{2,1,0:T(8,128)(2,1)S(1)}, u32[]{:S(2)}, u32[]{:S(2)}) collective-permute-start(bf16[4,128,384]{2,1,0:T(8,128)(2,1)S(1)} %depthwise.3), channel_id=1, source_target_pairs={{1,2},{2,1},{5,6},{6,5},{9,10},{10,9},{13,14},{14,13},{17,18},{18,... | collective-permute-start | bytes 1179656 | tf_op jit(solution)/shard_map/ppermute | solution.py:221
  49.6 1.6 %collective-permute-start.9 = (bf16[192,1536]{1,0:T(8,128)(2,1)S(1)}, bf16[192,1536]{1,0:T(8,128)(2,1)S(1)}, u32[]{:S(2)}, u32[]{:S(2)}) collective-permute-start(bf16[192,1536]{1,0:T(8,128)(2,1)S(1)} %slice.21), channel_id=1, source_target_pairs={{0,16},{4,20},{8,24},{12,28},{16,0},{20,4},{24,8},{28,12},{1,17},{... | collective-permute-start | bytes 1769480 | tf_op jit(solution)/shard_map/ppermute | solution.py:241
  52.1 2.1 %collective-permute-done.5 = bf16[4,128,384]{2,1,0:T(8,128)(2,1)S(1)} collective-permute-done((bf16[4,128,384]{2,1,0:T(8,128)(2,1)S(1)}, bf16[4,128,384]{2,1,0:T(8,128)(2,1)S(1)}, u32[]{:S(2)}, u32[]{:S(2)}) %collective-permute-start.5) | collective-permute-done | bytes 393248 | tf_op jit(solution)/shard_map/ppermute | solution.py:225
  54.2 6.9 %collective-permute-done.11 = bf16[4,128,384]{2,1,0:T(8,128)(2,1)S(1)} collective-permute-done((bf16[4,128,384]{2,1,0:T(8,128)(2,1)S(1)}, bf16[4,128,384]{2,1,0:T(8,128)(2,1)S(1)}, u32[]{:S(2)}, u32[]{:S(2)}) %collective-permute-start.11) | collective-permute-done | bytes 393248 | tf_op jit(solution)/shard_map/ppermute | solution.py:217
  61.1 3.0 %collective-permute-done.9.refs_9_ = bf16[192,1536]{1,0:T(8,128)(2,1)S(1)} collective-permute-done((bf16[192,1536]{1,0:T(8,128)(2,1)S(1)}, bf16[192,1536]{1,0:T(8,128)(2,1)S(1)}, u32[]{:S(2)}, u32[]{:S(2)}) %collective-permute-start.9) | collective-permute-done | bytes 589856 | tf_op jit(solution)/shard_map/ppermute | solution.py:241
  64.0 1.6 %collective-permute-done.10.refs_10_ = bf16[192,1536]{1,0:T(8,128)(2,1)S(1)} collective-permute-done((bf16[192,1536]{1,0:T(8,128)(2,1)S(1)}, bf16[192,1536]{1,0:T(8,128)(2,1)S(1)}, u32[]{:S(2)}, u32[]{:S(2)}) %collective-permute-start.10) | collective-permute-done | bytes 589856 | tf_op jit(solution)/shard_map/ppermute | solution.py:241
  67.6 2.2 %collective-permute-start.21 = (bf16[4,128,384]{2,1,0:T(8,128)(2,1)S(1)}, bf16[4,128,384]{2,1,0:T(8,128)(2,1)S(1)}, u32[]{:S(2)}, u32[]{:S(2)}) collective-permute-start(bf16[4,128,384]{2,1,0:T(8,128)(2,1)S(1)} %collective-permute-done.11), channel_id=1, source_target_pairs={{1,2},{2,1},{5,6},{6,5},{9,10},{10,9},{13,14},{14,13},{17,18},{18,... | collective-permute-start | bytes 1179656 | tf_op jit(solution)/shard_map/ppermute | solution.py:221
  69.9 3.7 %collective-permute-done.14.refs_12_ = bf16[384,1536]{1,0:T(8,128)(2,1)S(1)} collective-permute-done((bf16[384,1536]{1,0:T(8,128)(2,1)S(1)}, bf16[384,1536]{1,0:T(8,128)(2,1)S(1)}, u32[]{:S(2)}, u32[]{:S(2)}) %collective-permute-start.14) | collective-permute-done | bytes 1179680 | tf_op jit(solution)/shard_map/ppermute | solution.py:241
  73.5 9.6 %mlp.2 = (bf16[4,384,128]{2,1,0:T(8,128)(2,1)S(1)}, bf16[4,384,128]{2,1,0:T(8,128)(2,1)S(1)}, bf16[4,384,128]{2,1,0:T(8,128)(2,1)S(1)}, bf16[4,384,128]{2,1,0:T(8,128)(2,1)S(1)}) custom-call(bf16[512,384]{1,0:T(8,128)(2,1)S(1)} %bitcast.15, bf16[512,384]{1,0:T(8,128)(2,1)S(1)} %bitcast.18, bf16[512,384]{1,0:T(8,128)(2,1)S(1)} %bitcast.19, ...), custom_call_target="tpu_custom_call" | custom-call | flops 4831838208 | bytes 12582912 | tf_op jit(solution)/shard_map/mlp/pallas_call | solution.py:186
  87.1 6.3 %collective-permute-done.22 = bf16[4,128,384]{2,1,0:T(8,128)(2,1)S(1)} collective-permute-done((bf16[4,128,384]{2,1,0:T(8,128)(2,1)S(1)}, bf16[4,128,384]{2,1,0:T(8,128)(2,1)S(1)}, u32[]{:S(2)}, u32[]{:S(2)}) %collective-permute-start.22) | collective-permute-done | bytes 393248 | tf_op jit(solution)/shard_map/ppermute | solution.py:225
  93.4 9.6 %mlp.3 = (bf16[4,384,128]{2,1,0:T(8,128)(2,1)S(1)}, bf16[4,384,128]{2,1,0:T(8,128)(2,1)S(1)}, bf16[4,384,128]{2,1,0:T(8,128)(2,1)S(1)}, bf16[4,384,128]{2,1,0:T(8,128)(2,1)S(1)}) custom-call(bf16[512,384]{1,0:T(8,128)(2,1)S(1)} %bitcast.14, bf16[512,384]{1,0:T(8,128)(2,1)S(1)} %bitcast.20, bf16[512,384]{1,0:T(8,128)(2,1)S(1)} %bitcast.22, ...), custom_call_target="tpu_custom_call" | custom-call | flops 4831838208 | bytes 12582912 | tf_op jit(solution)/shard_map/mlp/pallas_call | solution.py:186
  104.4 2.2 %collective-permute-start.18 = (bf16[4,384,128]{2,1,0:T(8,128)(2,1)S(1)}, bf16[4,384,128]{2,1,0:T(8,128)(2,1)S(1)}, u32[]{:S(2)}, u32[]{:S(2)}) collective-permute-start(bf16[4,384,128]{2,1,0:T(8,128)(2,1)S(1)} %add_convert_fusion.6), channel_id=1, source_target_pairs={{1,2},{2,1},{5,6},{6,5},{9,10},{10,9},{13,14},{14,13},{17,18},{18,... | collective-permute-start | bytes 1179656 | tf_op jit(solution)/shard_map/ppermute | solution.py:221
  106.8 3.6 %collective-permute-start.16 = (bf16[4,384,128]{2,1,0:T(8,128)(2,1)S(1)}, bf16[4,384,128]{2,1,0:T(8,128)(2,1)S(1)}, u32[]{:S(2)}, u32[]{:S(2)}) collective-permute-start(bf16[4,384,128]{2,1,0:T(8,128)(2,1)S(1)} %add_convert_fusion.7), channel_id=1, source_target_pairs={{1,2},{2,1},{5,6},{6,5},{9,10},{10,9},{13,14},{14,13},{17,18},{18,... | collective-permute-start | bytes 1179656 | tf_op jit(solution)/shard_map/ppermute | solution.py:221
  111.7 5.2 %collective-permute-done.25 = bf16[4,384,128]{2,1,0:T(8,128)(2,1)S(1)} collective-permute-done((bf16[4,384,128]{2,1,0:T(8,128)(2,1)S(1)}, bf16[4,384,128]{2,1,0:T(8,128)(2,1)S(1)}, u32[]{:S(2)}, u32[]{:S(2)}) %collective-permute-start.25) | collective-permute-done | bytes 393248 | tf_op jit(solution)/shard_map/ppermute | solution.py:229
  117.0 2.2 %collective-permute-start.26 = (bf16[4,384,128]{2,1,0:T(8,128)(2,1)S(1)}, bf16[4,384,128]{2,1,0:T(8,128)(2,1)S(1)}, u32[]{:S(2)}, u32[]{:S(2)}) collective-permute-start(bf16[4,384,128]{2,1,0:T(8,128)(2,1)S(1)} %add_convert_fusion.2), channel_id=1, source_target_pairs={{1,2},{2,1},{5,6},{6,5},{9,10},{10,9},{13,14},{14,13},{17,18},{18,... | collective-permute-start | bytes 1179656 | tf_op jit(solution)/shard_map/ppermute | solution.py:221
  120.1 5.2 %collective-permute-done.23 = bf16[4,384,128]{2,1,0:T(8,128)(2,1)S(1)} collective-permute-done((bf16[4,384,128]{2,1,0:T(8,128)(2,1)S(1)}, bf16[4,384,128]{2,1,0:T(8,128)(2,1)S(1)}, u32[]{:S(2)}, u32[]{:S(2)}) %collective-permute-start.23) | collective-permute-done | bytes 393248 | tf_op jit(solution)/shard_map/ppermute | solution.py:229
  126.2 2.2 %collective-permute-start.24 = (bf16[4,384,128]{2,1,0:T(8,128)(2,1)}, bf16[4,384,128]{2,1,0:T(8,128)(2,1)S(1)}, u32[]{:S(2)}, u32[]{:S(2)}) collective-permute-start(bf16[4,384,128]{2,1,0:T(8,128)(2,1)} %add_convert_fusion.3), channel_id=1, source_target_pairs={{1,2},{2,1},{5,6},{6,5},{9,10},{10,9},{13,14},{14,13},{17,18},{18,... | collective-permute-start | bytes 1179656 | tf_op jit(solution)/shard_map/ppermute | solution.py:221
  128.4 6.8 %collective-permute-done.26 = bf16[4,384,128]{2,1,0:T(8,128)(2,1)S(1)} collective-permute-done((bf16[4,384,128]{2,1,0:T(8,128)(2,1)S(1)}, bf16[4,384,128]{2,1,0:T(8,128)(2,1)S(1)}, u32[]{:S(2)}, u32[]{:S(2)}) %collective-permute-start.26) | collective-permute-done | bytes 393248 | tf_op jit(solution)/shard_map/ppermute | solution.py:221
  136.1 6.2 %collective-permute-done.24 = bf16[4,384,128]{2,1,0:T(8,128)(2,1)S(1)} collective-permute-done((bf16[4,384,128]{2,1,0:T(8,128)(2,1)}, bf16[4,384,128]{2,1,0:T(8,128)(2,1)S(1)}, u32[]{:S(2)}, u32[]{:S(2)}) %collective-permute-start.24) | collective-permute-done | bytes 393248 | tf_op jit(solution)/shard_map/ppermute | solution.py:221
  142.3 2.4 %collective-permute-done.27 = bf16[4,384,128]{2,1,0:T(8,128)(2,1)S(1)} collective-permute-done((bf16[4,384,128]{2,1,0:T(8,128)(2,1)}, bf16[4,384,128]{2,1,0:T(8,128)(2,1)S(1)}, u32[]{:S(2)}, u32[]{:S(2)}) %collective-permute-start.27) | collective-permute-done | bytes 393248 | tf_op jit(solution)/shard_map/ppermute | solution.py:217
  144.6 1.4 add_convert_fusion.4
  (66 shorter events, 19.1 us)
Async XLA Ops:
  1.2 4.4 %collective-permute-start = (bf16[3,384,128]{2,1,0:T(8,128)(2,1)S(1)}, bf16[3,384,128]{2,1,0:T(8,128)(2,1)S(1)}, u32[]{:S(2)}, u32[]{:S(2)}) collective-permute-start(bf16[3,384,128]{2,1,0:T(8,128)(2,1)S(1)} %get-tuple-element.41), channel_id=1, source_target_pairs={{0,4},{4,8},{8,12},{12,16},{16,20},{20,24},{24,28},{1,5},{5,9},{9,... | collective-permute-start | bytes 884744 | tf_op jit(solution)/shard_map/ppermute | solution.py:248
  2.9 4.7 %collective-permute-start.6 = (bf16[3,384,128]{2,1,0:T(8,128)(2,1)S(1)}, bf16[3,384,128]{2,1,0:T(8,128)(2,1)S(1)}, u32[]{:S(2)}, u32[]{:S(2)}) collective-permute-start(bf16[3,384,128]{2,1,0:T(8,128)(2,1)S(1)} %get-tuple-element.42), channel_id=1, source_target_pairs={{4,0},{8,4},{12,8},{16,12},{20,16},{24,20},{28,24},{5,1},{9,5},{13... | collective-permute-start | bytes 884744 | tf_op jit(solution)/shard_map/ppermute | solution.py:248
  7.7 37.0 %collective-permute-start.7 = (bf16[384,1536]{1,0:T(8,128)(2,1)S(1)}, bf16[384,1536]{1,0:T(8,128)(2,1)S(1)}, u32[]{:S(2)}, u32[]{:S(2)}) collective-permute-start(bf16[384,1536]{1,0:T(8,128)(2,1)S(1)} %pad_maximum_fusion.1.refs_6_), channel_id=1, source_target_pairs={{0,8},{4,12},{8,0},{12,4},{16,24},{20,28},{24,16},{28,20},{1,9},{5... | collective-permute-start | bytes 3538952 | tf_op jit(solution)/shard_map/ppermute | solution.py:241
  12.9 31.8 %collective-permute-start.8 = (bf16[384,1536]{1,0:T(8,128)(2,1)S(1)}, bf16[384,1536]{1,0:T(8,128)(2,1)S(1)}, u32[]{:S(2)}, u32[]{:S(2)}) collective-permute-start(bf16[384,1536]{1,0:T(8,128)(2,1)S(1)} %pad_maximum_fusion.1.refs_6_), channel_id=1, source_target_pairs={{0,16},{4,20},{8,24},{12,28},{16,0},{20,4},{24,8},{28,12},{1,17},{... | collective-permute-start | bytes 3538952 | tf_op jit(solution)/shard_map/ppermute | solution.py:241
  14.0 37.8 %copy-start.2 = (bf16[1536,192]{0,1:T(8,128)(2,1)S(1)}, bf16[1536,192]{0,1:T(8,128)(2,1)}, u32[]{:S(2)}) copy-start(bf16[1536,192]{0,1:T(8,128)(2,1)} %param.17) | copy-start | bytes 1769476
  14.0 37.8 %copy-start.3 = (bf16[192,1536]{1,0:T(8,128)(2,1)S(1)}, bf16[192,1536]{1,0:T(8,128)(2,1)}, u32[]{:S(2)}) copy-start(bf16[192,1536]{1,0:T(8,128)(2,1)} %param.15) | copy-start | bytes 1769476
  18.5 12.0 %collective-permute-start.1 = (bf16[4,128,384]{2,1,0:T(8,128)(2,1)S(1)}, bf16[4,128,384]{2,1,0:T(8,128)(2,1)S(1)}, u32[]{:S(2)}, u32[]{:S(2)}) collective-permute-start(bf16[4,128,384]{2,1,0:T(8,128)(2,1)S(1)} %depthwise.2), channel_id=1, source_target_pairs={{0,1},{1,0},{2,3},{3,2},{4,5},{5,4},{6,7},{7,6},{8,9},{9,8},{10,11... | collective-permute-start | bytes 1179656 | tf_op jit(solution)/shard_map/ppermute | solution.py:217
  19.0 14.9 %collective-permute-start.2 = (bf16[4,128,384]{2,1,0:T(8,128)(2,1)S(1)}, bf16[4,128,384]{2,1,0:T(8,128)(2,1)S(1)}, u32[]{:S(2)}, u32[]{:S(2)}) collective-permute-start(bf16[4,128,384]{2,1,0:T(8,128)(2,1)S(1)} %depthwise.2), channel_id=1, source_target_pairs={{1,2},{2,1},{5,6},{6,5},{9,10},{10,9},{13,14},{14,13},{17,18},{18,... | collective-permute-start | bytes 1179656 | tf_op jit(solution)/shard_map/ppermute | solution.py:221
  30.5 12.9 %collective-permute-start.4 = (bf16[4,128,384]{2,1,0:T(8,128)(2,1)S(1)}, bf16[4,128,384]{2,1,0:T(8,128)(2,1)S(1)}, u32[]{:S(2)}, u32[]{:S(2)}) collective-permute-start(bf16[4,128,384]{2,1,0:T(8,128)(2,1)S(1)} %collective-permute-done.1), channel_id=1, source_target_pairs={{1,2},{2,1},{5,6},{6,5},{9,10},{10,9},{13,14},{14,13},{17,18},{18,... | collective-permute-start | bytes 1179656 | tf_op jit(solution)/shard_map/ppermute | solution.py:221
  33.9 10.8 %collective-permute-start.3 = (bf16[4,128,384]{2,1,0:T(8,128)(2,1)S(1)}, bf16[4,128,384]{2,1,0:T(8,128)(2,1)S(1)}, u32[]{:S(2)}, u32[]{:S(2)}) collective-permute-start(bf16[4,128,384]{2,1,0:T(8,128)(2,1)S(1)} %collective-permute-done.2), channel_id=1, source_target_pairs={{1,0},{2,3},{5,4},{6,7},{9,8},{10,11},{13,12},{14,15},{17,16},{18,... | collective-permute-start | bytes 1179656 | tf_op jit(solution)/shard_map/ppermute | solution.py:225
  43.4 10.8 %collective-permute-start.5 = (bf16[4,128,384]{2,1,0:T(8,128)(2,1)S(1)}, bf16[4,128,384]{2,1,0:T(8,128)(2,1)S(1)}, u32[]{:S(2)}, u32[]{:S(2)}) collective-permute-start(bf16[4,128,384]{2,1,0:T(8,128)(2,1)S(1)} %collective-permute-done.4), channel_id=1, source_target_pairs={{1,0},{2,3},{5,4},{6,7},{9,8},{10,11},{13,12},{14,15},{17,16},{18,... | collective-permute-start | bytes 1179656 | tf_op jit(solution)/shard_map/ppermute | solution.py:225
  44.7 16.4 %collective-permute-start.11 = (bf16[4,128,384]{2,1,0:T(8,128)(2,1)S(1)}, bf16[4,128,384]{2,1,0:T(8,128)(2,1)S(1)}, u32[]{:S(2)}, u32[]{:S(2)}) collective-permute-start(bf16[4,128,384]{2,1,0:T(8,128)(2,1)S(1)} %depthwise.3), channel_id=1, source_target_pairs={{0,1},{1,0},{2,3},{3,2},{4,5},{5,4},{6,7},{7,6},{8,9},{9,8},{10,11... | collective-permute-start | bytes 1179656 | tf_op jit(solution)/shard_map/ppermute | solution.py:217
  46.3 14.8 %collective-permute-start.12 = (bf16[4,128,384]{2,1,0:T(8,128)(2,1)S(1)}, bf16[4,128,384]{2,1,0:T(8,128)(2,1)S(1)}, u32[]{:S(2)}, u32[]{:S(2)}) collective-permute-start(bf16[4,128,384]{2,1,0:T(8,128)(2,1)S(1)} %depthwise.3), channel_id=1, source_target_pairs={{1,2},{2,1},{5,6},{6,5},{9,10},{10,9},{13,14},{14,13},{17,18},{18,... | collective-permute-start | bytes 1179656 | tf_op jit(solution)/shard_map/ppermute | solution.py:221
  49.6 14.5 %collective-permute-start.9 = (bf16[192,1536]{1,0:T(8,128)(2,1)S(1)}, bf16[192,1536]{1,0:T(8,128)(2,1)S(1)}, u32[]{:S(2)}, u32[]{:S(2)}) collective-permute-start(bf16[192,1536]{1,0:T(8,128)(2,1)S(1)} %slice.21), channel_id=1, source_target_pairs={{0,16},{4,20},{8,24},{12,28},{16,0},{20,4},{24,8},{28,12},{1,17},{... | collective-permute-start | bytes 1769480 | tf_op jit(solution)/shard_map/ppermute | solution.py:241
  51.2 14.4 %collective-permute-start.10 = (bf16[192,1536]{1,0:T(8,128)(2,1)S(1)}, bf16[192,1536]{1,0:T(8,128)(2,1)S(1)}, u32[]{:S(2)}, u32[]{:S(2)}) collective-permute-start(bf16[192,1536]{1,0:T(8,128)(2,1)S(1)} %slice.22), channel_id=1, source_target_pairs={{0,8},{4,12},{8,0},{12,4},{16,24},{20,28},{24,16},{28,20},{1,9},{5... | collective-permute-start | bytes 1769480 | tf_op jit(solution)/shard_map/ppermute | solution.py:241
  65.6 7.9 %collective-permute-start.13 = (bf16[1152,1536]{1,0:T(8,128)(2,1)S(1)}, bf16[1152,1536]{1,0:T(8,128)(2,1)S(1)}, u32[]{:S(2)}, u32[]{:S(2)}) collective-permute-start(bf16[1152,1536]{1,0:T(8,128)(2,1)S(1)} %pad_maximum_fusion), channel_id=1, source_target_pairs={{0,4},{4,0},{8,12},{12,8},{16,20},{20,16},{24,28},{28,24},{1,5},{5... | collective-permute-start | bytes 10616840 | tf_op jit(solution)/shard_map/ppermute | solution.py:241
  65.7 7.8 %collective-permute-start.14 = (bf16[384,1536]{1,0:T(8,128)(2,1)S(1)}, bf16[384,1536]{1,0:T(8,128)(2,1)S(1)}, u32[]{:S(2)}, u32[]{:S(2)}) collective-permute-start(bf16[384,1536]{1,0:T(8,128)(2,1)S(1)} %pad_maximum_fusion.2), channel_id=1, source_target_pairs={{0,4},{4,0},{8,12},{12,8},{16,20},{20,16},{24,28},{28,24},{1,5},{5... | collective-permute-start | bytes 3538952 | tf_op jit(solution)/shard_map/ppermute | solution.py:241
  66.3 20.8 %collective-permute-start.20 = (bf16[4,128,384]{2,1,0:T(8,128)(2,1)S(1)}, bf16[4,128,384]{2,1,0:T(8,128)(2,1)S(1)}, u32[]{:S(2)}, u32[]{:S(2)}) collective-permute-start(bf16[4,128,384]{2,1,0:T(8,128)(2,1)S(1)} %collective-permute-done.12), channel_id=1, source_target_pairs={{1,0},{2,3},{5,4},{6,7},{9,8},{10,11},{13,12},{14,15},{17,16},{18,... | collective-permute-start | bytes 1179656 | tf_op jit(solution)/shard_map/ppermute | solution.py:225
  67.6 15.5 %collective-permute-start.21 = (bf16[4,128,384]{2,1,0:T(8,128)(2,1)S(1)}, bf16[4,128,384]{2,1,0:T(8,128)(2,1)S(1)}, u32[]{:S(2)}, u32[]{:S(2)}) collective-permute-start(bf16[4,128,384]{2,1,0:T(8,128)(2,1)S(1)} %collective-permute-done.11), channel_id=1, source_target_pairs={{1,2},{2,1},{5,6},{6,5},{9,10},{10,9},{13,14},{14,13},{17,18},{18,... | collective-permute-start | bytes 1179656 | tf_op jit(solution)/shard_map/ppermute | solution.py:221
  83.2 10.2 %collective-permute-start.22 = (bf16[4,128,384]{2,1,0:T(8,128)(2,1)S(1)}, bf16[4,128,384]{2,1,0:T(8,128)(2,1)S(1)}, u32[]{:S(2)}, u32[]{:S(2)}) collective-permute-start(bf16[4,128,384]{2,1,0:T(8,128)(2,1)S(1)} %collective-permute-done.21), channel_id=1, source_target_pairs={{1,0},{2,3},{5,4},{6,7},{9,8},{10,11},{13,12},{14,15},{17,16},{18,... | collective-permute-start | bytes 1179656 | tf_op jit(solution)/shard_map/ppermute | solution.py:225
  84.5 19.8 %collective-permute-start.17 = (bf16[4,384,128]{2,1,0:T(8,128)(2,1)S(1)}, bf16[4,384,128]{2,1,0:T(8,128)(2,1)S(1)}, u32[]{:S(2)}, u32[]{:S(2)}) collective-permute-start(bf16[4,384,128]{2,1,0:T(8,128)(2,1)S(1)} %get-tuple-element.31), channel_id=1, source_target_pairs={{0,1},{3,2},{4,5},{7,6},{8,9},{11,10},{12,13},{15,14},{16,17},{19,... | collective-permute-start | bytes 1179656 | tf_op jit(solution)/shard_map/ppermute | solution.py:229
  85.8 20.9 %collective-permute-start.15 = (bf16[4,384,128]{2,1,0:T(8,128)(2,1)S(1)}, bf16[4,384,128]{2,1,0:T(8,128)(2,1)S(1)}, u32[]{:S(2)}, u32[]{:S(2)}) collective-permute-start(bf16[4,384,128]{2,1,0:T(8,128)(2,1)S(1)} %get-tuple-element.29), channel_id=1, source_target_pairs={{0,1},{3,2},{4,5},{7,6},{8,9},{11,10},{12,13},{15,14},{16,17},{19,... | collective-permute-start | bytes 1179656 | tf_op jit(solution)/shard_map/ppermute | solution.py:229
  103.0 13.9 %collective-permute-start.25 = (bf16[4,384,128]{2,1,0:T(8,128)(2,1)S(1)}, bf16[4,384,128]{2,1,0:T(8,128)(2,1)S(1)}, u32[]{:S(2)}, u32[]{:S(2)}) collective-permute-start(bf16[4,384,128]{2,1,0:T(8,128)(2,1)S(1)} %get-tuple-element.38), channel_id=1, source_target_pairs={{0,1},{3,2},{4,5},{7,6},{8,9},{11,10},{12,13},{15,14},{16,17},{19,... | collective-permute-start | bytes 1179656 | tf_op jit(solution)/shard_map/ppermute | solution.py:229
  104.4 14.8 %collective-permute-start.18 = (bf16[4,384,128]{2,1,0:T(8,128)(2,1)S(1)}, bf16[4,384,128]{2,1,0:T(8,128)(2,1)S(1)}, u32[]{:S(2)}, u32[]{:S(2)}) collective-permute-start(bf16[4,384,128]{2,1,0:T(8,128)(2,1)S(1)} %add_convert_fusion.6), channel_id=1, source_target_pairs={{1,2},{2,1},{5,6},{6,5},{9,10},{10,9},{13,14},{14,13},{17,18},{18,... | collective-permute-start | bytes 1179656 | tf_op jit(solution)/shard_map/ppermute | solution.py:221
  106.8 29.3 %collective-permute-start.16 = (bf16[4,384,128]{2,1,0:T(8,128)(2,1)S(1)}, bf16[4,384,128]{2,1,0:T(8,128)(2,1)S(1)}, u32[]{:S(2)}, u32[]{:S(2)}) collective-permute-start(bf16[4,384,128]{2,1,0:T(8,128)(2,1)S(1)} %add_convert_fusion.7), channel_id=1, source_target_pairs={{1,2},{2,1},{5,6},{6,5},{9,10},{10,9},{13,14},{14,13},{17,18},{18,... | collective-permute-start | bytes 1179656 | tf_op jit(solution)/shard_map/ppermute | solution.py:221
  110.4 34.2 %copy-start.7 = (f32[384]{0:T(512)S(1)}, f32[384]{0:T(512)}, u32[]{:S(2)}) copy-start(f32[384]{0:T(512)} %param.18) | copy-start | bytes 4612
  110.4 34.2 %copy-start.8 = (f32[384]{0:T(512)S(1)}, f32[384]{0:T(512)}, u32[]{:S(2)}) copy-start(f32[384]{0:T(512)} %param.19) | copy-start | bytes 4612
  110.4 14.9 %collective-permute-start.23 = (bf16[4,384,128]{2,1,0:T(8,128)(2,1)S(1)}, bf16[4,384,128]{2,1,0:T(8,128)(2,1)S(1)}, u32[]{:S(2)}, u32[]{:S(2)}) collective-permute-start(bf16[4,384,128]{2,1,0:T(8,128)(2,1)S(1)} %get-tuple-element.36), channel_id=1, source_target_pairs={{0,1},{3,2},{4,5},{7,6},{8,9},{11,10},{12,13},{15,14},{16,17},{19,... | collective-permute-start | bytes 1179656 | tf_op jit(solution)/shard_map/ppermute | solution.py:229
  117.0 18.2 %collective-permute-start.26 = (bf16[4,384,128]{2,1,0:T(8,128)(2,1)S(1)}, bf16[4,384,128]{2,1,0:T(8,128)(2,1)S(1)}, u32[]{:S(2)}, u32[]{:S(2)}) collective-permute-start(bf16[4,384,128]{2,1,0:T(8,128)(2,1)S(1)} %add_convert_fusion.2), channel_id=1, source_target_pairs={{1,2},{2,1},{5,6},{6,5},{9,10},{10,9},{13,14},{14,13},{17,18},{18,... | collective-permute-start | bytes 1179656 | tf_op jit(solution)/shard_map/ppermute | solution.py:221
  120.1 16.0 %collective-permute-start.19 = (bf16[4,384,128]{2,1,0:T(8,128)(2,1)}, bf16[4,384,128]{2,1,0:T(8,128)(2,1)S(1)}, u32[]{:S(2)}, u32[]{:S(2)}) collective-permute-start(bf16[4,384,128]{2,1,0:T(8,128)(2,1)} %add_convert_fusion.5), channel_id=1, source_target_pairs={{0,1},{1,0},{2,3},{3,2},{4,5},{5,4},{6,7},{7,6},{8,9},{9,8},{10,11... | collective-permute-start | bytes 1179656 | tf_op jit(solution)/shard_map/ppermute | solution.py:217
  126.2 16.1 %collective-permute-start.24 = (bf16[4,384,128]{2,1,0:T(8,128)(2,1)}, bf16[4,384,128]{2,1,0:T(8,128)(2,1)S(1)}, u32[]{:S(2)}, u32[]{:S(2)}) collective-permute-start(bf16[4,384,128]{2,1,0:T(8,128)(2,1)} %add_convert_fusion.3), channel_id=1, source_target_pairs={{1,2},{2,1},{5,6},{6,5},{9,10},{10,9},{13,14},{14,13},{17,18},{18,... | collective-permute-start | bytes 1179656 | tf_op jit(solution)/shard_map/ppermute | solution.py:221
  136.1 8.6 %collective-permute-start.27 = (bf16[4,384,128]{2,1,0:T(8,128)(2,1)}, bf16[4,384,128]{2,1,0:T(8,128)(2,1)S(1)}, u32[]{:S(2)}, u32[]{:S(2)}) collective-permute-start(bf16[4,384,128]{2,1,0:T(8,128)(2,1)} %add_convert_fusion.1), channel_id=1, source_target_pairs={{0,1},{1,0},{2,3},{3,2},{4,5},{5,4},{6,7},{7,6},{8,9},{9,8},{10,11... | collective-permute-start | bytes 1179656 | tf_op jit(solution)/shard_map/ppermute | solution.py:217
  (6 other events, 84.5 us)

commit v4 on v3

--- a/solution.py
+++ b/solution.py
@@ -140,7 +140,7 @@
     slab_copy(mid_inner, mid, 2).wait()
     slab_copy(far_inner, far, 3).wait()
 
-    step = 64
+    step = 256
     gain, shift = gain_ref[...], shift_ref[...]
 
     def normalize(i, carry):
@@ -287,11 +287,11 @@
     far_1, mid_1, pair_1, home_1 = mlp(line_1, weights)
 
     far_across_0 = to_middle(far_sum_0)
-    mid_across_0 = to_middle(add(mid_0, mid_from_0))
     from_pair_0 = to_pair(add(pair_0, far_across_0))
 
     far_sum_1, mid_from_1 = add(far_1, inward(far_1)), inward(mid_1)
     far_across_1 = to_middle(far_sum_1)
+    mid_across_0 = to_middle(after(add(mid_0, mid_from_0), far_sum_1))
     mid_across_1 = to_middle(add(mid_1, mid_from_1))
     from_pair_1 = to_pair(add(pair_1, far_across_1))
 

time: 148 us -> 145 us (0.980)
  Pallas kernels: 28.1 us -> 26.4 us
    pallas_call x2, Pallas kernels: 19.2 us -> 17.6 us  [mlp_chunk(): pl.pallas_call(mlp_kernel, in_specs=[anywhere] * (len(slabs) + len(weight...]
  transfers between devices with their start and end apart: 28 -> 28, of which waited for: 14 -> 15; matrix products, arithmetic and copies ran while one was open for 3% -> 3% of each run, Pallas kernels for 19% -> 18%
where the time goes in v4:
time: 145 us; the launch traced here: 144 us
  waiting for transfers between devices  61.6 us (42%)
  starting transfers between devices  48.4 us (33%)
  Pallas kernels  26.4 us (18%)
  other arithmetic  5.98 us (4%)
    ppermute x8, starting transfers between devices, to_middle(): return lax.ppermute(array, 'chan', [(1, 2), (2, 1)])  23.7 us
    pallas_call x2, Pallas kernels, mlp_chunk(): pl.pallas_call(mlp_kernel, in_specs=[anywhere] * (len(slabs) + len(weight...  17.6 us
    ppermute x8, waiting for transfers between devices, to_middle(): return lax.ppermute(array, 'chan', [(1, 2), (2, 1)])  16.9 us
    ppermute x4, waiting for transfers between devices, to_pair(): return lax.ppermute(array, 'chan', [(0, 1), (1, 0), (2, 3), (3, 2)])  15.6 us
    ppermute x4, waiting for transfers between devices, inward(): return lax.ppermute(array, 'chan', [(0, 1), (3, 2)])  10.4 us
    ppermute x6, starting transfers between devices, flipped(): return lax.ppermute(array, 'tile', [(i, i ^ bit) for i in range(8)])  9.1 us
    pallas_call x2, Pallas kernels, conv_chunk(): pl.pallas_call(functools.partial(conv_kernel, tuple(plan)), grid=(slab //...  8.89 us
    ppermute x4, waiting for transfers between devices, outward(): return lax.ppermute(array, 'chan', [(1, 0), (2, 3)])  8.38 us
  transfers between devices with their start and end apart: 28, of which 15 were waited for; matrix products, arithmetic and copies ran while one was open for 3% of the time, Pallas kernels for 18%

profile of v4, /device:TPU:8, one launch (start us, length us, event | category | flops | bytes accessed | tf_op | source)
XLA Modules:
  0.0 144.2 jit_solution(248056795164187215)
XLA Ops:
  1.2 1.8 %collective-permute-start = (bf16[3,384,128]{2,1,0:T(8,128)(2,1)S(1)}, bf16[3,384,128]{2,1,0:T(8,128)(2,1)S(1)}, u32[]{:S(2)}, u32[]{:S(2)}) collective-permute-start(bf16[3,384,128]{2,1,0:T(8,128)(2,1)S(1)} %get-tuple-element.43), channel_id=1, source_target_pairs={{0,4},{4,8},{8,12},{12,16},{16,20},{20,24},{24,28},{1,5},{5,9},{9,... | collective-permute-start | bytes 884744 | tf_op jit(solution)/shard_map/ppermute | solution.py:248
  5.6 2.1 %collective-permute-done.6.refs_1_ = bf16[3,384,128]{2,1,0:T(8,128)(2,1)S(1)} collective-permute-done((bf16[3,384,128]{2,1,0:T(8,128)(2,1)S(1)}, bf16[3,384,128]{2,1,0:T(8,128)(2,1)S(1)}, u32[]{:S(2)}, u32[]{:S(2)}) %collective-permute-start.6) | collective-permute-done | bytes 294944 | tf_op jit(solution)/shard_map/ppermute | solution.py:248
  7.7 5.2 %collective-permute-start.7 = (bf16[384,1536]{1,0:T(8,128)(2,1)S(1)}, bf16[384,1536]{1,0:T(8,128)(2,1)S(1)}, u32[]{:S(2)}, u32[]{:S(2)}) collective-permute-start(bf16[384,1536]{1,0:T(8,128)(2,1)S(1)} %pad_maximum_fusion.1.refs_6_), channel_id=1, source_target_pairs={{0,8},{4,12},{8,0},{12,4},{16,24},{20,28},{24,16},{28,20},{1,9},{5... | collective-permute-start | bytes 3538952 | tf_op jit(solution)/shard_map/ppermute | solution.py:241
  14.0 4.4 %depthwise.2 = bf16[4,128,384]{2,1,0:T(8,128)(2,1)S(1)} custom-call(bf16[8,384,128]{2,1,0:T(8,128)(2,1)S(1)} %copy-done, bf16[3,384,128]{2,1,0:T(8,128)(2,1)S(1)} %collective-permute-done.refs_1_, f32[49,384]{1,0:T(8,128)S(1)} %bitcast.16, f32[1,384]{1,0:T(1,128)S(1)} %broadcast_in_dim.8.refs_3_), custom_call_target="tpu_custom_call" | custom-call | flops 19267584 | bytes 786432 | tf_op jit(solution)/shard_map/depthwise/pallas_call | solution.py:61
  19.0 4.6 %collective-permute-start.2 = (bf16[4,128,384]{2,1,0:T(8,128)(2,1)S(1)}, bf16[4,128,384]{2,1,0:T(8,128)(2,1)S(1)}, u32[]{:S(2)}, u32[]{:S(2)}) collective-permute-start(bf16[4,128,384]{2,1,0:T(8,128)(2,1)S(1)} %depthwise.2), channel_id=1, source_target_pairs={{1,2},{2,1},{5,6},{6,5},{9,10},{10,9},{13,14},{14,13},{17,18},{18,... | collective-permute-start | bytes 1179656 | tf_op jit(solution)/shard_map/ppermute | solution.py:221
  23.6 6.8 %collective-permute-done.1 = bf16[4,128,384]{2,1,0:T(8,128)(2,1)S(1)} collective-permute-done((bf16[4,128,384]{2,1,0:T(8,128)(2,1)S(1)}, bf16[4,128,384]{2,1,0:T(8,128)(2,1)S(1)}, u32[]{:S(2)}, u32[]{:S(2)}) %collective-permute-start.1) | collective-permute-done | bytes 393248 | tf_op jit(solution)/shard_map/ppermute | solution.py:217
  30.5 3.5 %collective-permute-start.4 = (bf16[4,128,384]{2,1,0:T(8,128)(2,1)S(1)}, bf16[4,128,384]{2,1,0:T(8,128)(2,1)S(1)}, u32[]{:S(2)}, u32[]{:S(2)}) collective-permute-start(bf16[4,128,384]{2,1,0:T(8,128)(2,1)S(1)} %collective-permute-done.1), channel_id=1, source_target_pairs={{1,2},{2,1},{5,6},{6,5},{9,10},{10,9},{13,14},{14,13},{17,18},{18,... | collective-permute-start | bytes 1179656 | tf_op jit(solution)/shard_map/ppermute | solution.py:221
  35.3 4.4 %depthwise.3 = bf16[4,128,384]{2,1,0:T(8,128)(2,1)S(1)} custom-call(bf16[8,384,128]{2,1,0:T(8,128)(2,1)S(1)} %copy-done, bf16[3,384,128]{2,1,0:T(8,128)(2,1)S(1)} %collective-permute-done.6.refs_1_, f32[49,384]{1,0:T(8,128)S(1)} %bitcast.17, f32[1,384]{1,0:T(1,128)S(1)} %broadcast_in_dim.8.refs_3_), custom_call_target="tpu_custom_call" | custom-call | flops 19267584 | bytes 786432 | tf_op jit(solution)/shard_map/depthwise/pallas_call | solution.py:61
  39.7 3.7 %collective-permute-done.4 = bf16[4,128,384]{2,1,0:T(8,128)(2,1)S(1)} collective-permute-done((bf16[4,128,384]{2,1,0:T(8,128)(2,1)S(1)}, bf16[4,128,384]{2,1,0:T(8,128)(2,1)S(1)}, u32[]{:S(2)}, u32[]{:S(2)}) %collective-permute-start.4) | collective-permute-done | bytes 393248 | tf_op jit(solution)/shard_map/ppermute | solution.py:221
  44.7 1.6 %collective-permute-start.11 = (bf16[4,128,384]{2,1,0:T(8,128)(2,1)S(1)}, bf16[4,128,384]{2,1,0:T(8,128)(2,1)S(1)}, u32[]{:S(2)}, u32[]{:S(2)}) collective-permute-start(bf16[4,128,384]{2,1,0:T(8,128)(2,1)S(1)} %depthwise.3), channel_id=1, source_target_pairs={{0,1},{1,0},{2,3},{3,2},{4,5},{5,4},{6,7},{7,6},{8,9},{9,8},{10,11... | collective-permute-start | bytes 1179656 | tf_op jit(solution)/shard_map/ppermute | solution.py:217
  46.3 3.2 %collective-permute-start.12 = (bf16[4,128,384]{2,1,0:T(8,128)(2,1)S(1)}, bf16[4,128,384]{2,1,0:T(8,128)(2,1)S(1)}, u32[]{:S(2)}, u32[]{:S(2)}) collective-permute-start(bf16[4,128,384]{2,1,0:T(8,128)(2,1)S(1)} %depthwise.3), channel_id=1, source_target_pairs={{1,2},{2,1},{5,6},{6,5},{9,10},{10,9},{13,14},{14,13},{17,18},{18,... | collective-permute-start | bytes 1179656 | tf_op jit(solution)/shard_map/ppermute | solution.py:221
  49.6 1.6 %collective-permute-start.9 = (bf16[192,1536]{1,0:T(8,128)(2,1)S(1)}, bf16[192,1536]{1,0:T(8,128)(2,1)S(1)}, u32[]{:S(2)}, u32[]{:S(2)}) collective-permute-start(bf16[192,1536]{1,0:T(8,128)(2,1)S(1)} %slice.21), channel_id=1, source_target_pairs={{0,16},{4,20},{8,24},{12,28},{16,0},{20,4},{24,8},{28,12},{1,17},{... | collective-permute-start | bytes 1769480 | tf_op jit(solution)/shard_map/ppermute | solution.py:241
  52.1 2.1 %collective-permute-done.5 = bf16[4,128,384]{2,1,0:T(8,128)(2,1)S(1)} collective-permute-done((bf16[4,128,384]{2,1,0:T(8,128)(2,1)S(1)}, bf16[4,128,384]{2,1,0:T(8,128)(2,1)S(1)}, u32[]{:S(2)}, u32[]{:S(2)}) %collective-permute-start.5) | collective-permute-done | bytes 393248 | tf_op jit(solution)/shard_map/ppermute | solution.py:225
  54.2 6.9 %collective-permute-done.11 = bf16[4,128,384]{2,1,0:T(8,128)(2,1)S(1)} collective-permute-done((bf16[4,128,384]{2,1,0:T(8,128)(2,1)S(1)}, bf16[4,128,384]{2,1,0:T(8,128)(2,1)S(1)}, u32[]{:S(2)}, u32[]{:S(2)}) %collective-permute-start.11) | collective-permute-done | bytes 393248 | tf_op jit(solution)/shard_map/ppermute | solution.py:217
  61.1 3.0 %collective-permute-done.9.refs_9_ = bf16[192,1536]{1,0:T(8,128)(2,1)S(1)} collective-permute-done((bf16[192,1536]{1,0:T(8,128)(2,1)S(1)}, bf16[192,1536]{1,0:T(8,128)(2,1)S(1)}, u32[]{:S(2)}, u32[]{:S(2)}) %collective-permute-start.9) | collective-permute-done | bytes 589856 | tf_op jit(solution)/shard_map/ppermute | solution.py:241
  64.0 1.6 %collective-permute-done.10.refs_10_ = bf16[192,1536]{1,0:T(8,128)(2,1)S(1)} collective-permute-done((bf16[192,1536]{1,0:T(8,128)(2,1)S(1)}, bf16[192,1536]{1,0:T(8,128)(2,1)S(1)}, u32[]{:S(2)}, u32[]{:S(2)}) %collective-permute-start.10) | collective-permute-done | bytes 589856 | tf_op jit(solution)/shard_map/ppermute | solution.py:241
  67.6 2.2 %collective-permute-start.17 = (bf16[4,128,384]{2,1,0:T(8,128)(2,1)S(1)}, bf16[4,128,384]{2,1,0:T(8,128)(2,1)S(1)}, u32[]{:S(2)}, u32[]{:S(2)}) collective-permute-start(bf16[4,128,384]{2,1,0:T(8,128)(2,1)S(1)} %collective-permute-done.11), channel_id=1, source_target_pairs={{1,2},{2,1},{5,6},{6,5},{9,10},{10,9},{13,14},{14,13},{17,18},{18,... | collective-permute-start | bytes 1179656 | tf_op jit(solution)/shard_map/ppermute | solution.py:221
  69.9 3.7 %collective-permute-done.14.refs_12_ = bf16[384,1536]{1,0:T(8,128)(2,1)S(1)} collective-permute-done((bf16[384,1536]{1,0:T(8,128)(2,1)S(1)}, bf16[384,1536]{1,0:T(8,128)(2,1)S(1)}, u32[]{:S(2)}, u32[]{:S(2)}) %collective-permute-start.14) | collective-permute-done | bytes 1179680 | tf_op jit(solution)/shard_map/ppermute | solution.py:241
  73.5 8.7 %mlp.2 = (bf16[4,384,128]{2,1,0:T(8,128)(2,1)S(1)}, bf16[4,384,128]{2,1,0:T(8,128)(2,1)S(1)}, bf16[4,384,128]{2,1,0:T(8,128)(2,1)S(1)}, bf16[4,384,128]{2,1,0:T(8,128)(2,1)S(1)}) custom-call(bf16[512,384]{1,0:T(8,128)(2,1)S(1)} %bitcast.15, bf16[512,384]{1,0:T(8,128)(2,1)S(1)} %bitcast.18, bf16[512,384]{1,0:T(8,128)(2,1)S(1)} %bitcast.19, ...), custom_call_target="tpu_custom_call" | custom-call | flops 4831838208 | bytes 12582912 | tf_op jit(solution)/shard_map/mlp/pallas_call | solution.py:186
  86.2 6.3 %collective-permute-done.18 = bf16[4,128,384]{2,1,0:T(8,128)(2,1)S(1)} collective-permute-done((bf16[4,128,384]{2,1,0:T(8,128)(2,1)S(1)}, bf16[4,128,384]{2,1,0:T(8,128)(2,1)S(1)}, u32[]{:S(2)}, u32[]{:S(2)}) %collective-permute-start.18) | collective-permute-done | bytes 393248 | tf_op jit(solution)/shard_map/ppermute | solution.py:225
  92.5 8.9 %mlp.3 = (bf16[4,384,128]{2,1,0:T(8,128)(2,1)S(1)}, bf16[4,384,128]{2,1,0:T(8,128)(2,1)S(1)}, bf16[4,384,128]{2,1,0:T(8,128)(2,1)S(1)}, bf16[4,384,128]{2,1,0:T(8,128)(2,1)S(1)}) custom-call(bf16[512,384]{1,0:T(8,128)(2,1)S(1)} %bitcast.14, bf16[512,384]{1,0:T(8,128)(2,1)S(1)} %bitcast.20, bf16[512,384]{1,0:T(8,128)(2,1)S(1)} %bitcast.22, ...), custom_call_target="tpu_custom_call" | custom-call | flops 4831838208 | bytes 12582912 | tf_op jit(solution)/shard_map/mlp/pallas_call | solution.py:186
  102.8 2.2 %collective-permute-start.22 = (bf16[4,384,128]{2,1,0:T(8,128)(2,1)S(1)}, bf16[4,384,128]{2,1,0:T(8,128)(2,1)S(1)}, u32[]{:S(2)}, u32[]{:S(2)}) collective-permute-start(bf16[4,384,128]{2,1,0:T(8,128)(2,1)S(1)} %add_convert_fusion.5), channel_id=1, source_target_pairs={{1,2},{2,1},{5,6},{6,5},{9,10},{10,9},{13,14},{14,13},{17,18},{18,... | collective-permute-start | bytes 1179656 | tf_op jit(solution)/shard_map/ppermute | solution.py:221
  106.4 8.8 %collective-permute-done.19 = bf16[4,384,128]{2,1,0:T(8,128)(2,1)S(1)} collective-permute-done((bf16[4,384,128]{2,1,0:T(8,128)(2,1)S(1)}, bf16[4,384,128]{2,1,0:T(8,128)(2,1)S(1)}, u32[]{:S(2)}, u32[]{:S(2)}) %collective-permute-start.19) | collective-permute-done | bytes 393248 | tf_op jit(solution)/shard_map/ppermute | solution.py:229
  115.4 2.2 %collective-permute-start.26 = (bf16[4,384,128]{2,1,0:T(8,128)(2,1)S(1)}, bf16[4,384,128]{2,1,0:T(8,128)(2,1)S(1)}, u32[]{:S(2)}, u32[]{:S(2)}) collective-permute-start(bf16[4,384,128]{2,1,0:T(8,128)(2,1)S(1)} %add_convert_fusion.6), channel_id=1, source_target_pairs={{1,2},{2,1},{5,6},{6,5},{9,10},{10,9},{13,14},{14,13},{17,18},{18,... | collective-permute-start | bytes 1179656 | tf_op jit(solution)/shard_map/ppermute | solution.py:221
  118.4 3.6 %collective-permute-start.20 = (bf16[4,384,128]{2,1,0:T(8,128)(2,1)S(1)}, bf16[4,384,128]{2,1,0:T(8,128)(2,1)S(1)}, u32[]{:S(2)}, u32[]{:S(2)}) collective-permute-start(bf16[4,384,128]{2,1,0:T(8,128)(2,1)S(1)} %add_convert_fusion.7), channel_id=1, source_target_pairs={{1,2},{2,1},{5,6},{6,5},{9,10},{10,9},{13,14},{14,13},{17,18},{18,... | collective-permute-start | bytes 1179656 | tf_op jit(solution)/shard_map/ppermute | solution.py:221
  122.1 1.6 %collective-permute-done.24 = bf16[4,384,128]{2,1,0:T(8,128)(2,1)S(1)} collective-permute-done((bf16[4,384,128]{2,1,0:T(8,128)(2,1)S(1)}, bf16[4,384,128]{2,1,0:T(8,128)(2,1)S(1)}, u32[]{:S(2)}, u32[]{:S(2)}) %collective-permute-start.24) | collective-permute-done | bytes 393248 | tf_op jit(solution)/shard_map/ppermute | solution.py:229
  124.5 2.2 %collective-permute-start.25 = (bf16[4,384,128]{2,1,0:T(8,128)(2,1)}, bf16[4,384,128]{2,1,0:T(8,128)(2,1)S(1)}, u32[]{:S(2)}, u32[]{:S(2)}) collective-permute-start(bf16[4,384,128]{2,1,0:T(8,128)(2,1)} %add_convert_fusion.2), channel_id=1, source_target_pairs={{1,2},{2,1},{5,6},{6,5},{9,10},{10,9},{13,14},{14,13},{17,18},{18,... | collective-permute-start | bytes 1179656 | tf_op jit(solution)/shard_map/ppermute | solution.py:221
  126.7 2.6 %collective-permute-done.26 = bf16[4,384,128]{2,1,0:T(8,128)(2,1)S(1)} collective-permute-done((bf16[4,384,128]{2,1,0:T(8,128)(2,1)S(1)}, bf16[4,384,128]{2,1,0:T(8,128)(2,1)S(1)}, u32[]{:S(2)}, u32[]{:S(2)}) %collective-permute-start.26) | collective-permute-done | bytes 393248 | tf_op jit(solution)/shard_map/ppermute | solution.py:221
  130.2 1.9 %collective-permute-done.23 = bf16[4,384,128]{2,1,0:T(8,128)(2,1)S(1)} collective-permute-done((bf16[4,384,128]{2,1,0:T(8,128)(2,1)}, bf16[4,384,128]{2,1,0:T(8,128)(2,1)S(1)}, u32[]{:S(2)}, u32[]{:S(2)}) %collective-permute-start.23) | collective-permute-done | bytes 393248 | tf_op jit(solution)/shard_map/ppermute | solution.py:217
  132.1 5.6 %collective-permute-done.20 = bf16[4,384,128]{2,1,0:T(8,128)(2,1)S(1)} collective-permute-done((bf16[4,384,128]{2,1,0:T(8,128)(2,1)S(1)}, bf16[4,384,128]{2,1,0:T(8,128)(2,1)S(1)}, u32[]{:S(2)}, u32[]{:S(2)}) %collective-permute-start.20) | collective-permute-done | bytes 393248 | tf_op jit(solution)/shard_map/ppermute | solution.py:221
  137.7 5.0 %collective-permute-done.25 = bf16[4,384,128]{2,1,0:T(8,128)(2,1)S(1)} collective-permute-done((bf16[4,384,128]{2,1,0:T(8,128)(2,1)}, bf16[4,384,128]{2,1,0:T(8,128)(2,1)S(1)}, u32[]{:S(2)}, u32[]{:S(2)}) %collective-permute-start.25) | collective-permute-done | bytes 393248 | tf_op jit(solution)/shard_map/ppermute | solution.py:221
  142.7 1.5 %add_convert_fusion.3 = (bf16[8,384,128]{2,1,0:T(8,128)(2,1)}, bf16[8,384,128]{2,1,0:T(8,128)(2,1)}) fusion(bf16[4,384,128]{2,1,0:T(8,128)(2,1)S(1)} %collective-permute-done.23, bf16[4,384,128]{2,1,0:T(8,128)(2,1)S(1)} %collective-permute-done.20, bf16[4,384,128]{2,1,0:T(8,128)(2,1)S(1)} %get-tuple-element.29, ...), kind=kLoop, output_to_operand_aliasing={{0}: (9, {}), {1}: (9, {})}, calls=%fused_computation.7 | loop fusion | flops 3932160 | bytes 3935232 | tf_op jit(solution)/shard_map/convert_element_type | solution.py:305
  (66 shorter events, 20.4 us)
Async XLA Ops:
  1.2 4.4 %collective-permute-start = (bf16[3,384,128]{2,1,0:T(8,128)(2,1)S(1)}, bf16[3,384,128]{2,1,0:T(8,128)(2,1)S(1)}, u32[]{:S(2)}, u32[]{:S(2)}) collective-permute-start(bf16[3,384,128]{2,1,0:T(8,128)(2,1)S(1)} %get-tuple-element.43), channel_id=1, source_target_pairs={{0,4},{4,8},{8,12},{12,16},{16,20},{20,24},{24,28},{1,5},{5,9},{9,... | collective-permute-start | bytes 884744 | tf_op jit(solution)/shard_map/ppermute | solution.py:248
  2.9 4.7 %collective-permute-start.6 = (bf16[3,384,128]{2,1,0:T(8,128)(2,1)S(1)}, bf16[3,384,128]{2,1,0:T(8,128)(2,1)S(1)}, u32[]{:S(2)}, u32[]{:S(2)}) collective-permute-start(bf16[3,384,128]{2,1,0:T(8,128)(2,1)S(1)} %get-tuple-element.44), channel_id=1, source_target_pairs={{4,0},{8,4},{12,8},{16,12},{20,16},{24,20},{28,24},{5,1},{9,5},{13... | collective-permute-start | bytes 884744 | tf_op jit(solution)/shard_map/ppermute | solution.py:248
  7.7 37.0 %collective-permute-start.7 = (bf16[384,1536]{1,0:T(8,128)(2,1)S(1)}, bf16[384,1536]{1,0:T(8,128)(2,1)S(1)}, u32[]{:S(2)}, u32[]{:S(2)}) collective-permute-start(bf16[384,1536]{1,0:T(8,128)(2,1)S(1)} %pad_maximum_fusion.1.refs_6_), channel_id=1, source_target_pairs={{0,8},{4,12},{8,0},{12,4},{16,24},{20,28},{24,16},{28,20},{1,9},{5... | collective-permute-start | bytes 3538952 | tf_op jit(solution)/shard_map/ppermute | solution.py:241
  12.9 31.8 %collective-permute-start.8 = (bf16[384,1536]{1,0:T(8,128)(2,1)S(1)}, bf16[384,1536]{1,0:T(8,128)(2,1)S(1)}, u32[]{:S(2)}, u32[]{:S(2)}) collective-permute-start(bf16[384,1536]{1,0:T(8,128)(2,1)S(1)} %pad_maximum_fusion.1.refs_6_), channel_id=1, source_target_pairs={{0,16},{4,20},{8,24},{12,28},{16,0},{20,4},{24,8},{28,12},{1,17},{... | collective-permute-start | bytes 3538952 | tf_op jit(solution)/shard_map/ppermute | solution.py:241
  14.0 37.8 %copy-start.2 = (bf16[1536,192]{0,1:T(8,128)(2,1)S(1)}, bf16[1536,192]{0,1:T(8,128)(2,1)}, u32[]{:S(2)}) copy-start(bf16[1536,192]{0,1:T(8,128)(2,1)} %param.17) | copy-start | bytes 1769476
  14.0 37.8 %copy-start.3 = (bf16[192,1536]{1,0:T(8,128)(2,1)S(1)}, bf16[192,1536]{1,0:T(8,128)(2,1)}, u32[]{:S(2)}) copy-start(bf16[192,1536]{1,0:T(8,128)(2,1)} %param.15) | copy-start | bytes 1769476
  18.5 12.0 %collective-permute-start.1 = (bf16[4,128,384]{2,1,0:T(8,128)(2,1)S(1)}, bf16[4,128,384]{2,1,0:T(8,128)(2,1)S(1)}, u32[]{:S(2)}, u32[]{:S(2)}) collective-permute-start(bf16[4,128,384]{2,1,0:T(8,128)(2,1)S(1)} %depthwise.2), channel_id=1, source_target_pairs={{0,1},{1,0},{2,3},{3,2},{4,5},{5,4},{6,7},{7,6},{8,9},{9,8},{10,11... | collective-permute-start | bytes 1179656 | tf_op jit(solution)/shard_map/ppermute | solution.py:217
  19.0 14.9 %collective-permute-start.2 = (bf16[4,128,384]{2,1,0:T(8,128)(2,1)S(1)}, bf16[4,128,384]{2,1,0:T(8,128)(2,1)S(1)}, u32[]{:S(2)}, u32[]{:S(2)}) collective-permute-start(bf16[4,128,384]{2,1,0:T(8,128)(2,1)S(1)} %depthwise.2), channel_id=1, source_target_pairs={{1,2},{2,1},{5,6},{6,5},{9,10},{10,9},{13,14},{14,13},{17,18},{18,... | collective-permute-start | bytes 1179656 | tf_op jit(solution)/shard_map/ppermute | solution.py:221
  30.5 12.9 %collective-permute-start.4 = (bf16[4,128,384]{2,1,0:T(8,128)(2,1)S(1)}, bf16[4,128,384]{2,1,0:T(8,128)(2,1)S(1)}, u32[]{:S(2)}, u32[]{:S(2)}) collective-permute-start(bf16[4,128,384]{2,1,0:T(8,128)(2,1)S(1)} %collective-permute-done.1), channel_id=1, source_target_pairs={{1,2},{2,1},{5,6},{6,5},{9,10},{10,9},{13,14},{14,13},{17,18},{18,... | collective-permute-start | bytes 1179656 | tf_op jit(solution)/shard_map/ppermute | solution.py:221
  33.9 10.8 %collective-permute-start.3 = (bf16[4,128,384]{2,1,0:T(8,128)(2,1)S(1)}, bf16[4,128,384]{2,1,0:T(8,128)(2,1)S(1)}, u32[]{:S(2)}, u32[]{:S(2)}) collective-permute-start(bf16[4,128,384]{2,1,0:T(8,128)(2,1)S(1)} %collective-permute-done.2), channel_id=1, source_target_pairs={{1,0},{2,3},{5,4},{6,7},{9,8},{10,11},{13,12},{14,15},{17,16},{18,... | collective-permute-start | bytes 1179656 | tf_op jit(solution)/shard_map/ppermute | solution.py:225
  43.4 10.8 %collective-permute-start.5 = (bf16[4,128,384]{2,1,0:T(8,128)(2,1)S(1)}, bf16[4,128,384]{2,1,0:T(8,128)(2,1)S(1)}, u32[]{:S(2)}, u32[]{:S(2)}) collective-permute-start(bf16[4,128,384]{2,1,0:T(8,128)(2,1)S(1)} %collective-permute-done.4), channel_id=1, source_target_pairs={{1,0},{2,3},{5,4},{6,7},{9,8},{10,11},{13,12},{14,15},{17,16},{18,... | collective-permute-start | bytes 1179656 | tf_op jit(solution)/shard_map/ppermute | solution.py:225
  44.7 16.4 %collective-permute-start.11 = (bf16[4,128,384]{2,1,0:T(8,128)(2,1)S(1)}, bf16[4,128,384]{2,1,0:T(8,128)(2,1)S(1)}, u32[]{:S(2)}, u32[]{:S(2)}) collective-permute-start(bf16[4,128,384]{2,1,0:T(8,128)(2,1)S(1)} %depthwise.3), channel_id=1, source_target_pairs={{0,1},{1,0},{2,3},{3,2},{4,5},{5,4},{6,7},{7,6},{8,9},{9,8},{10,11... | collective-permute-start | bytes 1179656 | tf_op jit(solution)/shard_map/ppermute | solution.py:217
  46.3 14.8 %collective-permute-start.12 = (bf16[4,128,384]{2,1,0:T(8,128)(2,1)S(1)}, bf16[4,128,384]{2,1,0:T(8,128)(2,1)S(1)}, u32[]{:S(2)}, u32[]{:S(2)}) collective-permute-start(bf16[4,128,384]{2,1,0:T(8,128)(2,1)S(1)} %depthwise.3), channel_id=1, source_target_pairs={{1,2},{2,1},{5,6},{6,5},{9,10},{10,9},{13,14},{14,13},{17,18},{18,... | collective-permute-start | bytes 1179656 | tf_op jit(solution)/shard_map/ppermute | solution.py:221
  49.6 14.5 %collective-permute-start.9 = (bf16[192,1536]{1,0:T(8,128)(2,1)S(1)}, bf16[192,1536]{1,0:T(8,128)(2,1)S(1)}, u32[]{:S(2)}, u32[]{:S(2)}) collective-permute-start(bf16[192,1536]{1,0:T(8,128)(2,1)S(1)} %slice.21), channel_id=1, source_target_pairs={{0,16},{4,20},{8,24},{12,28},{16,0},{20,4},{24,8},{28,12},{1,17},{... | collective-permute-start | bytes 1769480 | tf_op jit(solution)/shard_map/ppermute | solution.py:241
  51.2 14.4 %collective-permute-start.10 = (bf16[192,1536]{1,0:T(8,128)(2,1)S(1)}, bf16[192,1536]{1,0:T(8,128)(2,1)S(1)}, u32[]{:S(2)}, u32[]{:S(2)}) collective-permute-start(bf16[192,1536]{1,0:T(8,128)(2,1)S(1)} %slice.22), channel_id=1, source_target_pairs={{0,8},{4,12},{8,0},{12,4},{16,24},{20,28},{24,16},{28,20},{1,9},{5... | collective-permute-start | bytes 1769480 | tf_op jit(solution)/shard_map/ppermute | solution.py:241
  65.6 7.9 %collective-permute-start.13 = (bf16[1152,1536]{1,0:T(8,128)(2,1)S(1)}, bf16[1152,1536]{1,0:T(8,128)(2,1)S(1)}, u32[]{:S(2)}, u32[]{:S(2)}) collective-permute-start(bf16[1152,1536]{1,0:T(8,128)(2,1)S(1)} %pad_maximum_fusion), channel_id=1, source_target_pairs={{0,4},{4,0},{8,12},{12,8},{16,20},{20,16},{24,28},{28,24},{1,5},{5... | collective-permute-start | bytes 10616840 | tf_op jit(solution)/shard_map/ppermute | solution.py:241
  65.7 7.8 %collective-permute-start.14 = (bf16[384,1536]{1,0:T(8,128)(2,1)S(1)}, bf16[384,1536]{1,0:T(8,128)(2,1)S(1)}, u32[]{:S(2)}, u32[]{:S(2)}) collective-permute-start(bf16[384,1536]{1,0:T(8,128)(2,1)S(1)} %pad_maximum_fusion.2), channel_id=1, source_target_pairs={{0,4},{4,0},{8,12},{12,8},{16,20},{20,16},{24,28},{28,24},{1,5},{5... | collective-permute-start | bytes 3538952 | tf_op jit(solution)/shard_map/ppermute | solution.py:241
  66.3 19.8 %collective-permute-start.16 = (bf16[4,128,384]{2,1,0:T(8,128)(2,1)S(1)}, bf16[4,128,384]{2,1,0:T(8,128)(2,1)S(1)}, u32[]{:S(2)}, u32[]{:S(2)}) collective-permute-start(bf16[4,128,384]{2,1,0:T(8,128)(2,1)S(1)} %collective-permute-done.12), channel_id=1, source_target_pairs={{1,0},{2,3},{5,4},{6,7},{9,8},{10,11},{13,12},{14,15},{17,16},{18,... | collective-permute-start | bytes 1179656 | tf_op jit(solution)/shard_map/ppermute | solution.py:225
  67.6 14.6 %collective-permute-start.17 = (bf16[4,128,384]{2,1,0:T(8,128)(2,1)S(1)}, bf16[4,128,384]{2,1,0:T(8,128)(2,1)S(1)}, u32[]{:S(2)}, u32[]{:S(2)}) collective-permute-start(bf16[4,128,384]{2,1,0:T(8,128)(2,1)S(1)} %collective-permute-done.11), channel_id=1, source_target_pairs={{1,2},{2,1},{5,6},{6,5},{9,10},{10,9},{13,14},{14,13},{17,18},{18,... | collective-permute-start | bytes 1179656 | tf_op jit(solution)/shard_map/ppermute | solution.py:221
  82.2 10.2 %collective-permute-start.18 = (bf16[4,128,384]{2,1,0:T(8,128)(2,1)S(1)}, bf16[4,128,384]{2,1,0:T(8,128)(2,1)S(1)}, u32[]{:S(2)}, u32[]{:S(2)}) collective-permute-start(bf16[4,128,384]{2,1,0:T(8,128)(2,1)S(1)} %collective-permute-done.17), channel_id=1, source_target_pairs={{1,0},{2,3},{5,4},{6,7},{9,8},{10,11},{13,12},{14,15},{17,16},{18,... | collective-permute-start | bytes 1179656 | tf_op jit(solution)/shard_map/ppermute | solution.py:225
  83.6 19.1 %collective-permute-start.21 = (bf16[4,384,128]{2,1,0:T(8,128)(2,1)S(1)}, bf16[4,384,128]{2,1,0:T(8,128)(2,1)S(1)}, u32[]{:S(2)}, u32[]{:S(2)}) collective-permute-start(bf16[4,384,128]{2,1,0:T(8,128)(2,1)S(1)} %get-tuple-element.33), channel_id=1, source_target_pairs={{0,1},{3,2},{4,5},{7,6},{8,9},{11,10},{12,13},{15,14},{16,17},{19,... | collective-permute-start | bytes 1179656 | tf_op jit(solution)/shard_map/ppermute | solution.py:229
  84.9 21.4 %collective-permute-start.15 = (bf16[4,384,128]{2,1,0:T(8,128)(2,1)S(1)}, bf16[4,384,128]{2,1,0:T(8,128)(2,1)S(1)}, u32[]{:S(2)}, u32[]{:S(2)}) collective-permute-start(bf16[4,384,128]{2,1,0:T(8,128)(2,1)S(1)} %get-tuple-element.30), channel_id=1, source_target_pairs={{0,1},{3,2},{4,5},{7,6},{8,9},{11,10},{12,13},{15,14},{16,17},{19,... | collective-permute-start | bytes 1179656 | tf_op jit(solution)/shard_map/ppermute | solution.py:229
  101.3 13.9 %collective-permute-start.19 = (bf16[4,384,128]{2,1,0:T(8,128)(2,1)S(1)}, bf16[4,384,128]{2,1,0:T(8,128)(2,1)S(1)}, u32[]{:S(2)}, u32[]{:S(2)}) collective-permute-start(bf16[4,384,128]{2,1,0:T(8,128)(2,1)S(1)} %get-tuple-element.35), channel_id=1, source_target_pairs={{0,1},{3,2},{4,5},{7,6},{8,9},{11,10},{12,13},{15,14},{16,17},{19,... | collective-permute-start | bytes 1179656 | tf_op jit(solution)/shard_map/ppermute | solution.py:229
  102.8 14.8 %collective-permute-start.22 = (bf16[4,384,128]{2,1,0:T(8,128)(2,1)S(1)}, bf16[4,384,128]{2,1,0:T(8,128)(2,1)S(1)}, u32[]{:S(2)}, u32[]{:S(2)}) collective-permute-start(bf16[4,384,128]{2,1,0:T(8,128)(2,1)S(1)} %add_convert_fusion.5), channel_id=1, source_target_pairs={{1,2},{2,1},{5,6},{6,5},{9,10},{10,9},{13,14},{14,13},{17,18},{18,... | collective-permute-start | bytes 1179656 | tf_op jit(solution)/shard_map/ppermute | solution.py:221
  105.0 18.7 %collective-permute-start.24 = (bf16[4,384,128]{2,1,0:T(8,128)(2,1)S(1)}, bf16[4,384,128]{2,1,0:T(8,128)(2,1)S(1)}, u32[]{:S(2)}, u32[]{:S(2)}) collective-permute-start(bf16[4,384,128]{2,1,0:T(8,128)(2,1)S(1)} %get-tuple-element.39), channel_id=1, source_target_pairs={{0,1},{3,2},{4,5},{7,6},{8,9},{11,10},{12,13},{15,14},{16,17},{19,... | collective-permute-start | bytes 1179656 | tf_op jit(solution)/shard_map/ppermute | solution.py:229
  106.4 36.3 %copy-start.7 = (f32[384]{0:T(512)S(1)}, f32[384]{0:T(512)}, u32[]{:S(2)}) copy-start(f32[384]{0:T(512)} %param.18) | copy-start | bytes 4612
  106.4 36.3 %copy-start.8 = (f32[384]{0:T(512)S(1)}, f32[384]{0:T(512)}, u32[]{:S(2)}) copy-start(f32[384]{0:T(512)} %param.19) | copy-start | bytes 4612
  115.4 13.9 %collective-permute-start.26 = (bf16[4,384,128]{2,1,0:T(8,128)(2,1)S(1)}, bf16[4,384,128]{2,1,0:T(8,128)(2,1)S(1)}, u32[]{:S(2)}, u32[]{:S(2)}) collective-permute-start(bf16[4,384,128]{2,1,0:T(8,128)(2,1)S(1)} %add_convert_fusion.6), channel_id=1, source_target_pairs={{1,2},{2,1},{5,6},{6,5},{9,10},{10,9},{13,14},{14,13},{17,18},{18,... | collective-permute-start | bytes 1179656 | tf_op jit(solution)/shard_map/ppermute | solution.py:221
  118.4 13.7 %collective-permute-start.23 = (bf16[4,384,128]{2,1,0:T(8,128)(2,1)}, bf16[4,384,128]{2,1,0:T(8,128)(2,1)S(1)}, u32[]{:S(2)}, u32[]{:S(2)}) collective-permute-start(bf16[4,384,128]{2,1,0:T(8,128)(2,1)} %add_convert_fusion.4), channel_id=1, source_target_pairs={{0,1},{1,0},{2,3},{3,2},{4,5},{5,4},{6,7},{7,6},{8,9},{9,8},{10,11... | collective-permute-start | bytes 1179656 | tf_op jit(solution)/shard_map/ppermute | solution.py:217
  118.4 19.3 %collective-permute-start.20 = (bf16[4,384,128]{2,1,0:T(8,128)(2,1)S(1)}, bf16[4,384,128]{2,1,0:T(8,128)(2,1)S(1)}, u32[]{:S(2)}, u32[]{:S(2)}) collective-permute-start(bf16[4,384,128]{2,1,0:T(8,128)(2,1)S(1)} %add_convert_fusion.7), channel_id=1, source_target_pairs={{1,2},{2,1},{5,6},{6,5},{9,10},{10,9},{13,14},{14,13},{17,18},{18,... | collective-permute-start | bytes 1179656 | tf_op jit(solution)/shard_map/ppermute | solution.py:221
  124.5 18.2 %collective-permute-start.25 = (bf16[4,384,128]{2,1,0:T(8,128)(2,1)}, bf16[4,384,128]{2,1,0:T(8,128)(2,1)S(1)}, u32[]{:S(2)}, u32[]{:S(2)}) collective-permute-start(bf16[4,384,128]{2,1,0:T(8,128)(2,1)} %add_convert_fusion.2), channel_id=1, source_target_pairs={{1,2},{2,1},{5,6},{6,5},{9,10},{10,9},{13,14},{14,13},{17,18},{18,... | collective-permute-start | bytes 1179656 | tf_op jit(solution)/shard_map/ppermute | solution.py:221
  130.2 12.6 %collective-permute-start.27 = (bf16[4,384,128]{2,1,0:T(8,128)(2,1)}, bf16[4,384,128]{2,1,0:T(8,128)(2,1)S(1)}, u32[]{:S(2)}, u32[]{:S(2)}) collective-permute-start(bf16[4,384,128]{2,1,0:T(8,128)(2,1)} %add_convert_fusion.1), channel_id=1, source_target_pairs={{0,1},{1,0},{2,3},{3,2},{4,5},{5,4},{6,7},{7,6},{8,9},{9,8},{10,11... | collective-permute-start | bytes 1179656 | tf_op jit(solution)/shard_map/ppermute | solution.py:217
  (6 other events, 84.5 us)

commit v5 on v4

--- a/solution.py
+++ b/solution.py
@@ -10,6 +10,8 @@
 SIDE = 7
 REACH = SIDE // 2
 VMEM_LIMIT = 48 * 1024 * 1024
+MLP_LIMIT = 28 * 1024 * 1024
+NORM_FLOPS = 2000
 EPSILON = 1e-06
 
 
@@ -92,25 +94,16 @@
     return ins, outs
 
 
-def mlp_kernel(*refs):
-    own, near, mid_inner, mid_outer, far_inner, far_outer = refs[:6]
-    refs = refs[6:]
-    parts, refs = refs[: len(refs) - 14], refs[len(refs) - 14 :]
-    shard = parts[0].shape[0] // 2
-    w_in_parts, w_out_parts = weight_pieces(parts, shard)
-    gain_ref, shift_ref, b_in_ref = refs[:3]
-    out_refs = refs[3:7]
-    x, w_in, w_out, hidden, x_sem, in_sem, out_sem = refs[7:]
-    pixels, channels = x.shape
+def start_slabs(slabs, x, sems):
+    own, near, mid_inner, mid_outer, far_inner, far_outer = slabs
     slab = own.shape[1]
-    units = hidden.shape[1]
-    z, t = lax.axis_index("chan"), lax.axis_index("tile")
+    z = lax.axis_index("chan")
     pair, mid, far = line_places(z)
     inner = jnp.logical_or(z == 1, z == 2)
 
     def slab_copy(part, place, sem):
         at = pl.ds(pl.multiple_of(place * slab, 128), slab)
-        return pltpu.make_async_copy(part, x.at[:, at], x_sem.at[sem])
+        return pltpu.make_async_copy(part, x.at[:, at], sems.at[sem])
 
     slab_copy(own, z, 0).start()
     slab_copy(near, pair, 1).start()
@@ -125,48 +118,52 @@
         slab_copy(mid_outer, mid, 2).start()
         slab_copy(far_outer, far, 3).start()
 
-    def shard_copy(piece, target, sems):
-        part, first, k = piece
-        at = pl.ds(pl.multiple_of((t ^ k) * shard, 16), shard)
-        return pltpu.make_async_copy(part.at[first : first + shard, :], target.at[at, :], sems.at[k])
-
-    for piece in w_in_parts:
-        shard_copy(piece, w_in, in_sem).start()
-    for piece in w_out_parts:
-        shard_copy(piece, w_out, out_sem).start()
-
-    slab_copy(own, z, 0).wait()
-    slab_copy(near, pair, 1).wait()
-    slab_copy(mid_inner, mid, 2).wait()
-    slab_copy(far_inner, far, 3).wait()
-
-    step = 256
+    def wait():
+        slab_copy(own, z, 0).wait()
+        slab_copy(near, pair, 1).wait()
+        slab_copy(mid_inner, mid, 2).wait()
+        slab_copy(far_inner, far, 3).wait()
+
+    return wait
+
+
+def normalize(x, out, gain_ref, shift_ref):
+    pixels, channels = x.shape
+    step = 256 if pixels % 256 == 0 else 64
     gain, shift = gain_ref[...], shift_ref[...]
 
-    def normalize(i, carry):
+    def block(i, carry):
         at = pl.ds(pl.multiple_of(i * step, step), step)
         values = x[at, :].astype(jnp.float32)
         average = jnp.sum(values, axis=1, keepdims=True) * (1.0 / channels)
         centered = values - average
         variance = jnp.sum(centered * centered, axis=1, keepdims=True) * (1.0 / channels)
-        x[at, :] = (centered * lax.rsqrt(variance + EPSILON) * gain + shift).astype(x.dtype)
+        out[at, :] = (centered * lax.rsqrt(variance + EPSILON) * gain + shift).astype(out.dtype)
         return carry
 
-    lax.fori_loop(0, pixels // step, normalize, 0)
-
-    for piece in w_in_parts:
-        shard_copy(piece, w_in, in_sem).wait()
+    lax.fori_loop(0, pixels // step, block, 0)
+
+
+def norm_kernel(*refs):
+    gain_ref, shift_ref, out_ref, x, x_sem = refs[6:]
+    start_slabs(refs[:6], x, x_sem)()
+    normalize(x, out_ref, gain_ref, shift_ref)
+
+
+def lift(x, w_in, b_in_ref, hidden):
     block = 256
-    for f in range(0, units, block):
+    for f in range(0, hidden.shape[1], block):
         pre_act = jnp.dot(x[...], w_in[:, f : f + block], preferred_element_type=jnp.float32)
         pre_act = pre_act + b_in_ref[:, f : f + block]
         gelu = pre_act * (lax.erf(pre_act * (0.5**0.5)) * 0.5 + 0.5)
         hidden[:, f : f + block] = gelu.astype(hidden.dtype)
 
-    for piece in w_out_parts:
-        shard_copy(piece, w_out, out_sem).wait()
+
+def project(hidden, w_out, out_refs):
+    z = lax.axis_index("chan")
+    pair, mid, far = line_places(z)
     for out_ref, place in zip(out_refs, (far, mid, pair, z), strict=True):
-        rows, _, width = out_ref.shape
+        rows, slab, width = out_ref.shape
         at = pl.ds(pl.multiple_of(place * slab, 16), slab)
         partial = lax.dot_general(
             w_out[at, :], hidden[...], (((1,), (1,)), ((), ())), preferred_element_type=jnp.float32
@@ -175,42 +172,114 @@
             out_ref[row] = partial[:, row * width : (row + 1) * width].astype(out_ref.dtype)
 
 
-def mlp_chunk(slabs, weights, gain, shift, b_in):
+def start_shards(pieces, target, shard, sems):
+    t = lax.axis_index("tile")
+
+    def shard_copy(piece):
+        part, first, k = piece
+        at = pl.ds(pl.multiple_of((t ^ k) * shard, 16), shard)
+        return pltpu.make_async_copy(part.at[first : first + shard, :], target.at[at, :], sems.at[k])
+
+    for piece in pieces:
+        shard_copy(piece).start()
+
+    def wait():
+        for piece in pieces:
+            shard_copy(piece).wait()
+
+    return wait
+
+
+def mlp_kernel(*refs):
+    normed_ref, parts, b_in_ref, out_refs = refs[0], refs[1:8], refs[8], refs[9:13]
+    w_in, w_out, hidden, in_sem, out_sem = refs[13:]
+    shard = parts[0].shape[0] // 2
+    ins, outs = weight_pieces(parts, shard)
+    w_in_there = start_shards(ins, w_in, shard, in_sem)
+    w_out_there = start_shards(outs, w_out, shard, out_sem)
+    w_in_there()
+    lift(normed_ref, w_in, b_in_ref, hidden)
+    w_out_there()
+    project(hidden, w_out, out_refs)
+
+
+def norm_mlp_kernel(*refs):
+    parts, (gain_ref, shift_ref, b_in_ref), out_refs = refs[6:13], refs[13:16], refs[16:20]
+    x, w_in, w_out, hidden, x_sem, in_sem, out_sem = refs[20:]
+    shard = parts[0].shape[0] // 2
+    ins, outs = weight_pieces(parts, shard)
+    x_there = start_slabs(refs[:6], x, x_sem)
+    w_in_there = start_shards(ins, w_in, shard, in_sem)
+    w_out_there = start_shards(outs, w_out, shard, out_sem)
+    x_there()
+    normalize(x, x, gain_ref, shift_ref)
+    w_in_there()
+    lift(x, w_in, b_in_ref, hidden)
+    w_out_there()
+    project(hidden, w_out, out_refs)
+
+
+ANYWHERE = pl.BlockSpec(memory_space=pl.ANY)
+WHOLE = pl.BlockSpec(memory_space=pltpu.VMEM)
+SHARDS = 8
+
+
+def norm_chunk(slabs, gain, shift):
     rows, width, slab = slabs[0].shape
-    shards = 8
-    units = weights[0].shape[1]
-    channels = slab * 4
-    pixels = rows * width
-    anywhere = pl.BlockSpec(memory_space=pl.ANY)
-    whole = pl.BlockSpec(memory_space=pltpu.VMEM)
+    pixels, channels = rows * width, 4 * slab
     return pl.pallas_call(
-        mlp_kernel,
-        in_specs=[anywhere] * (len(slabs) + len(weights)) + [whole] * 3,
-        out_specs=[whole] * 4,
-        out_shape=[jax.ShapeDtypeStruct((rows, slab, width), jnp.bfloat16)] * 4,
+        norm_kernel,
+        in_specs=[ANYWHERE] * 6 + [WHOLE] * 2,
+        out_specs=WHOLE,
+        out_shape=jax.ShapeDtypeStruct((pixels, channels), jnp.bfloat16),
         scratch_shapes=[
             pltpu.VMEM((pixels, channels), jnp.bfloat16),
+            pltpu.SemaphoreType.DMA((4,)),
+        ],
+        compiler_params=pltpu.CompilerParams(vmem_limit_bytes=MLP_LIMIT),
+        cost_estimate=pl.CostEstimate(
+            flops=NORM_FLOPS * pixels * channels, bytes_accessed=4 * pixels * channels, transcendentals=0
+        ),
+        name="norm",
+    )(*[s.reshape(pixels, slab) for s in slabs], gain[None], shift[None])
+
+
+def mlp_chunk(x, weights, rows, gain, shift, b_in):
+    normed = not isinstance(x, list)
+    if normed:
+        pixels, channels = x.shape
+        slab, width = channels // 4, pixels // rows
+        inputs, vectors = [x], [b_in[None]]
+        kernel, scratch = mlp_kernel, []
+        specs = [WHOLE]
+    else:
+        _, width, slab = x[0].shape
+        pixels, channels = rows * width, 4 * slab
+        inputs, vectors = [s.reshape(pixels, slab) for s in x], [gain[None], shift[None], b_in[None]]
+        kernel, scratch = norm_mlp_kernel, [pltpu.VMEM((pixels, channels), jnp.bfloat16)]
+        specs = [ANYWHERE] * 6
+    units = weights[0].shape[1]
+    return pl.pallas_call(
+        kernel,
+        in_specs=specs + [ANYWHERE] * len(weights) + [WHOLE] * len(vectors),
+        out_specs=[WHOLE] * 4,
+        out_shape=[jax.ShapeDtypeStruct((rows, slab, width), jnp.bfloat16)] * 4,
+        scratch_shapes=scratch
+        + [
             pltpu.VMEM((channels, units), jnp.bfloat16),
             pltpu.VMEM((channels, units), jnp.bfloat16),
             pltpu.VMEM((pixels, units), jnp.bfloat16),
-            pltpu.SemaphoreType.DMA((4,)),
-            pltpu.SemaphoreType.DMA((shards,)),
-            pltpu.SemaphoreType.DMA((shards,)),
-        ],
-        compiler_params=pltpu.CompilerParams(vmem_limit_bytes=28 * 1024 * 1024),
+        ]
+        + ([] if normed else [pltpu.SemaphoreType.DMA((4,))])
+        + [pltpu.SemaphoreType.DMA((SHARDS,)), pltpu.SemaphoreType.DMA((SHARDS,))],
+        compiler_params=pltpu.CompilerParams(vmem_limit_bytes=MLP_LIMIT),
         cost_estimate=pl.CostEstimate(
             flops=4 * pixels * channels * units,
             bytes_accessed=4 * channels * units + 4 * pixels * channels,
             transcendentals=pixels * units,
         ),
         name="mlp",
-    )(
-        *[s.reshape(pixels, slab) for s in slabs],
-        *weights,
-        gain[None],
-        shift[None],
-        b_in[None],
-    )
+    )(*inputs, *weights, *vectors)
 
 
 def to_pair(array):
@@ -253,7 +322,7 @@
     rows = height // 2
     shard = w_in.shape[0]
     conv = functools.partial(conv_chunk, features=features, taps=dw_weight.T, bias=dw_bias[None])
-    mlp = functools.partial(mlp_chunk, gain=ln_gain, shift=ln_bias, b_in=b_in)
+    mlp = functools.partial(mlp_chunk, rows=rows, gain=ln_gain, shift=ln_bias, b_in=b_in)
 
     low, high = rims(features[:REACH], features[-REACH:])
     slab_0 = conv(0, rows, low=low, high=high)
@@ -279,7 +348,8 @@
     weights = [own, own_x, own_y, in_xy, out_xy, others, other_xy]
 
     line_0 = [slab_0, near_0, mid_in_0, mid_out_0, far_in_0, far_out_0]
-    far_0, mid_0, pair_0, home_0 = mlp(line_0, weights)
+    normed_0 = norm_chunk(line_0, ln_gain, ln_bias)
+    far_0, mid_0, pair_0, home_0 = mlp(normed_0, weights)
     far_out_1 = outward(after(far_in_1, far_0))
     far_sum_0, mid_from_0 = add(far_0, inward(far_0)), inward(mid_0)
 

time: 145 us -> 142 us (0.979)
  waiting for transfers between devices: 61.6 us -> 59.3 us
    pallas_call x2 -> x3, Pallas kernels: 17.6 us -> 17.6 us  [the longest x2 16.3 us: mlp_chunk(): pl.pallas_call(kernel, in_specs=specs + [ANYWHERE] * len(weights) + [WHOL...]
  transfers between devices with their start and end apart: 28 -> 28, of which waited for: 15 -> 16; matrix products, arithmetic and copies ran while one was open for 3% -> 3% of each run, Pallas kernels for 18% -> 19%
where the time goes in v5:
time: 142 us
  waiting for transfers between devices  59.3 us (42%)
  starting transfers between devices  48.4 us (34%)
  Pallas kernels  26.5 us (19%)
  other arithmetic  5.99 us (4%)
    ppermute x8, starting transfers between devices, to_middle(): return lax.ppermute(array, 'chan', [(1, 2), (2, 1)])  23.7 us
    ppermute x8, waiting for transfers between devices, to_middle(): return lax.ppermute(array, 'chan', [(1, 2), (2, 1)])  16.6 us
    pallas_call x2, Pallas kernels, mlp_chunk(): pl.pallas_call(kernel, in_specs=specs + [ANYWHERE] * len(weights) + [WHOL...  16.3 us
    ppermute x4, waiting for transfers between devices, to_pair(): return lax.ppermute(array, 'chan', [(0, 1), (1, 0), (2, 3), (3, 2)])  15.6 us
    ppermute x4, waiting for transfers between devices, inward(): return lax.ppermute(array, 'chan', [(0, 1), (3, 2)])  10.5 us
    ppermute x6, starting transfers between devices, flipped(): return lax.ppermute(array, 'tile', [(i, i ^ bit) for i in range(8)])  9.1 us
    pallas_call x2, Pallas kernels, conv_chunk(): pl.pallas_call(functools.partial(conv_kernel, tuple(plan)), grid=(slab //...  8.89 us
    ppermute x4, waiting for transfers between devices, outward(): return lax.ppermute(array, 'chan', [(1, 0), (2, 3)])  7.54 us
  transfers between devices with their start and end apart: 28, of which 16 were waited for; matrix products, arithmetic and copies ran while one was open for 3% of the time, Pallas kernels for 19%

profile of v5, /device:TPU:8, one launch (start us, length us, event | category | flops | bytes accessed | tf_op | source)
XLA Modules:
  0.0 141.8 jit_solution(8748204590534001837)
XLA Ops:
  1.2 1.8 %collective-permute-start = (bf16[3,384,128]{2,1,0:T(8,128)(2,1)S(1)}, bf16[3,384,128]{2,1,0:T(8,128)(2,1)S(1)}, u32[]{:S(2)}, u32[]{:S(2)}) collective-permute-start(bf16[3,384,128]{2,1,0:T(8,128)(2,1)S(1)} %get-tuple-element.43), channel_id=1, source_target_pairs={{0,4},{4,8},{8,12},{12,16},{16,20},{20,24},{24,28},{1,5},{5,9},{9,... | collective-permute-start | bytes 884744 | tf_op jit(solution)/shard_map/ppermute | solution.py:317
  5.6 2.1 %collective-permute-done.6.refs_1_ = bf16[3,384,128]{2,1,0:T(8,128)(2,1)S(1)} collective-permute-done((bf16[3,384,128]{2,1,0:T(8,128)(2,1)S(1)}, bf16[3,384,128]{2,1,0:T(8,128)(2,1)S(1)}, u32[]{:S(2)}, u32[]{:S(2)}) %collective-permute-start.6) | collective-permute-done | bytes 294944 | tf_op jit(solution)/shard_map/ppermute | solution.py:317
  7.7 5.2 %collective-permute-start.7 = (bf16[384,1536]{1,0:T(8,128)(2,1)S(1)}, bf16[384,1536]{1,0:T(8,128)(2,1)S(1)}, u32[]{:S(2)}, u32[]{:S(2)}) collective-permute-start(bf16[384,1536]{1,0:T(8,128)(2,1)S(1)} %pad_maximum_fusion.1.refs_1_.refs_6_), channel_id=1, source_target_pairs={{0,8},{4,12},{8,0},{12,4},{16,24},{20,28},{24,16},{28,20},{1,9},{5... | collective-permute-start | bytes 3538952 | tf_op jit(solution)/shard_map/ppermute | solution.py:310
  14.0 4.4 %depthwise.2 = bf16[4,128,384]{2,1,0:T(8,128)(2,1)S(1)} custom-call(bf16[8,384,128]{2,1,0:T(8,128)(2,1)S(1)} %copy-done, bf16[3,384,128]{2,1,0:T(8,128)(2,1)S(1)} %collective-permute-done.refs_1_, f32[49,384]{1,0:T(8,128)S(1)} %bitcast.16, f32[1,384]{1,0:T(1,128)S(1)} %broadcast_in_dim.8.refs_3_), custom_call_target="tpu_custom_call" | custom-call | flops 19267584 | bytes 786432 | tf_op jit(solution)/shard_map/depthwise/pallas_call | solution.py:63
  19.0 4.6 %collective-permute-start.2 = (bf16[4,128,384]{2,1,0:T(8,128)(2,1)S(1)}, bf16[4,128,384]{2,1,0:T(8,128)(2,1)S(1)}, u32[]{:S(2)}, u32[]{:S(2)}) collective-permute-start(bf16[4,128,384]{2,1,0:T(8,128)(2,1)S(1)} %depthwise.2), channel_id=1, source_target_pairs={{1,2},{2,1},{5,6},{6,5},{9,10},{10,9},{13,14},{14,13},{17,18},{18,... | collective-permute-start | bytes 1179656 | tf_op jit(solution)/shard_map/ppermute | solution.py:290
  23.6 6.8 %collective-permute-done.1 = bf16[4,128,384]{2,1,0:T(8,128)(2,1)S(1)} collective-permute-done((bf16[4,128,384]{2,1,0:T(8,128)(2,1)S(1)}, bf16[4,128,384]{2,1,0:T(8,128)(2,1)S(1)}, u32[]{:S(2)}, u32[]{:S(2)}) %collective-permute-start.1) | collective-permute-done | bytes 393248 | tf_op jit(solution)/shard_map/ppermute | solution.py:286
  30.5 3.5 %collective-permute-start.4 = (bf16[4,128,384]{2,1,0:T(8,128)(2,1)S(1)}, bf16[4,128,384]{2,1,0:T(8,128)(2,1)S(1)}, u32[]{:S(2)}, u32[]{:S(2)}) collective-permute-start(bf16[4,128,384]{2,1,0:T(8,128)(2,1)S(1)} %collective-permute-done.1), channel_id=1, source_target_pairs={{1,2},{2,1},{5,6},{6,5},{9,10},{10,9},{13,14},{14,13},{17,18},{18,... | collective-permute-start | bytes 1179656 | tf_op jit(solution)/shard_map/ppermute | solution.py:290
  35.3 4.4 %depthwise.3 = bf16[4,128,384]{2,1,0:T(8,128)(2,1)S(1)} custom-call(bf16[8,384,128]{2,1,0:T(8,128)(2,1)S(1)} %copy-done, bf16[3,384,128]{2,1,0:T(8,128)(2,1)S(1)} %collective-permute-done.6.refs_1_, f32[49,384]{1,0:T(8,128)S(1)} %bitcast.17, f32[1,384]{1,0:T(1,128)S(1)} %broadcast_in_dim.8.refs_3_), custom_call_target="tpu_custom_call" | custom-call | flops 19267584 | bytes 786432 | tf_op jit(solution)/shard_map/depthwise/pallas_call | solution.py:63
  39.7 3.7 %collective-permute-done.4 = bf16[4,128,384]{2,1,0:T(8,128)(2,1)S(1)} collective-permute-done((bf16[4,128,384]{2,1,0:T(8,128)(2,1)S(1)}, bf16[4,128,384]{2,1,0:T(8,128)(2,1)S(1)}, u32[]{:S(2)}, u32[]{:S(2)}) %collective-permute-start.4) | collective-permute-done | bytes 393248 | tf_op jit(solution)/shard_map/ppermute | solution.py:290
  44.7 1.6 %collective-permute-start.11 = (bf16[4,128,384]{2,1,0:T(8,128)(2,1)S(1)}, bf16[4,128,384]{2,1,0:T(8,128)(2,1)S(1)}, u32[]{:S(2)}, u32[]{:S(2)}) collective-permute-start(bf16[4,128,384]{2,1,0:T(8,128)(2,1)S(1)} %depthwise.3), channel_id=1, source_target_pairs={{0,1},{1,0},{2,3},{3,2},{4,5},{5,4},{6,7},{7,6},{8,9},{9,8},{10,11... | collective-permute-start | bytes 1179656 | tf_op jit(solution)/shard_map/ppermute | solution.py:286
  46.3 3.2 %collective-permute-start.12 = (bf16[4,128,384]{2,1,0:T(8,128)(2,1)S(1)}, bf16[4,128,384]{2,1,0:T(8,128)(2,1)S(1)}, u32[]{:S(2)}, u32[]{:S(2)}) collective-permute-start(bf16[4,128,384]{2,1,0:T(8,128)(2,1)S(1)} %depthwise.3), channel_id=1, source_target_pairs={{1,2},{2,1},{5,6},{6,5},{9,10},{10,9},{13,14},{14,13},{17,18},{18,... | collective-permute-start | bytes 1179656 | tf_op jit(solution)/shard_map/ppermute | solution.py:290
  49.6 1.6 %collective-permute-start.9 = (bf16[192,1536]{1,0:T(8,128)(2,1)S(1)}, bf16[192,1536]{1,0:T(8,128)(2,1)S(1)}, u32[]{:S(2)}, u32[]{:S(2)}) collective-permute-start(bf16[192,1536]{1,0:T(8,128)(2,1)S(1)} %slice.21), channel_id=1, source_target_pairs={{0,16},{4,20},{8,24},{12,28},{16,0},{20,4},{24,8},{28,12},{1,17},{... | collective-permute-start | bytes 1769480 | tf_op jit(solution)/shard_map/ppermute | solution.py:310
  52.1 2.1 %collective-permute-done.5 = bf16[4,128,384]{2,1,0:T(8,128)(2,1)S(1)} collective-permute-done((bf16[4,128,384]{2,1,0:T(8,128)(2,1)S(1)}, bf16[4,128,384]{2,1,0:T(8,128)(2,1)S(1)}, u32[]{:S(2)}, u32[]{:S(2)}) %collective-permute-start.5) | collective-permute-done | bytes 393248 | tf_op jit(solution)/shard_map/ppermute | solution.py:294
  54.2 6.9 %collective-permute-done.11 = bf16[4,128,384]{2,1,0:T(8,128)(2,1)S(1)} collective-permute-done((bf16[4,128,384]{2,1,0:T(8,128)(2,1)S(1)}, bf16[4,128,384]{2,1,0:T(8,128)(2,1)S(1)}, u32[]{:S(2)}, u32[]{:S(2)}) %collective-permute-start.11) | collective-permute-done | bytes 393248 | tf_op jit(solution)/shard_map/ppermute | solution.py:286
  61.1 3.0 %collective-permute-done.9.refs_4_.refs_9_ = bf16[192,1536]{1,0:T(8,128)(2,1)S(1)} collective-permute-done((bf16[192,1536]{1,0:T(8,128)(2,1)S(1)}, bf16[192,1536]{1,0:T(8,128)(2,1)S(1)}, u32[]{:S(2)}, u32[]{:S(2)}) %collective-permute-start.9) | collective-permute-done | bytes 589856 | tf_op jit(solution)/shard_map/ppermute | solution.py:310
  64.0 1.6 %collective-permute-done.10.refs_5_.refs_10_ = bf16[192,1536]{1,0:T(8,128)(2,1)S(1)} collective-permute-done((bf16[192,1536]{1,0:T(8,128)(2,1)S(1)}, bf16[192,1536]{1,0:T(8,128)(2,1)S(1)}, u32[]{:S(2)}, u32[]{:S(2)}) %collective-permute-start.10) | collective-permute-done | bytes 589856 | tf_op jit(solution)/shard_map/ppermute | solution.py:310
  68.9 2.2 %collective-permute-start.17 = (bf16[4,128,384]{2,1,0:T(8,128)(2,1)S(1)}, bf16[4,128,384]{2,1,0:T(8,128)(2,1)S(1)}, u32[]{:S(2)}, u32[]{:S(2)}) collective-permute-start(bf16[4,128,384]{2,1,0:T(8,128)(2,1)S(1)} %collective-permute-done.11), channel_id=1, source_target_pairs={{1,2},{2,1},{5,6},{6,5},{9,10},{10,9},{13,14},{14,13},{17,18},{18,... | collective-permute-start | bytes 1179656 | tf_op jit(solution)/shard_map/ppermute | solution.py:290
  71.1 2.4 %collective-permute-done.14.refs_7_.refs_12_ = bf16[384,1536]{1,0:T(8,128)(2,1)S(1)} collective-permute-done((bf16[384,1536]{1,0:T(8,128)(2,1)S(1)}, bf16[384,1536]{1,0:T(8,128)(2,1)S(1)}, u32[]{:S(2)}, u32[]{:S(2)}) %collective-permute-start.14) | collective-permute-done | bytes 1179680 | tf_op jit(solution)/shard_map/ppermute | solution.py:310
  73.5 7.4 %mlp.2 = (bf16[4,384,128]{2,1,0:T(8,128)(2,1)S(1)}, bf16[4,384,128]{2,1,0:T(8,128)(2,1)S(1)}, bf16[4,384,128]{2,1,0:T(8,128)(2,1)S(1)}, bf16[4,384,128]{2,1,0:T(8,128)(2,1)S(1)}) custom-call(bf16[512,1536]{1,0:T(8,128)(2,1)S(1)} %norm.1.refs_0_, bf16[384,1536]{1,0:T(8,128)(2,1)S(1)} %pad_maximum_fusion.1.refs_1_.refs_6_, ...), custom_call_target="tpu_custom_call" | custom-call | flops 4831838208 | bytes 12582912 | tf_op jit(solution)/shard_map/mlp/pallas_call | solution.py:262
  85.8 5.5 %collective-permute-done.18 = bf16[4,128,384]{2,1,0:T(8,128)(2,1)S(1)} collective-permute-done((bf16[4,128,384]{2,1,0:T(8,128)(2,1)S(1)}, bf16[4,128,384]{2,1,0:T(8,128)(2,1)S(1)}, u32[]{:S(2)}, u32[]{:S(2)}) %collective-permute-start.18) | collective-permute-done | bytes 393248 | tf_op jit(solution)/shard_map/ppermute | solution.py:294
  91.2 8.9 %mlp.3 = (bf16[4,384,128]{2,1,0:T(8,128)(2,1)S(1)}, bf16[4,384,128]{2,1,0:T(8,128)(2,1)S(1)}, bf16[4,384,128]{2,1,0:T(8,128)(2,1)S(1)}, bf16[4,384,128]{2,1,0:T(8,128)(2,1)S(1)}) custom-call(bf16[512,384]{1,0:T(8,128)(2,1)S(1)} %bitcast.14, bf16[512,384]{1,0:T(8,128)(2,1)S(1)} %bitcast.18, bf16[512,384]{1,0:T(8,128)(2,1)S(1)} %bitcast.19, ...), custom_call_target="tpu_custom_call" | custom-call | flops 4831838208 | bytes 12582912 | tf_op jit(solution)/shard_map/mlp/pallas_call | solution.py:262
  101.5 2.2 %collective-permute-start.22 = (bf16[4,384,128]{2,1,0:T(8,128)(2,1)S(1)}, bf16[4,384,128]{2,1,0:T(8,128)(2,1)S(1)}, u32[]{:S(2)}, u32[]{:S(2)}) collective-permute-start(bf16[4,384,128]{2,1,0:T(8,128)(2,1)S(1)} %add_convert_fusion.5), channel_id=1, source_target_pairs={{1,2},{2,1},{5,6},{6,5},{9,10},{10,9},{13,14},{14,13},{17,18},{18,... | collective-permute-start | bytes 1179656 | tf_op jit(solution)/shard_map/ppermute | solution.py:290
  105.2 8.9 %collective-permute-done.19 = bf16[4,384,128]{2,1,0:T(8,128)(2,1)S(1)} collective-permute-done((bf16[4,384,128]{2,1,0:T(8,128)(2,1)S(1)}, bf16[4,384,128]{2,1,0:T(8,128)(2,1)S(1)}, u32[]{:S(2)}, u32[]{:S(2)}) %collective-permute-start.19) | collective-permute-done | bytes 393248 | tf_op jit(solution)/shard_map/ppermute | solution.py:298
  114.2 2.2 %collective-permute-start.26 = (bf16[4,384,128]{2,1,0:T(8,128)(2,1)S(1)}, bf16[4,384,128]{2,1,0:T(8,128)(2,1)S(1)}, u32[]{:S(2)}, u32[]{:S(2)}) collective-permute-start(bf16[4,384,128]{2,1,0:T(8,128)(2,1)S(1)} %add_convert_fusion.6), channel_id=1, source_target_pairs={{1,2},{2,1},{5,6},{6,5},{9,10},{10,9},{13,14},{14,13},{17,18},{18,... | collective-permute-start | bytes 1179656 | tf_op jit(solution)/shard_map/ppermute | solution.py:290
  117.2 3.6 %collective-permute-start.20 = (bf16[4,384,128]{2,1,0:T(8,128)(2,1)S(1)}, bf16[4,384,128]{2,1,0:T(8,128)(2,1)S(1)}, u32[]{:S(2)}, u32[]{:S(2)}) collective-permute-start(bf16[4,384,128]{2,1,0:T(8,128)(2,1)S(1)} %add_convert_fusion.7), channel_id=1, source_target_pairs={{1,2},{2,1},{5,6},{6,5},{9,10},{10,9},{13,14},{14,13},{17,18},{18,... | collective-permute-start | bytes 1179656 | tf_op jit(solution)/shard_map/ppermute | solution.py:290
  120.9 1.6 %collective-permute-done.24 = bf16[4,384,128]{2,1,0:T(8,128)(2,1)S(1)} collective-permute-done((bf16[4,384,128]{2,1,0:T(8,128)(2,1)S(1)}, bf16[4,384,128]{2,1,0:T(8,128)(2,1)S(1)}, u32[]{:S(2)}, u32[]{:S(2)}) %collective-permute-start.24) | collective-permute-done | bytes 393248 | tf_op jit(solution)/shard_map/ppermute | solution.py:298
  123.3 2.2 %collective-permute-start.25 = (bf16[4,384,128]{2,1,0:T(8,128)(2,1)}, bf16[4,384,128]{2,1,0:T(8,128)(2,1)S(1)}, u32[]{:S(2)}, u32[]{:S(2)}) collective-permute-start(bf16[4,384,128]{2,1,0:T(8,128)(2,1)} %add_convert_fusion.2), channel_id=1, source_target_pairs={{1,2},{2,1},{5,6},{6,5},{9,10},{10,9},{13,14},{14,13},{17,18},{18,... | collective-permute-start | bytes 1179656 | tf_op jit(solution)/shard_map/ppermute | solution.py:290
  125.5 2.6 %collective-permute-done.26 = bf16[4,384,128]{2,1,0:T(8,128)(2,1)S(1)} collective-permute-done((bf16[4,384,128]{2,1,0:T(8,128)(2,1)S(1)}, bf16[4,384,128]{2,1,0:T(8,128)(2,1)S(1)}, u32[]{:S(2)}, u32[]{:S(2)}) %collective-permute-start.26) | collective-permute-done | bytes 393248 | tf_op jit(solution)/shard_map/ppermute | solution.py:290
  129.0 1.9 %collective-permute-done.23 = bf16[4,384,128]{2,1,0:T(8,128)(2,1)S(1)} collective-permute-done((bf16[4,384,128]{2,1,0:T(8,128)(2,1)}, bf16[4,384,128]{2,1,0:T(8,128)(2,1)S(1)}, u32[]{:S(2)}, u32[]{:S(2)}) %collective-permute-start.23) | collective-permute-done | bytes 393248 | tf_op jit(solution)/shard_map/ppermute | solution.py:286
  130.9 5.2 %collective-permute-done.20 = bf16[4,384,128]{2,1,0:T(8,128)(2,1)S(1)} collective-permute-done((bf16[4,384,128]{2,1,0:T(8,128)(2,1)S(1)}, bf16[4,384,128]{2,1,0:T(8,128)(2,1)S(1)}, u32[]{:S(2)}, u32[]{:S(2)}) %collective-permute-start.20) | collective-permute-done | bytes 393248 | tf_op jit(solution)/shard_map/ppermute | solution.py:290
  136.1 4.2 %collective-permute-done.25 = bf16[4,384,128]{2,1,0:T(8,128)(2,1)S(1)} collective-permute-done((bf16[4,384,128]{2,1,0:T(8,128)(2,1)}, bf16[4,384,128]{2,1,0:T(8,128)(2,1)S(1)}, u32[]{:S(2)}, u32[]{:S(2)}) %collective-permute-start.25) | collective-permute-done | bytes 393248 | tf_op jit(solution)/shard_map/ppermute | solution.py:290
  140.4 1.5 %add_convert_fusion.3 = (bf16[8,384,128]{2,1,0:T(8,128)(2,1)}, bf16[8,384,128]{2,1,0:T(8,128)(2,1)}) fusion(bf16[4,384,128]{2,1,0:T(8,128)(2,1)S(1)} %collective-permute-done.23, bf16[4,384,128]{2,1,0:T(8,128)(2,1)S(1)} %collective-permute-done.20, bf16[4,384,128]{2,1,0:T(8,128)(2,1)S(1)} %get-tuple-element.29, ...), kind=kLoop, output_to_operand_aliasing={{0}: (9, {}), {1}: (9, {})}, calls=%fused_computation.7 | loop fusion | flops 3932160 | bytes 3935232 | tf_op jit(solution)/shard_map/convert_element_type | solution.py:375
  (67 shorter events, 22.5 us)
Async XLA Ops:
  1.2 4.4 %collective-permute-start = (bf16[3,384,128]{2,1,0:T(8,128)(2,1)S(1)}, bf16[3,384,128]{2,1,0:T(8,128)(2,1)S(1)}, u32[]{:S(2)}, u32[]{:S(2)}) collective-permute-start(bf16[3,384,128]{2,1,0:T(8,128)(2,1)S(1)} %get-tuple-element.43), channel_id=1, source_target_pairs={{0,4},{4,8},{8,12},{12,16},{16,20},{20,24},{24,28},{1,5},{5,9},{9,... | collective-permute-start | bytes 884744 | tf_op jit(solution)/shard_map/ppermute | solution.py:317
  2.9 4.7 %collective-permute-start.6 = (bf16[3,384,128]{2,1,0:T(8,128)(2,1)S(1)}, bf16[3,384,128]{2,1,0:T(8,128)(2,1)S(1)}, u32[]{:S(2)}, u32[]{:S(2)}) collective-permute-start(bf16[3,384,128]{2,1,0:T(8,128)(2,1)S(1)} %get-tuple-element.44), channel_id=1, source_target_pairs={{4,0},{8,4},{12,8},{16,12},{20,16},{24,20},{28,24},{5,1},{9,5},{13... | collective-permute-start | bytes 884744 | tf_op jit(solution)/shard_map/ppermute | solution.py:317
  7.7 37.0 %collective-permute-start.7 = (bf16[384,1536]{1,0:T(8,128)(2,1)S(1)}, bf16[384,1536]{1,0:T(8,128)(2,1)S(1)}, u32[]{:S(2)}, u32[]{:S(2)}) collective-permute-start(bf16[384,1536]{1,0:T(8,128)(2,1)S(1)} %pad_maximum_fusion.1.refs_1_.refs_6_), channel_id=1, source_target_pairs={{0,8},{4,12},{8,0},{12,4},{16,24},{20,28},{24,16},{28,20},{1,9},{5... | collective-permute-start | bytes 3538952 | tf_op jit(solution)/shard_map/ppermute | solution.py:310
  12.9 31.8 %collective-permute-start.8 = (bf16[384,1536]{1,0:T(8,128)(2,1)S(1)}, bf16[384,1536]{1,0:T(8,128)(2,1)S(1)}, u32[]{:S(2)}, u32[]{:S(2)}) collective-permute-start(bf16[384,1536]{1,0:T(8,128)(2,1)S(1)} %pad_maximum_fusion.1.refs_1_.refs_6_), channel_id=1, source_target_pairs={{0,16},{4,20},{8,24},{12,28},{16,0},{20,4},{24,8},{28,12},{1,17},{... | collective-permute-start | bytes 3538952 | tf_op jit(solution)/shard_map/ppermute | solution.py:310
  14.0 37.8 %copy-start.2 = (bf16[1536,192]{0,1:T(8,128)(2,1)S(1)}, bf16[1536,192]{0,1:T(8,128)(2,1)}, u32[]{:S(2)}) copy-start(bf16[1536,192]{0,1:T(8,128)(2,1)} %param.17) | copy-start | bytes 1769476
  14.0 37.8 %copy-start.3 = (bf16[192,1536]{1,0:T(8,128)(2,1)S(1)}, bf16[192,1536]{1,0:T(8,128)(2,1)}, u32[]{:S(2)}) copy-start(bf16[192,1536]{1,0:T(8,128)(2,1)} %param.15) | copy-start | bytes 1769476
  18.5 12.0 %collective-permute-start.1 = (bf16[4,128,384]{2,1,0:T(8,128)(2,1)S(1)}, bf16[4,128,384]{2,1,0:T(8,128)(2,1)S(1)}, u32[]{:S(2)}, u32[]{:S(2)}) collective-permute-start(bf16[4,128,384]{2,1,0:T(8,128)(2,1)S(1)} %depthwise.2), channel_id=1, source_target_pairs={{0,1},{1,0},{2,3},{3,2},{4,5},{5,4},{6,7},{7,6},{8,9},{9,8},{10,11... | collective-permute-start | bytes 1179656 | tf_op jit(solution)/shard_map/ppermute | solution.py:286
  19.0 14.9 %collective-permute-start.2 = (bf16[4,128,384]{2,1,0:T(8,128)(2,1)S(1)}, bf16[4,128,384]{2,1,0:T(8,128)(2,1)S(1)}, u32[]{:S(2)}, u32[]{:S(2)}) collective-permute-start(bf16[4,128,384]{2,1,0:T(8,128)(2,1)S(1)} %depthwise.2), channel_id=1, source_target_pairs={{1,2},{2,1},{5,6},{6,5},{9,10},{10,9},{13,14},{14,13},{17,18},{18,... | collective-permute-start | bytes 1179656 | tf_op jit(solution)/shard_map/ppermute | solution.py:290
  30.5 12.9 %collective-permute-start.4 = (bf16[4,128,384]{2,1,0:T(8,128)(2,1)S(1)}, bf16[4,128,384]{2,1,0:T(8,128)(2,1)S(1)}, u32[]{:S(2)}, u32[]{:S(2)}) collective-permute-start(bf16[4,128,384]{2,1,0:T(8,128)(2,1)S(1)} %collective-permute-done.1), channel_id=1, source_target_pairs={{1,2},{2,1},{5,6},{6,5},{9,10},{10,9},{13,14},{14,13},{17,18},{18,... | collective-permute-start | bytes 1179656 | tf_op jit(solution)/shard_map/ppermute | solution.py:290
  33.9 10.8 %collective-permute-start.3 = (bf16[4,128,384]{2,1,0:T(8,128)(2,1)S(1)}, bf16[4,128,384]{2,1,0:T(8,128)(2,1)S(1)}, u32[]{:S(2)}, u32[]{:S(2)}) collective-permute-start(bf16[4,128,384]{2,1,0:T(8,128)(2,1)S(1)} %collective-permute-done.2), channel_id=1, source_target_pairs={{1,0},{2,3},{5,4},{6,7},{9,8},{10,11},{13,12},{14,15},{17,16},{18,... | collective-permute-start | bytes 1179656 | tf_op jit(solution)/shard_map/ppermute | solution.py:294
  43.4 10.8 %collective-permute-start.5 = (bf16[4,128,384]{2,1,0:T(8,128)(2,1)S(1)}, bf16[4,128,384]{2,1,0:T(8,128)(2,1)S(1)}, u32[]{:S(2)}, u32[]{:S(2)}) collective-permute-start(bf16[4,128,384]{2,1,0:T(8,128)(2,1)S(1)} %collective-permute-done.4), channel_id=1, source_target_pairs={{1,0},{2,3},{5,4},{6,7},{9,8},{10,11},{13,12},{14,15},{17,16},{18,... | collective-permute-start | bytes 1179656 | tf_op jit(solution)/shard_map/ppermute | solution.py:294
  44.7 16.4 %collective-permute-start.11 = (bf16[4,128,384]{2,1,0:T(8,128)(2,1)S(1)}, bf16[4,128,384]{2,1,0:T(8,128)(2,1)S(1)}, u32[]{:S(2)}, u32[]{:S(2)}) collective-permute-start(bf16[4,128,384]{2,1,0:T(8,128)(2,1)S(1)} %depthwise.3), channel_id=1, source_target_pairs={{0,1},{1,0},{2,3},{3,2},{4,5},{5,4},{6,7},{7,6},{8,9},{9,8},{10,11... | collective-permute-start | bytes 1179656 | tf_op jit(solution)/shard_map/ppermute | solution.py:286
  46.3 14.8 %collective-permute-start.12 = (bf16[4,128,384]{2,1,0:T(8,128)(2,1)S(1)}, bf16[4,128,384]{2,1,0:T(8,128)(2,1)S(1)}, u32[]{:S(2)}, u32[]{:S(2)}) collective-permute-start(bf16[4,128,384]{2,1,0:T(8,128)(2,1)S(1)} %depthwise.3), channel_id=1, source_target_pairs={{1,2},{2,1},{5,6},{6,5},{9,10},{10,9},{13,14},{14,13},{17,18},{18,... | collective-permute-start | bytes 1179656 | tf_op jit(solution)/shard_map/ppermute | solution.py:290
  49.6 14.5 %collective-permute-start.9 = (bf16[192,1536]{1,0:T(8,128)(2,1)S(1)}, bf16[192,1536]{1,0:T(8,128)(2,1)S(1)}, u32[]{:S(2)}, u32[]{:S(2)}) collective-permute-start(bf16[192,1536]{1,0:T(8,128)(2,1)S(1)} %slice.21), channel_id=1, source_target_pairs={{0,16},{4,20},{8,24},{12,28},{16,0},{20,4},{24,8},{28,12},{1,17},{... | collective-permute-start | bytes 1769480 | tf_op jit(solution)/shard_map/ppermute | solution.py:310
  51.2 14.4 %collective-permute-start.10 = (bf16[192,1536]{1,0:T(8,128)(2,1)S(1)}, bf16[192,1536]{1,0:T(8,128)(2,1)S(1)}, u32[]{:S(2)}, u32[]{:S(2)}) collective-permute-start(bf16[192,1536]{1,0:T(8,128)(2,1)S(1)} %slice.22), channel_id=1, source_target_pairs={{0,8},{4,12},{8,0},{12,4},{16,24},{20,28},{24,16},{28,20},{1,9},{5... | collective-permute-start | bytes 1769480 | tf_op jit(solution)/shard_map/ppermute | solution.py:310
  65.6 7.9 %collective-permute-start.13 = (bf16[1152,1536]{1,0:T(8,128)(2,1)S(1)}, bf16[1152,1536]{1,0:T(8,128)(2,1)S(1)}, u32[]{:S(2)}, u32[]{:S(2)}) collective-permute-start(bf16[1152,1536]{1,0:T(8,128)(2,1)S(1)} %pad_maximum_fusion), channel_id=1, source_target_pairs={{0,4},{4,0},{8,12},{12,8},{16,20},{20,16},{24,28},{28,24},{1,5},{5... | collective-permute-start | bytes 10616840 | tf_op jit(solution)/shard_map/ppermute | solution.py:310
  65.7 7.8 %collective-permute-start.14 = (bf16[384,1536]{1,0:T(8,128)(2,1)S(1)}, bf16[384,1536]{1,0:T(8,128)(2,1)S(1)}, u32[]{:S(2)}, u32[]{:S(2)}) collective-permute-start(bf16[384,1536]{1,0:T(8,128)(2,1)S(1)} %pad_maximum_fusion.2), channel_id=1, source_target_pairs={{0,4},{4,0},{8,12},{12,8},{16,20},{20,16},{24,28},{28,24},{1,5},{5... | collective-permute-start | bytes 3538952 | tf_op jit(solution)/shard_map/ppermute | solution.py:310
  67.6 18.2 %collective-permute-start.16 = (bf16[4,128,384]{2,1,0:T(8,128)(2,1)S(1)}, bf16[4,128,384]{2,1,0:T(8,128)(2,1)S(1)}, u32[]{:S(2)}, u32[]{:S(2)}) collective-permute-start(bf16[4,128,384]{2,1,0:T(8,128)(2,1)S(1)} %collective-permute-done.12), channel_id=1, source_target_pairs={{1,0},{2,3},{5,4},{6,7},{9,8},{10,11},{13,12},{14,15},{17,16},{18,... | collective-permute-start | bytes 1179656 | tf_op jit(solution)/shard_map/ppermute | solution.py:294
  68.9 12.9 %collective-permute-start.17 = (bf16[4,128,384]{2,1,0:T(8,128)(2,1)S(1)}, bf16[4,128,384]{2,1,0:T(8,128)(2,1)S(1)}, u32[]{:S(2)}, u32[]{:S(2)}) collective-permute-start(bf16[4,128,384]{2,1,0:T(8,128)(2,1)S(1)} %collective-permute-done.11), channel_id=1, source_target_pairs={{1,2},{2,1},{5,6},{6,5},{9,10},{10,9},{13,14},{14,13},{17,18},{18,... | collective-permute-start | bytes 1179656 | tf_op jit(solution)/shard_map/ppermute | solution.py:290
  81.8 9.4 %collective-permute-start.18 = (bf16[4,128,384]{2,1,0:T(8,128)(2,1)S(1)}, bf16[4,128,384]{2,1,0:T(8,128)(2,1)S(1)}, u32[]{:S(2)}, u32[]{:S(2)}) collective-permute-start(bf16[4,128,384]{2,1,0:T(8,128)(2,1)S(1)} %collective-permute-done.17), channel_id=1, source_target_pairs={{1,0},{2,3},{5,4},{6,7},{9,8},{10,11},{13,12},{14,15},{17,16},{18,... | collective-permute-start | bytes 1179656 | tf_op jit(solution)/shard_map/ppermute | solution.py:294
  83.1 18.3 %collective-permute-start.21 = (bf16[4,384,128]{2,1,0:T(8,128)(2,1)S(1)}, bf16[4,384,128]{2,1,0:T(8,128)(2,1)S(1)}, u32[]{:S(2)}, u32[]{:S(2)}) collective-permute-start(bf16[4,384,128]{2,1,0:T(8,128)(2,1)S(1)} %get-tuple-element.33), channel_id=1, source_target_pairs={{0,1},{3,2},{4,5},{7,6},{8,9},{11,10},{12,13},{15,14},{16,17},{19,... | collective-permute-start | bytes 1179656 | tf_op jit(solution)/shard_map/ppermute | solution.py:298
  84.4 20.6 %collective-permute-start.15 = (bf16[4,384,128]{2,1,0:T(8,128)(2,1)S(1)}, bf16[4,384,128]{2,1,0:T(8,128)(2,1)S(1)}, u32[]{:S(2)}, u32[]{:S(2)}) collective-permute-start(bf16[4,384,128]{2,1,0:T(8,128)(2,1)S(1)} %get-tuple-element.30), channel_id=1, source_target_pairs={{0,1},{3,2},{4,5},{7,6},{8,9},{11,10},{12,13},{15,14},{16,17},{19,... | collective-permute-start | bytes 1179656 | tf_op jit(solution)/shard_map/ppermute | solution.py:298
  100.1 13.9 %collective-permute-start.19 = (bf16[4,384,128]{2,1,0:T(8,128)(2,1)S(1)}, bf16[4,384,128]{2,1,0:T(8,128)(2,1)S(1)}, u32[]{:S(2)}, u32[]{:S(2)}) collective-permute-start(bf16[4,384,128]{2,1,0:T(8,128)(2,1)S(1)} %get-tuple-element.35), channel_id=1, source_target_pairs={{0,1},{3,2},{4,5},{7,6},{8,9},{11,10},{12,13},{15,14},{16,17},{19,... | collective-permute-start | bytes 1179656 | tf_op jit(solution)/shard_map/ppermute | solution.py:298
  101.5 14.8 %collective-permute-start.22 = (bf16[4,384,128]{2,1,0:T(8,128)(2,1)S(1)}, bf16[4,384,128]{2,1,0:T(8,128)(2,1)S(1)}, u32[]{:S(2)}, u32[]{:S(2)}) collective-permute-start(bf16[4,384,128]{2,1,0:T(8,128)(2,1)S(1)} %add_convert_fusion.5), channel_id=1, source_target_pairs={{1,2},{2,1},{5,6},{6,5},{9,10},{10,9},{13,14},{14,13},{17,18},{18,... | collective-permute-start | bytes 1179656 | tf_op jit(solution)/shard_map/ppermute | solution.py:290
  103.7 18.7 %collective-permute-start.24 = (bf16[4,384,128]{2,1,0:T(8,128)(2,1)S(1)}, bf16[4,384,128]{2,1,0:T(8,128)(2,1)S(1)}, u32[]{:S(2)}, u32[]{:S(2)}) collective-permute-start(bf16[4,384,128]{2,1,0:T(8,128)(2,1)S(1)} %get-tuple-element.39), channel_id=1, source_target_pairs={{0,1},{3,2},{4,5},{7,6},{8,9},{11,10},{12,13},{15,14},{16,17},{19,... | collective-permute-start | bytes 1179656 | tf_op jit(solution)/shard_map/ppermute | solution.py:298
  105.2 35.2 %copy-start.7 = (f32[384]{0:T(512)S(1)}, f32[384]{0:T(512)}, u32[]{:S(2)}) copy-start(f32[384]{0:T(512)} %param.18) | copy-start | bytes 4612
  105.2 35.2 %copy-start.8 = (f32[384]{0:T(512)S(1)}, f32[384]{0:T(512)}, u32[]{:S(2)}) copy-start(f32[384]{0:T(512)} %param.19) | copy-start | bytes 4612
  114.2 13.9 %collective-permute-start.26 = (bf16[4,384,128]{2,1,0:T(8,128)(2,1)S(1)}, bf16[4,384,128]{2,1,0:T(8,128)(2,1)S(1)}, u32[]{:S(2)}, u32[]{:S(2)}) collective-permute-start(bf16[4,384,128]{2,1,0:T(8,128)(2,1)S(1)} %add_convert_fusion.6), channel_id=1, source_target_pairs={{1,2},{2,1},{5,6},{6,5},{9,10},{10,9},{13,14},{14,13},{17,18},{18,... | collective-permute-start | bytes 1179656 | tf_op jit(solution)/shard_map/ppermute | solution.py:290
  117.2 13.7 %collective-permute-start.23 = (bf16[4,384,128]{2,1,0:T(8,128)(2,1)}, bf16[4,384,128]{2,1,0:T(8,128)(2,1)S(1)}, u32[]{:S(2)}, u32[]{:S(2)}) collective-permute-start(bf16[4,384,128]{2,1,0:T(8,128)(2,1)} %add_convert_fusion.4), channel_id=1, source_target_pairs={{0,1},{1,0},{2,3},{3,2},{4,5},{5,4},{6,7},{7,6},{8,9},{9,8},{10,11... | collective-permute-start | bytes 1179656 | tf_op jit(solution)/shard_map/ppermute | solution.py:286
  117.2 18.9 %collective-permute-start.20 = (bf16[4,384,128]{2,1,0:T(8,128)(2,1)S(1)}, bf16[4,384,128]{2,1,0:T(8,128)(2,1)S(1)}, u32[]{:S(2)}, u32[]{:S(2)}) collective-permute-start(bf16[4,384,128]{2,1,0:T(8,128)(2,1)S(1)} %add_convert_fusion.7), channel_id=1, source_target_pairs={{1,2},{2,1},{5,6},{6,5},{9,10},{10,9},{13,14},{14,13},{17,18},{18,... | collective-permute-start | bytes 1179656 | tf_op jit(solution)/shard_map/ppermute | solution.py:290
  123.3 17.0 %collective-permute-start.25 = (bf16[4,384,128]{2,1,0:T(8,128)(2,1)}, bf16[4,384,128]{2,1,0:T(8,128)(2,1)S(1)}, u32[]{:S(2)}, u32[]{:S(2)}) collective-permute-start(bf16[4,384,128]{2,1,0:T(8,128)(2,1)} %add_convert_fusion.2), channel_id=1, source_target_pairs={{1,2},{2,1},{5,6},{6,5},{9,10},{10,9},{13,14},{14,13},{17,18},{18,... | collective-permute-start | bytes 1179656 | tf_op jit(solution)/shard_map/ppermute | solution.py:290
  129.0 11.4 %collective-permute-start.27 = (bf16[4,384,128]{2,1,0:T(8,128)(2,1)}, bf16[4,384,128]{2,1,0:T(8,128)(2,1)S(1)}, u32[]{:S(2)}, u32[]{:S(2)}) collective-permute-start(bf16[4,384,128]{2,1,0:T(8,128)(2,1)} %add_convert_fusion.1), channel_id=1, source_target_pairs={{0,1},{1,0},{2,3},{3,2},{4,5},{5,4},{6,7},{7,6},{8,9},{9,8},{10,11... | collective-permute-start | bytes 1179656 | tf_op jit(solution)/shard_map/ppermute | solution.py:286
  (6 other events, 84.5 us)

commit v6 on v5

--- a/solution.py
+++ b/solution.py
@@ -159,10 +159,10 @@
         hidden[:, f : f + block] = gelu.astype(hidden.dtype)
 
 
-def project(hidden, w_out, out_refs):
+def project(hidden, w_out, out_refs, which=slice(None)):
     z = lax.axis_index("chan")
     pair, mid, far = line_places(z)
-    for out_ref, place in zip(out_refs, (far, mid, pair, z), strict=True):
+    for out_ref, place in zip(out_refs, (far, mid, pair, z)[which], strict=True):
         rows, slab, width = out_ref.shape
         at = pl.ds(pl.multiple_of(place * slab, 16), slab)
         partial = lax.dot_general(
@@ -190,9 +190,9 @@
     return wait
 
 
-def mlp_kernel(*refs):
-    normed_ref, parts, b_in_ref, out_refs = refs[0], refs[1:8], refs[8], refs[9:13]
-    w_in, w_out, hidden, in_sem, out_sem = refs[13:]
+def first_kernel(*refs):
+    normed_ref, parts, b_in_ref, hidden, out_ref = refs[0], refs[1:8], refs[8], refs[9], refs[10]
+    w_in, w_out, in_sem, out_sem = refs[11:]
     shard = parts[0].shape[0] // 2
     ins, outs = weight_pieces(parts, shard)
     w_in_there = start_shards(ins, w_in, shard, in_sem)
@@ -200,7 +200,49 @@
     w_in_there()
     lift(normed_ref, w_in, b_in_ref, hidden)
     w_out_there()
-    project(hidden, w_out, out_refs)
+    project(hidden, w_out, [out_ref], slice(0, 1))
+
+
+def rest_kernel(*refs):
+    hidden, parts, out_refs = refs[0], refs[1:8], refs[8:11]
+    w_out, out_sem = refs[11:]
+    shard = parts[0].shape[0] // 2
+    start_shards(weight_pieces(parts, shard)[1], w_out, shard, out_sem)()
+    project(hidden, w_out, out_refs, slice(1, 4))
+
+
+def split_mlp(x, weights, rows, b_in):
+    pixels, channels = x.shape
+    slab, width, units = channels // 4, pixels // rows, weights[0].shape[1]
+    part = jax.ShapeDtypeStruct((rows, slab, width), jnp.bfloat16)
+    matrix = pltpu.VMEM((channels, units), jnp.bfloat16)
+    sems = pltpu.SemaphoreType.DMA((SHARDS,))
+    params = pltpu.CompilerParams(vmem_limit_bytes=MLP_LIMIT)
+    hidden, far = pl.pallas_call(
+        first_kernel,
+        in_specs=[WHOLE] + [ANYWHERE] * len(weights) + [WHOLE],
+        out_specs=[WHOLE] * 2,
+        out_shape=[jax.ShapeDtypeStruct((pixels, units), jnp.bfloat16), part],
+        scratch_shapes=[matrix, matrix, sems, sems],
+        compiler_params=params,
+        cost_estimate=pl.CostEstimate(
+            flops=3 * pixels * channels * units, bytes_accessed=4 * channels * units, transcendentals=0
+        ),
+        name="mlp_first",
+    )(x, *weights, b_in[None])
+    mid, pair, home = pl.pallas_call(
+        rest_kernel,
+        in_specs=[WHOLE] + [ANYWHERE] * len(weights),
+        out_specs=[WHOLE] * 3,
+        out_shape=[part] * 3,
+        scratch_shapes=[matrix, sems],
+        compiler_params=params,
+        cost_estimate=pl.CostEstimate(
+            flops=2 * pixels * channels * units, bytes_accessed=2 * channels * units, transcendentals=0
+        ),
+        name="mlp_rest",
+    )(hidden, *weights)
+    return far, mid, pair, home
 
 
 def norm_mlp_kernel(*refs):
@@ -244,34 +286,24 @@
     )(*[s.reshape(pixels, slab) for s in slabs], gain[None], shift[None])
 
 
-def mlp_chunk(x, weights, rows, gain, shift, b_in):
-    normed = not isinstance(x, list)
-    if normed:
-        pixels, channels = x.shape
-        slab, width = channels // 4, pixels // rows
-        inputs, vectors = [x], [b_in[None]]
-        kernel, scratch = mlp_kernel, []
-        specs = [WHOLE]
-    else:
-        _, width, slab = x[0].shape
-        pixels, channels = rows * width, 4 * slab
-        inputs, vectors = [s.reshape(pixels, slab) for s in x], [gain[None], shift[None], b_in[None]]
-        kernel, scratch = norm_mlp_kernel, [pltpu.VMEM((pixels, channels), jnp.bfloat16)]
-        specs = [ANYWHERE] * 6
+def mlp_chunk(slabs, weights, rows, gain, shift, b_in):
+    _, width, slab = slabs[0].shape
+    pixels, channels = rows * width, 4 * slab
     units = weights[0].shape[1]
     return pl.pallas_call(
-        kernel,
-        in_specs=specs + [ANYWHERE] * len(weights) + [WHOLE] * len(vectors),
+        norm_mlp_kernel,
+        in_specs=[ANYWHERE] * (len(slabs) + len(weights)) + [WHOLE] * 3,
         out_specs=[WHOLE] * 4,
         out_shape=[jax.ShapeDtypeStruct((rows, slab, width), jnp.bfloat16)] * 4,
-        scratch_shapes=scratch
-        + [
+        scratch_shapes=[
+            pltpu.VMEM((pixels, channels), jnp.bfloat16),
             pltpu.VMEM((channels, units), jnp.bfloat16),
             pltpu.VMEM((channels, units), jnp.bfloat16),
             pltpu.VMEM((pixels, units), jnp.bfloat16),
-        ]
-        + ([] if normed else [pltpu.SemaphoreType.DMA((4,))])
-        + [pltpu.SemaphoreType.DMA((SHARDS,)), pltpu.SemaphoreType.DMA((SHARDS,))],
+            pltpu.SemaphoreType.DMA((4,)),
+            pltpu.SemaphoreType.DMA((SHARDS,)),
+            pltpu.SemaphoreType.DMA((SHARDS,)),
+        ],
         compiler_params=pltpu.CompilerParams(vmem_limit_bytes=MLP_LIMIT),
         cost_estimate=pl.CostEstimate(
             flops=4 * pixels * channels * units,
@@ -279,7 +311,13 @@
             transcendentals=pixels * units,
         ),
         name="mlp",
-    )(*inputs, *weights, *vectors)
+    )(
+        *[s.reshape(pixels, slab) for s in slabs],
+        *weights,
+        gain[None],
+        shift[None],
+        b_in[None],
+    )
 
 
 def to_pair(array):
@@ -349,7 +387,7 @@
 
     line_0 = [slab_0, near_0, mid_in_0, mid_out_0, far_in_0, far_out_0]
     normed_0 = norm_chunk(line_0, ln_gain, ln_bias)
-    far_0, mid_0, pair_0, home_0 = mlp(normed_0, weights)
+    far_0, mid_0, pair_0, home_0 = split_mlp(normed_0, weights, rows, b_in)
     far_out_1 = outward(after(far_in_1, far_0))
     far_sum_0, mid_from_0 = add(far_0, inward(far_0)), inward(mid_0)
 

time: 142 us -> 142 us (level)
  waiting for transfers between devices: 59.3 us -> 57.2 us
    ppermute x4, waiting for transfers between devices: 7.54 us -> 5.24 us  [outward(): return lax.ppermute(array, 'chan', [(1, 0), (2, 3)])]
    pallas_call x2 -> x3, Pallas kernels: 16.3 us -> 17.7 us  [the longest x1 8.87 us: mlp_chunk(): pl.pallas_call(norm_mlp_kernel, in_specs=[ANYWHERE] * (len(slabs) + len(w...]
  transfers between devices with their start and end apart: 28 -> 28, of which waited for: 16 -> 15; matrix products, arithmetic and copies ran while one was open for 3% -> 3% of each run, Pallas kernels for 19% -> 20%
where the time goes in v6:
time: 142 us; the launch traced here: 141 us
  waiting for transfers between devices  57.2 us (40%)
  starting transfers between devices  48.4 us (34%)
  Pallas kernels  27.8 us (20%)
  other arithmetic  6 us (4%)
    ppermute x8, starting transfers between devices, to_middle(): return lax.ppermute(array, 'chan', [(1, 2), (2, 1)])  23.8 us
    ppermute x8, waiting for transfers between devices, to_middle(): return lax.ppermute(array, 'chan', [(1, 2), (2, 1)])  16.8 us
    ppermute x4, waiting for transfers between devices, to_pair(): return lax.ppermute(array, 'chan', [(0, 1), (1, 0), (2, 3), (3, 2)])  15.6 us
    ppermute x4, waiting for transfers between devices, inward(): return lax.ppermute(array, 'chan', [(0, 1), (3, 2)])  10.4 us
    ppermute x6, starting transfers between devices, flipped(): return lax.ppermute(array, 'tile', [(i, i ^ bit) for i in range(8)])  9.1 us
    pallas_call x2, Pallas kernels, conv_chunk(): pl.pallas_call(functools.partial(conv_kernel, tuple(plan)), grid=(slab //...  8.89 us
    pallas_call x1, Pallas kernels, mlp_chunk(): pl.pallas_call(norm_mlp_kernel, in_specs=[ANYWHERE] * (len(slabs) + len(w...  8.87 us
    ppermute x6, waiting for transfers between devices, flipped(): return lax.ppermute(array, 'tile', [(i, i ^ bit) for i in range(8)])  6.94 us
  transfers between devices with their start and end apart: 28, of which 15 were waited for; matrix products, arithmetic and copies ran while one was open for 3% of the time, Pallas kernels for 20%

profile of v6, /device:TPU:8, one launch (start us, length us, event | category | flops | bytes accessed | tf_op | source)
XLA Modules:
  0.0 141.1 jit_solution(1677204148041158964)
XLA Ops:
  1.2 1.8 %collective-permute-start = (bf16[3,384,128]{2,1,0:T(8,128)(2,1)S(1)}, bf16[3,384,128]{2,1,0:T(8,128)(2,1)S(1)}, u32[]{:S(2)}, u32[]{:S(2)}) collective-permute-start(bf16[3,384,128]{2,1,0:T(8,128)(2,1)S(1)} %get-tuple-element.45), channel_id=1, source_target_pairs={{0,4},{4,8},{8,12},{12,16},{16,20},{20,24},{24,28},{1,5},{5,9},{9,... | collective-permute-start | bytes 884744 | tf_op jit(solution)/shard_map/ppermute | solution.py:355
  5.6 2.1 %collective-permute-done.6.refs_1_ = bf16[3,384,128]{2,1,0:T(8,128)(2,1)S(1)} collective-permute-done((bf16[3,384,128]{2,1,0:T(8,128)(2,1)S(1)}, bf16[3,384,128]{2,1,0:T(8,128)(2,1)S(1)}, u32[]{:S(2)}, u32[]{:S(2)}) %collective-permute-start.6) | collective-permute-done | bytes 294944 | tf_op jit(solution)/shard_map/ppermute | solution.py:355
  7.7 5.2 %collective-permute-start.7 = (bf16[384,1536]{1,0:T(8,128)(2,1)S(1)}, bf16[384,1536]{1,0:T(8,128)(2,1)S(1)}, u32[]{:S(2)}, u32[]{:S(2)}) collective-permute-start(bf16[384,1536]{1,0:T(8,128)(2,1)S(1)} %pad_maximum_fusion.1.refs_1_.refs_6_), channel_id=1, source_target_pairs={{0,8},{4,12},{8,0},{12,4},{16,24},{20,28},{24,16},{28,20},{1,9},{5... | collective-permute-start | bytes 3538952 | tf_op jit(solution)/shard_map/ppermute | solution.py:348
  14.0 4.4 %depthwise.2 = bf16[4,128,384]{2,1,0:T(8,128)(2,1)S(1)} custom-call(bf16[8,384,128]{2,1,0:T(8,128)(2,1)S(1)} %copy-done, bf16[3,384,128]{2,1,0:T(8,128)(2,1)S(1)} %collective-permute-done.refs_1_, f32[49,384]{1,0:T(8,128)S(1)} %bitcast.16, f32[1,384]{1,0:T(1,128)S(1)} %broadcast_in_dim.8.refs_3_), custom_call_target="tpu_custom_call" | custom-call | flops 19267584 | bytes 786432 | tf_op jit(solution)/shard_map/depthwise/pallas_call | solution.py:63
  19.0 4.6 %collective-permute-start.2 = (bf16[4,128,384]{2,1,0:T(8,128)(2,1)S(1)}, bf16[4,128,384]{2,1,0:T(8,128)(2,1)S(1)}, u32[]{:S(2)}, u32[]{:S(2)}) collective-permute-start(bf16[4,128,384]{2,1,0:T(8,128)(2,1)S(1)} %depthwise.2), channel_id=1, source_target_pairs={{1,2},{2,1},{5,6},{6,5},{9,10},{10,9},{13,14},{14,13},{17,18},{18,... | collective-permute-start | bytes 1179656 | tf_op jit(solution)/shard_map/ppermute | solution.py:328
  23.6 6.8 %collective-permute-done.1 = bf16[4,128,384]{2,1,0:T(8,128)(2,1)S(1)} collective-permute-done((bf16[4,128,384]{2,1,0:T(8,128)(2,1)S(1)}, bf16[4,128,384]{2,1,0:T(8,128)(2,1)S(1)}, u32[]{:S(2)}, u32[]{:S(2)}) %collective-permute-start.1) | collective-permute-done | bytes 393248 | tf_op jit(solution)/shard_map/ppermute | solution.py:324
  30.5 3.5 %collective-permute-start.4 = (bf16[4,128,384]{2,1,0:T(8,128)(2,1)S(1)}, bf16[4,128,384]{2,1,0:T(8,128)(2,1)S(1)}, u32[]{:S(2)}, u32[]{:S(2)}) collective-permute-start(bf16[4,128,384]{2,1,0:T(8,128)(2,1)S(1)} %collective-permute-done.1), channel_id=1, source_target_pairs={{1,2},{2,1},{5,6},{6,5},{9,10},{10,9},{13,14},{14,13},{17,18},{18,... | collective-permute-start | bytes 1179656 | tf_op jit(solution)/shard_map/ppermute | solution.py:328
  35.3 4.4 %depthwise.3 = bf16[4,128,384]{2,1,0:T(8,128)(2,1)S(1)} custom-call(bf16[8,384,128]{2,1,0:T(8,128)(2,1)S(1)} %copy-done, bf16[3,384,128]{2,1,0:T(8,128)(2,1)S(1)} %collective-permute-done.6.refs_1_, f32[49,384]{1,0:T(8,128)S(1)} %bitcast.17, f32[1,384]{1,0:T(1,128)S(1)} %broadcast_in_dim.8.refs_3_), custom_call_target="tpu_custom_call" | custom-call | flops 19267584 | bytes 786432 | tf_op jit(solution)/shard_map/depthwise/pallas_call | solution.py:63
  39.7 3.7 %collective-permute-done.4 = bf16[4,128,384]{2,1,0:T(8,128)(2,1)S(1)} collective-permute-done((bf16[4,128,384]{2,1,0:T(8,128)(2,1)S(1)}, bf16[4,128,384]{2,1,0:T(8,128)(2,1)S(1)}, u32[]{:S(2)}, u32[]{:S(2)}) %collective-permute-start.4) | collective-permute-done | bytes 393248 | tf_op jit(solution)/shard_map/ppermute | solution.py:328
  44.7 1.6 %collective-permute-start.11 = (bf16[4,128,384]{2,1,0:T(8,128)(2,1)S(1)}, bf16[4,128,384]{2,1,0:T(8,128)(2,1)S(1)}, u32[]{:S(2)}, u32[]{:S(2)}) collective-permute-start(bf16[4,128,384]{2,1,0:T(8,128)(2,1)S(1)} %depthwise.3), channel_id=1, source_target_pairs={{0,1},{1,0},{2,3},{3,2},{4,5},{5,4},{6,7},{7,6},{8,9},{9,8},{10,11... | collective-permute-start | bytes 1179656 | tf_op jit(solution)/shard_map/ppermute | solution.py:324
  46.3 3.2 %collective-permute-start.12 = (bf16[4,128,384]{2,1,0:T(8,128)(2,1)S(1)}, bf16[4,128,384]{2,1,0:T(8,128)(2,1)S(1)}, u32[]{:S(2)}, u32[]{:S(2)}) collective-permute-start(bf16[4,128,384]{2,1,0:T(8,128)(2,1)S(1)} %depthwise.3), channel_id=1, source_target_pairs={{1,2},{2,1},{5,6},{6,5},{9,10},{10,9},{13,14},{14,13},{17,18},{18,... | collective-permute-start | bytes 1179656 | tf_op jit(solution)/shard_map/ppermute | solution.py:328
  49.6 1.6 %collective-permute-start.9 = (bf16[192,1536]{1,0:T(8,128)(2,1)S(1)}, bf16[192,1536]{1,0:T(8,128)(2,1)S(1)}, u32[]{:S(2)}, u32[]{:S(2)}) collective-permute-start(bf16[192,1536]{1,0:T(8,128)(2,1)S(1)} %slice.21), channel_id=1, source_target_pairs={{0,16},{4,20},{8,24},{12,28},{16,0},{20,4},{24,8},{28,12},{1,17},{... | collective-permute-start | bytes 1769480 | tf_op jit(solution)/shard_map/ppermute | solution.py:348
  52.1 2.1 %collective-permute-done.5 = bf16[4,128,384]{2,1,0:T(8,128)(2,1)S(1)} collective-permute-done((bf16[4,128,384]{2,1,0:T(8,128)(2,1)S(1)}, bf16[4,128,384]{2,1,0:T(8,128)(2,1)S(1)}, u32[]{:S(2)}, u32[]{:S(2)}) %collective-permute-start.5) | collective-permute-done | bytes 393248 | tf_op jit(solution)/shard_map/ppermute | solution.py:332
  54.2 6.9 %collective-permute-done.11 = bf16[4,128,384]{2,1,0:T(8,128)(2,1)S(1)} collective-permute-done((bf16[4,128,384]{2,1,0:T(8,128)(2,1)S(1)}, bf16[4,128,384]{2,1,0:T(8,128)(2,1)S(1)}, u32[]{:S(2)}, u32[]{:S(2)}) %collective-permute-start.11) | collective-permute-done | bytes 393248 | tf_op jit(solution)/shard_map/ppermute | solution.py:324
  61.1 3.0 %collective-permute-done.9.refs_4_.refs_9_ = bf16[192,1536]{1,0:T(8,128)(2,1)S(1)} collective-permute-done((bf16[192,1536]{1,0:T(8,128)(2,1)S(1)}, bf16[192,1536]{1,0:T(8,128)(2,1)S(1)}, u32[]{:S(2)}, u32[]{:S(2)}) %collective-permute-start.9) | collective-permute-done | bytes 589856 | tf_op jit(solution)/shard_map/ppermute | solution.py:348
  64.0 1.6 %collective-permute-done.10.refs_5_.refs_10_ = bf16[192,1536]{1,0:T(8,128)(2,1)S(1)} collective-permute-done((bf16[192,1536]{1,0:T(8,128)(2,1)S(1)}, bf16[192,1536]{1,0:T(8,128)(2,1)S(1)}, u32[]{:S(2)}, u32[]{:S(2)}) %collective-permute-start.10) | collective-permute-done | bytes 589856 | tf_op jit(solution)/shard_map/ppermute | solution.py:348
  66.3 2.2 %collective-permute-start.17 = (bf16[4,128,384]{2,1,0:T(8,128)(2,1)S(1)}, bf16[4,128,384]{2,1,0:T(8,128)(2,1)S(1)}, u32[]{:S(2)}, u32[]{:S(2)}) collective-permute-start(bf16[4,128,384]{2,1,0:T(8,128)(2,1)S(1)} %collective-permute-done.11), channel_id=1, source_target_pairs={{1,2},{2,1},{5,6},{6,5},{9,10},{10,9},{13,14},{14,13},{17,18},{18,... | collective-permute-start | bytes 1179656 | tf_op jit(solution)/shard_map/ppermute | solution.py:328
  71.1 2.4 %collective-permute-done.14.refs_7_.refs_12_ = bf16[384,1536]{1,0:T(8,128)(2,1)S(1)} collective-permute-done((bf16[384,1536]{1,0:T(8,128)(2,1)S(1)}, bf16[384,1536]{1,0:T(8,128)(2,1)S(1)}, u32[]{:S(2)}, u32[]{:S(2)}) %collective-permute-start.14) | collective-permute-done | bytes 1179680 | tf_op jit(solution)/shard_map/ppermute | solution.py:348
  73.5 5.7 %mlp_first.1 = (bf16[512,1536]{1,0:T(8,128)(2,1)S(1)}, bf16[4,384,128]{2,1,0:T(8,128)(2,1)S(1)}) custom-call(bf16[512,1536]{1,0:T(8,128)(2,1)S(1)} %norm.1.refs_0_, bf16[384,1536]{1,0:T(8,128)(2,1)S(1)} %pad_maximum_fusion.1.refs_1_.refs_6_, bf16[384,1536]{1,0:T(8,128)(2,1)S(1)} %collective-permute-done.7.refs_2_.refs_7_, ...), custom_call_target="tpu_custom_call" | custom-call | flops 3623878656 | bytes 9437184 | tf_op jit(solution)/shard_map/mlp_first/pallas_call | solution.py:221
  81.9 3.1 %mlp_rest.1 = (bf16[4,384,128]{2,1,0:T(8,128)(2,1)S(1)}, bf16[4,384,128]{2,1,0:T(8,128)(2,1)S(1)}, bf16[4,384,128]{2,1,0:T(8,128)(2,1)S(1)}) custom-call(bf16[512,1536]{1,0:T(8,128)(2,1)S(1)} %get-tuple-element.30.refs_0_, bf16[384,1536]{1,0:T(8,128)(2,1)S(1)} %pad_maximum_fusion.1.refs_1_.refs_6_, ...), custom_call_target="tpu_custom_call" | custom-call | flops 2415919104 | bytes 4718592 | tf_op jit(solution)/shard_map/mlp_rest/pallas_call | solution.py:233
  86.3 3.2 %collective-permute-done.18 = bf16[4,128,384]{2,1,0:T(8,128)(2,1)S(1)} collective-permute-done((bf16[4,128,384]{2,1,0:T(8,128)(2,1)S(1)}, bf16[4,128,384]{2,1,0:T(8,128)(2,1)S(1)}, u32[]{:S(2)}, u32[]{:S(2)}) %collective-permute-start.18) | collective-permute-done | bytes 393248 | tf_op jit(solution)/shard_map/ppermute | solution.py:332
  89.5 8.9 %mlp.1 = (bf16[4,384,128]{2,1,0:T(8,128)(2,1)S(1)}, bf16[4,384,128]{2,1,0:T(8,128)(2,1)S(1)}, bf16[4,384,128]{2,1,0:T(8,128)(2,1)S(1)}, bf16[4,384,128]{2,1,0:T(8,128)(2,1)S(1)}) custom-call(bf16[512,384]{1,0:T(8,128)(2,1)S(1)} %bitcast.14, bf16[512,384]{1,0:T(8,128)(2,1)S(1)} %bitcast.18, bf16[512,384]{1,0:T(8,128)(2,1)S(1)} %bitcast.19, ...), custom_call_target="tpu_custom_call" | custom-call | flops 4831838208 | bytes 12582912 | tf_op jit(solution)/shard_map/mlp/pallas_call | solution.py:293
  99.8 2.2 %collective-permute-start.22 = (bf16[4,384,128]{2,1,0:T(8,128)(2,1)S(1)}, bf16[4,384,128]{2,1,0:T(8,128)(2,1)S(1)}, u32[]{:S(2)}, u32[]{:S(2)}) collective-permute-start(bf16[4,384,128]{2,1,0:T(8,128)(2,1)S(1)} %add_convert_fusion.5), channel_id=1, source_target_pairs={{1,2},{2,1},{5,6},{6,5},{9,10},{10,9},{13,14},{14,13},{17,18},{18,... | collective-permute-start | bytes 1179656 | tf_op jit(solution)/shard_map/ppermute | solution.py:328
  103.5 8.8 %collective-permute-done.19 = bf16[4,384,128]{2,1,0:T(8,128)(2,1)S(1)} collective-permute-done((bf16[4,384,128]{2,1,0:T(8,128)(2,1)S(1)}, bf16[4,384,128]{2,1,0:T(8,128)(2,1)S(1)}, u32[]{:S(2)}, u32[]{:S(2)}) %collective-permute-start.19) | collective-permute-done | bytes 393248 | tf_op jit(solution)/shard_map/ppermute | solution.py:336
  112.4 2.2 %collective-permute-start.26 = (bf16[4,384,128]{2,1,0:T(8,128)(2,1)S(1)}, bf16[4,384,128]{2,1,0:T(8,128)(2,1)S(1)}, u32[]{:S(2)}, u32[]{:S(2)}) collective-permute-start(bf16[4,384,128]{2,1,0:T(8,128)(2,1)S(1)} %add_convert_fusion.6), channel_id=1, source_target_pairs={{1,2},{2,1},{5,6},{6,5},{9,10},{10,9},{13,14},{14,13},{17,18},{18,... | collective-permute-start | bytes 1179656 | tf_op jit(solution)/shard_map/ppermute | solution.py:328
  115.5 3.6 %collective-permute-start.20 = (bf16[4,384,128]{2,1,0:T(8,128)(2,1)S(1)}, bf16[4,384,128]{2,1,0:T(8,128)(2,1)S(1)}, u32[]{:S(2)}, u32[]{:S(2)}) collective-permute-start(bf16[4,384,128]{2,1,0:T(8,128)(2,1)S(1)} %add_convert_fusion.7), channel_id=1, source_target_pairs={{1,2},{2,1},{5,6},{6,5},{9,10},{10,9},{13,14},{14,13},{17,18},{18,... | collective-permute-start | bytes 1179656 | tf_op jit(solution)/shard_map/ppermute | solution.py:328
  119.1 1.6 %collective-permute-done.24 = bf16[4,384,128]{2,1,0:T(8,128)(2,1)S(1)} collective-permute-done((bf16[4,384,128]{2,1,0:T(8,128)(2,1)S(1)}, bf16[4,384,128]{2,1,0:T(8,128)(2,1)S(1)}, u32[]{:S(2)}, u32[]{:S(2)}) %collective-permute-start.24) | collective-permute-done | bytes 393248 | tf_op jit(solution)/shard_map/ppermute | solution.py:336
  121.5 2.2 %collective-permute-start.25 = (bf16[4,384,128]{2,1,0:T(8,128)(2,1)}, bf16[4,384,128]{2,1,0:T(8,128)(2,1)S(1)}, u32[]{:S(2)}, u32[]{:S(2)}) collective-permute-start(bf16[4,384,128]{2,1,0:T(8,128)(2,1)} %add_convert_fusion.2), channel_id=1, source_target_pairs={{1,2},{2,1},{5,6},{6,5},{9,10},{10,9},{13,14},{14,13},{17,18},{18,... | collective-permute-start | bytes 1179656 | tf_op jit(solution)/shard_map/ppermute | solution.py:328
  123.8 2.5 %collective-permute-done.26 = bf16[4,384,128]{2,1,0:T(8,128)(2,1)S(1)} collective-permute-done((bf16[4,384,128]{2,1,0:T(8,128)(2,1)S(1)}, bf16[4,384,128]{2,1,0:T(8,128)(2,1)S(1)}, u32[]{:S(2)}, u32[]{:S(2)}) %collective-permute-start.26) | collective-permute-done | bytes 393248 | tf_op jit(solution)/shard_map/ppermute | solution.py:328
  127.2 1.9 %collective-permute-done.23 = bf16[4,384,128]{2,1,0:T(8,128)(2,1)S(1)} collective-permute-done((bf16[4,384,128]{2,1,0:T(8,128)(2,1)}, bf16[4,384,128]{2,1,0:T(8,128)(2,1)S(1)}, u32[]{:S(2)}, u32[]{:S(2)}) %collective-permute-start.23) | collective-permute-done | bytes 393248 | tf_op jit(solution)/shard_map/ppermute | solution.py:324
  129.1 5.6 %collective-permute-done.20 = bf16[4,384,128]{2,1,0:T(8,128)(2,1)S(1)} collective-permute-done((bf16[4,384,128]{2,1,0:T(8,128)(2,1)S(1)}, bf16[4,384,128]{2,1,0:T(8,128)(2,1)S(1)}, u32[]{:S(2)}, u32[]{:S(2)}) %collective-permute-start.20) | collective-permute-done | bytes 393248 | tf_op jit(solution)/shard_map/ppermute | solution.py:328
  134.7 4.9 %collective-permute-done.25 = bf16[4,384,128]{2,1,0:T(8,128)(2,1)S(1)} collective-permute-done((bf16[4,384,128]{2,1,0:T(8,128)(2,1)}, bf16[4,384,128]{2,1,0:T(8,128)(2,1)S(1)}, u32[]{:S(2)}, u32[]{:S(2)}) %collective-permute-start.25) | collective-permute-done | bytes 393248 | tf_op jit(solution)/shard_map/ppermute | solution.py:328
  (68 shorter events, 23.1 us)
Async XLA Ops:
  1.2 4.4 %collective-permute-start = (bf16[3,384,128]{2,1,0:T(8,128)(2,1)S(1)}, bf16[3,384,128]{2,1,0:T(8,128)(2,1)S(1)}, u32[]{:S(2)}, u32[]{:S(2)}) collective-permute-start(bf16[3,384,128]{2,1,0:T(8,128)(2,1)S(1)} %get-tuple-element.45), channel_id=1, source_target_pairs={{0,4},{4,8},{8,12},{12,16},{16,20},{20,24},{24,28},{1,5},{5,9},{9,... | collective-permute-start | bytes 884744 | tf_op jit(solution)/shard_map/ppermute | solution.py:355
  2.9 4.7 %collective-permute-start.6 = (bf16[3,384,128]{2,1,0:T(8,128)(2,1)S(1)}, bf16[3,384,128]{2,1,0:T(8,128)(2,1)S(1)}, u32[]{:S(2)}, u32[]{:S(2)}) collective-permute-start(bf16[3,384,128]{2,1,0:T(8,128)(2,1)S(1)} %get-tuple-element.46), channel_id=1, source_target_pairs={{4,0},{8,4},{12,8},{16,12},{20,16},{24,20},{28,24},{5,1},{9,5},{13... | collective-permute-start | bytes 884744 | tf_op jit(solution)/shard_map/ppermute | solution.py:355
  7.7 37.0 %collective-permute-start.7 = (bf16[384,1536]{1,0:T(8,128)(2,1)S(1)}, bf16[384,1536]{1,0:T(8,128)(2,1)S(1)}, u32[]{:S(2)}, u32[]{:S(2)}) collective-permute-start(bf16[384,1536]{1,0:T(8,128)(2,1)S(1)} %pad_maximum_fusion.1.refs_1_.refs_6_), channel_id=1, source_target_pairs={{0,8},{4,12},{8,0},{12,4},{16,24},{20,28},{24,16},{28,20},{1,9},{5... | collective-permute-start | bytes 3538952 | tf_op jit(solution)/shard_map/ppermute | solution.py:348
  12.9 31.8 %collective-permute-start.8 = (bf16[384,1536]{1,0:T(8,128)(2,1)S(1)}, bf16[384,1536]{1,0:T(8,128)(2,1)S(1)}, u32[]{:S(2)}, u32[]{:S(2)}) collective-permute-start(bf16[384,1536]{1,0:T(8,128)(2,1)S(1)} %pad_maximum_fusion.1.refs_1_.refs_6_), channel_id=1, source_target_pairs={{0,16},{4,20},{8,24},{12,28},{16,0},{20,4},{24,8},{28,12},{1,17},{... | collective-permute-start | bytes 3538952 | tf_op jit(solution)/shard_map/ppermute | solution.py:348
  14.0 37.8 %copy-start.2 = (bf16[1536,192]{0,1:T(8,128)(2,1)S(1)}, bf16[1536,192]{0,1:T(8,128)(2,1)}, u32[]{:S(2)}) copy-start(bf16[1536,192]{0,1:T(8,128)(2,1)} %param.17) | copy-start | bytes 1769476
  14.0 37.8 %copy-start.3 = (bf16[192,1536]{1,0:T(8,128)(2,1)S(1)}, bf16[192,1536]{1,0:T(8,128)(2,1)}, u32[]{:S(2)}) copy-start(bf16[192,1536]{1,0:T(8,128)(2,1)} %param.15) | copy-start | bytes 1769476
  18.5 12.0 %collective-permute-start.1 = (bf16[4,128,384]{2,1,0:T(8,128)(2,1)S(1)}, bf16[4,128,384]{2,1,0:T(8,128)(2,1)S(1)}, u32[]{:S(2)}, u32[]{:S(2)}) collective-permute-start(bf16[4,128,384]{2,1,0:T(8,128)(2,1)S(1)} %depthwise.2), channel_id=1, source_target_pairs={{0,1},{1,0},{2,3},{3,2},{4,5},{5,4},{6,7},{7,6},{8,9},{9,8},{10,11... | collective-permute-start | bytes 1179656 | tf_op jit(solution)/shard_map/ppermute | solution.py:324
  19.0 14.9 %collective-permute-start.2 = (bf16[4,128,384]{2,1,0:T(8,128)(2,1)S(1)}, bf16[4,128,384]{2,1,0:T(8,128)(2,1)S(1)}, u32[]{:S(2)}, u32[]{:S(2)}) collective-permute-start(bf16[4,128,384]{2,1,0:T(8,128)(2,1)S(1)} %depthwise.2), channel_id=1, source_target_pairs={{1,2},{2,1},{5,6},{6,5},{9,10},{10,9},{13,14},{14,13},{17,18},{18,... | collective-permute-start | bytes 1179656 | tf_op jit(solution)/shard_map/ppermute | solution.py:328
  30.5 12.9 %collective-permute-start.4 = (bf16[4,128,384]{2,1,0:T(8,128)(2,1)S(1)}, bf16[4,128,384]{2,1,0:T(8,128)(2,1)S(1)}, u32[]{:S(2)}, u32[]{:S(2)}) collective-permute-start(bf16[4,128,384]{2,1,0:T(8,128)(2,1)S(1)} %collective-permute-done.1), channel_id=1, source_target_pairs={{1,2},{2,1},{5,6},{6,5},{9,10},{10,9},{13,14},{14,13},{17,18},{18,... | collective-permute-start | bytes 1179656 | tf_op jit(solution)/shard_map/ppermute | solution.py:328
  33.9 10.8 %collective-permute-start.3 = (bf16[4,128,384]{2,1,0:T(8,128)(2,1)S(1)}, bf16[4,128,384]{2,1,0:T(8,128)(2,1)S(1)}, u32[]{:S(2)}, u32[]{:S(2)}) collective-permute-start(bf16[4,128,384]{2,1,0:T(8,128)(2,1)S(1)} %collective-permute-done.2), channel_id=1, source_target_pairs={{1,0},{2,3},{5,4},{6,7},{9,8},{10,11},{13,12},{14,15},{17,16},{18,... | collective-permute-start | bytes 1179656 | tf_op jit(solution)/shard_map/ppermute | solution.py:332
  43.4 10.8 %collective-permute-start.5 = (bf16[4,128,384]{2,1,0:T(8,128)(2,1)S(1)}, bf16[4,128,384]{2,1,0:T(8,128)(2,1)S(1)}, u32[]{:S(2)}, u32[]{:S(2)}) collective-permute-start(bf16[4,128,384]{2,1,0:T(8,128)(2,1)S(1)} %collective-permute-done.4), channel_id=1, source_target_pairs={{1,0},{2,3},{5,4},{6,7},{9,8},{10,11},{13,12},{14,15},{17,16},{18,... | collective-permute-start | bytes 1179656 | tf_op jit(solution)/shard_map/ppermute | solution.py:332
  44.7 16.4 %collective-permute-start.11 = (bf16[4,128,384]{2,1,0:T(8,128)(2,1)S(1)}, bf16[4,128,384]{2,1,0:T(8,128)(2,1)S(1)}, u32[]{:S(2)}, u32[]{:S(2)}) collective-permute-start(bf16[4,128,384]{2,1,0:T(8,128)(2,1)S(1)} %depthwise.3), channel_id=1, source_target_pairs={{0,1},{1,0},{2,3},{3,2},{4,5},{5,4},{6,7},{7,6},{8,9},{9,8},{10,11... | collective-permute-start | bytes 1179656 | tf_op jit(solution)/shard_map/ppermute | solution.py:324
  46.3 14.8 %collective-permute-start.12 = (bf16[4,128,384]{2,1,0:T(8,128)(2,1)S(1)}, bf16[4,128,384]{2,1,0:T(8,128)(2,1)S(1)}, u32[]{:S(2)}, u32[]{:S(2)}) collective-permute-start(bf16[4,128,384]{2,1,0:T(8,128)(2,1)S(1)} %depthwise.3), channel_id=1, source_target_pairs={{1,2},{2,1},{5,6},{6,5},{9,10},{10,9},{13,14},{14,13},{17,18},{18,... | collective-permute-start | bytes 1179656 | tf_op jit(solution)/shard_map/ppermute | solution.py:328
  49.6 14.5 %collective-permute-start.9 = (bf16[192,1536]{1,0:T(8,128)(2,1)S(1)}, bf16[192,1536]{1,0:T(8,128)(2,1)S(1)}, u32[]{:S(2)}, u32[]{:S(2)}) collective-permute-start(bf16[192,1536]{1,0:T(8,128)(2,1)S(1)} %slice.21), channel_id=1, source_target_pairs={{0,16},{4,20},{8,24},{12,28},{16,0},{20,4},{24,8},{28,12},{1,17},{... | collective-permute-start | bytes 1769480 | tf_op jit(solution)/shard_map/ppermute | solution.py:348
  51.2 14.4 %collective-permute-start.10 = (bf16[192,1536]{1,0:T(8,128)(2,1)S(1)}, bf16[192,1536]{1,0:T(8,128)(2,1)S(1)}, u32[]{:S(2)}, u32[]{:S(2)}) collective-permute-start(bf16[192,1536]{1,0:T(8,128)(2,1)S(1)} %slice.22), channel_id=1, source_target_pairs={{0,8},{4,12},{8,0},{12,4},{16,24},{20,28},{24,16},{28,20},{1,9},{5... | collective-permute-start | bytes 1769480 | tf_op jit(solution)/shard_map/ppermute | solution.py:348
  65.6 7.9 %collective-permute-start.13 = (bf16[1152,1536]{1,0:T(8,128)(2,1)S(1)}, bf16[1152,1536]{1,0:T(8,128)(2,1)S(1)}, u32[]{:S(2)}, u32[]{:S(2)}) collective-permute-start(bf16[1152,1536]{1,0:T(8,128)(2,1)S(1)} %pad_maximum_fusion), channel_id=1, source_target_pairs={{0,4},{4,0},{8,12},{12,8},{16,20},{20,16},{24,28},{28,24},{1,5},{5... | collective-permute-start | bytes 10616840 | tf_op jit(solution)/shard_map/ppermute | solution.py:348
  65.7 7.8 %collective-permute-start.14 = (bf16[384,1536]{1,0:T(8,128)(2,1)S(1)}, bf16[384,1536]{1,0:T(8,128)(2,1)S(1)}, u32[]{:S(2)}, u32[]{:S(2)}) collective-permute-start(bf16[384,1536]{1,0:T(8,128)(2,1)S(1)} %pad_maximum_fusion.2), channel_id=1, source_target_pairs={{0,4},{4,0},{8,12},{12,8},{16,20},{20,16},{24,28},{28,24},{1,5},{5... | collective-permute-start | bytes 3538952 | tf_op jit(solution)/shard_map/ppermute | solution.py:348
  66.3 12.9 %collective-permute-start.17 = (bf16[4,128,384]{2,1,0:T(8,128)(2,1)S(1)}, bf16[4,128,384]{2,1,0:T(8,128)(2,1)S(1)}, u32[]{:S(2)}, u32[]{:S(2)}) collective-permute-start(bf16[4,128,384]{2,1,0:T(8,128)(2,1)S(1)} %collective-permute-done.11), channel_id=1, source_target_pairs={{1,2},{2,1},{5,6},{6,5},{9,10},{10,9},{13,14},{14,13},{17,18},{18,... | collective-permute-start | bytes 1179656 | tf_op jit(solution)/shard_map/ppermute | solution.py:328
  69.8 16.5 %collective-permute-start.16 = (bf16[4,128,384]{2,1,0:T(8,128)(2,1)S(1)}, bf16[4,128,384]{2,1,0:T(8,128)(2,1)S(1)}, u32[]{:S(2)}, u32[]{:S(2)}) collective-permute-start(bf16[4,128,384]{2,1,0:T(8,128)(2,1)S(1)} %collective-permute-done.12), channel_id=1, source_target_pairs={{1,0},{2,3},{5,4},{6,7},{9,8},{10,11},{13,12},{14,15},{17,16},{18,... | collective-permute-start | bytes 1179656 | tf_op jit(solution)/shard_map/ppermute | solution.py:332
  79.3 10.2 %collective-permute-start.18 = (bf16[4,128,384]{2,1,0:T(8,128)(2,1)S(1)}, bf16[4,128,384]{2,1,0:T(8,128)(2,1)S(1)}, u32[]{:S(2)}, u32[]{:S(2)}) collective-permute-start(bf16[4,128,384]{2,1,0:T(8,128)(2,1)S(1)} %collective-permute-done.17), channel_id=1, source_target_pairs={{1,0},{2,3},{5,4},{6,7},{9,8},{10,11},{13,12},{14,15},{17,16},{18,... | collective-permute-start | bytes 1179656 | tf_op jit(solution)/shard_map/ppermute | solution.py:332
  80.6 19.1 %collective-permute-start.21 = (bf16[4,384,128]{2,1,0:T(8,128)(2,1)S(1)}, bf16[4,384,128]{2,1,0:T(8,128)(2,1)S(1)}, u32[]{:S(2)}, u32[]{:S(2)}) collective-permute-start(bf16[4,384,128]{2,1,0:T(8,128)(2,1)S(1)} %get-tuple-element.35), channel_id=1, source_target_pairs={{0,1},{3,2},{4,5},{7,6},{8,9},{11,10},{12,13},{15,14},{16,17},{19,... | collective-permute-start | bytes 1179656 | tf_op jit(solution)/shard_map/ppermute | solution.py:336
  85.0 18.3 %collective-permute-start.15 = (bf16[4,384,128]{2,1,0:T(8,128)(2,1)S(1)}, bf16[4,384,128]{2,1,0:T(8,128)(2,1)S(1)}, u32[]{:S(2)}, u32[]{:S(2)}) collective-permute-start(bf16[4,384,128]{2,1,0:T(8,128)(2,1)S(1)} %get-tuple-element.32), channel_id=1, source_target_pairs={{0,1},{3,2},{4,5},{7,6},{8,9},{11,10},{12,13},{15,14},{16,17},{19,... | collective-permute-start | bytes 1179656 | tf_op jit(solution)/shard_map/ppermute | solution.py:336
  98.3 13.9 %collective-permute-start.19 = (bf16[4,384,128]{2,1,0:T(8,128)(2,1)S(1)}, bf16[4,384,128]{2,1,0:T(8,128)(2,1)S(1)}, u32[]{:S(2)}, u32[]{:S(2)}) collective-permute-start(bf16[4,384,128]{2,1,0:T(8,128)(2,1)S(1)} %get-tuple-element.37), channel_id=1, source_target_pairs={{0,1},{3,2},{4,5},{7,6},{8,9},{11,10},{12,13},{15,14},{16,17},{19,... | collective-permute-start | bytes 1179656 | tf_op jit(solution)/shard_map/ppermute | solution.py:336
  99.8 14.8 %collective-permute-start.22 = (bf16[4,384,128]{2,1,0:T(8,128)(2,1)S(1)}, bf16[4,384,128]{2,1,0:T(8,128)(2,1)S(1)}, u32[]{:S(2)}, u32[]{:S(2)}) collective-permute-start(bf16[4,384,128]{2,1,0:T(8,128)(2,1)S(1)} %add_convert_fusion.5), channel_id=1, source_target_pairs={{1,2},{2,1},{5,6},{6,5},{9,10},{10,9},{13,14},{14,13},{17,18},{18,... | collective-permute-start | bytes 1179656 | tf_op jit(solution)/shard_map/ppermute | solution.py:328
  102.0 18.7 %collective-permute-start.24 = (bf16[4,384,128]{2,1,0:T(8,128)(2,1)S(1)}, bf16[4,384,128]{2,1,0:T(8,128)(2,1)S(1)}, u32[]{:S(2)}, u32[]{:S(2)}) collective-permute-start(bf16[4,384,128]{2,1,0:T(8,128)(2,1)S(1)} %get-tuple-element.41), channel_id=1, source_target_pairs={{0,1},{3,2},{4,5},{7,6},{8,9},{11,10},{12,13},{15,14},{16,17},{19,... | collective-permute-start | bytes 1179656 | tf_op jit(solution)/shard_map/ppermute | solution.py:336
  103.4 36.2 %copy-start.7 = (f32[384]{0:T(512)S(1)}, f32[384]{0:T(512)}, u32[]{:S(2)}) copy-start(f32[384]{0:T(512)} %param.18) | copy-start | bytes 4612
  103.4 36.2 %copy-start.8 = (f32[384]{0:T(512)S(1)}, f32[384]{0:T(512)}, u32[]{:S(2)}) copy-start(f32[384]{0:T(512)} %param.19) | copy-start | bytes 4612
  112.4 13.9 %collective-permute-start.26 = (bf16[4,384,128]{2,1,0:T(8,128)(2,1)S(1)}, bf16[4,384,128]{2,1,0:T(8,128)(2,1)S(1)}, u32[]{:S(2)}, u32[]{:S(2)}) collective-permute-start(bf16[4,384,128]{2,1,0:T(8,128)(2,1)S(1)} %add_convert_fusion.6), channel_id=1, source_target_pairs={{1,2},{2,1},{5,6},{6,5},{9,10},{10,9},{13,14},{14,13},{17,18},{18,... | collective-permute-start | bytes 1179656 | tf_op jit(solution)/shard_map/ppermute | solution.py:328
  115.5 13.6 %collective-permute-start.23 = (bf16[4,384,128]{2,1,0:T(8,128)(2,1)}, bf16[4,384,128]{2,1,0:T(8,128)(2,1)S(1)}, u32[]{:S(2)}, u32[]{:S(2)}) collective-permute-start(bf16[4,384,128]{2,1,0:T(8,128)(2,1)} %add_convert_fusion.4), channel_id=1, source_target_pairs={{0,1},{1,0},{2,3},{3,2},{4,5},{5,4},{6,7},{7,6},{8,9},{9,8},{10,11... | collective-permute-start | bytes 1179656 | tf_op jit(solution)/shard_map/ppermute | solution.py:324
  115.5 19.3 %collective-permute-start.20 = (bf16[4,384,128]{2,1,0:T(8,128)(2,1)S(1)}, bf16[4,384,128]{2,1,0:T(8,128)(2,1)S(1)}, u32[]{:S(2)}, u32[]{:S(2)}) collective-permute-start(bf16[4,384,128]{2,1,0:T(8,128)(2,1)S(1)} %add_convert_fusion.7), channel_id=1, source_target_pairs={{1,2},{2,1},{5,6},{6,5},{9,10},{10,9},{13,14},{14,13},{17,18},{18,... | collective-permute-start | bytes 1179656 | tf_op jit(solution)/shard_map/ppermute | solution.py:328
  121.5 18.1 %collective-permute-start.25 = (bf16[4,384,128]{2,1,0:T(8,128)(2,1)}, bf16[4,384,128]{2,1,0:T(8,128)(2,1)S(1)}, u32[]{:S(2)}, u32[]{:S(2)}) collective-permute-start(bf16[4,384,128]{2,1,0:T(8,128)(2,1)} %add_convert_fusion.2), channel_id=1, source_target_pairs={{1,2},{2,1},{5,6},{6,5},{9,10},{10,9},{13,14},{14,13},{17,18},{18,... | collective-permute-start | bytes 1179656 | tf_op jit(solution)/shard_map/ppermute | solution.py:328
  127.2 12.5 %collective-permute-start.27 = (bf16[4,384,128]{2,1,0:T(8,128)(2,1)}, bf16[4,384,128]{2,1,0:T(8,128)(2,1)S(1)}, u32[]{:S(2)}, u32[]{:S(2)}) collective-permute-start(bf16[4,384,128]{2,1,0:T(8,128)(2,1)} %add_convert_fusion.1), channel_id=1, source_target_pairs={{0,1},{1,0},{2,3},{3,2},{4,5},{5,4},{6,7},{7,6},{8,9},{9,8},{10,11... | collective-permute-start | bytes 1179656 | tf_op jit(solution)/shard_map/ppermute | solution.py:324
  (6 other events, 84.5 us)

commit v7 on v6

--- a/solution.py
+++ b/solution.py
@@ -172,7 +172,7 @@
             out_ref[row] = partial[:, row * width : (row + 1) * width].astype(out_ref.dtype)
 
 
-def start_shards(pieces, target, shard, sems):
+def start_shards(pieces, target, shard, sems, wanted=None):
     t = lax.axis_index("tile")
 
     def shard_copy(piece):
@@ -180,12 +180,18 @@
         at = pl.ds(pl.multiple_of((t ^ k) * shard, 16), shard)
         return pltpu.make_async_copy(part.at[first : first + shard, :], target.at[at, :], sems.at[k])
 
+    def on_wanted(piece, act):
+        if wanted is None:
+            act()
+        else:
+            pl.when(wanted(lax.div(t ^ piece[2], 2)))(act)
+
     for piece in pieces:
-        shard_copy(piece).start()
+        on_wanted(piece, lambda piece=piece: shard_copy(piece).start())
 
     def wait():
         for piece in pieces:
-            shard_copy(piece).wait()
+            on_wanted(piece, lambda piece=piece: shard_copy(piece).wait())
 
     return wait
 
@@ -194,9 +200,10 @@
     normed_ref, parts, b_in_ref, hidden, out_ref = refs[0], refs[1:8], refs[8], refs[9], refs[10]
     w_in, w_out, in_sem, out_sem = refs[11:]
     shard = parts[0].shape[0] // 2
+    far = line_places(lax.axis_index("chan"))[2]
     ins, outs = weight_pieces(parts, shard)
     w_in_there = start_shards(ins, w_in, shard, in_sem)
-    w_out_there = start_shards(outs, w_out, shard, out_sem)
+    w_out_there = start_shards(outs, w_out, shard, out_sem, lambda place: place == far)
     w_in_there()
     lift(normed_ref, w_in, b_in_ref, hidden)
     w_out_there()
@@ -207,7 +214,9 @@
     hidden, parts, out_refs = refs[0], refs[1:8], refs[8:11]
     w_out, out_sem = refs[11:]
     shard = parts[0].shape[0] // 2
-    start_shards(weight_pieces(parts, shard)[1], w_out, shard, out_sem)()
+    far = line_places(lax.axis_index("chan"))[2]
+    outs = weight_pieces(parts, shard)[1]
+    start_shards(outs, w_out, shard, out_sem, lambda place: place != far)()
     project(hidden, w_out, out_refs, slice(1, 4))
 
 

time: 142 us -> 140 us (0.986)
  waiting for transfers between devices: 57.2 us -> 55.1 us
  transfers between devices with their start and end apart: 28 -> 28, of which waited for: 15 -> 16; matrix products, arithmetic and copies ran while one was open for 3% -> 3% of each run, Pallas kernels for 20% -> 19%
where the time goes in v7:
time: 140 us
  waiting for transfers between devices  55.1 us (39%)
  starting transfers between devices  49.7 us (36%)
  Pallas kernels  27 us (19%)
  other arithmetic  6 us (4%)
    ppermute x8, starting transfers between devices, to_middle(): return lax.ppermute(array, 'chan', [(1, 2), (2, 1)])  25.1 us
    ppermute x8, waiting for transfers between devices, to_middle(): return lax.ppermute(array, 'chan', [(1, 2), (2, 1)])  15.7 us
    ppermute x4, waiting for transfers between devices, to_pair(): return lax.ppermute(array, 'chan', [(0, 1), (1, 0), (2, 3), (3, 2)])  15.7 us
    ppermute x4, waiting for transfers between devices, inward(): return lax.ppermute(array, 'chan', [(0, 1), (3, 2)])  9.81 us
    ppermute x6, starting transfers between devices, flipped(): return lax.ppermute(array, 'tile', [(i, i ^ bit) for i in range(8)])  9.1 us
    pallas_call x2, Pallas kernels, conv_chunk(): pl.pallas_call(functools.partial(conv_kernel, tuple(plan)), grid=(slab //...  8.89 us
    pallas_call x1, Pallas kernels, mlp_chunk(): pl.pallas_call(norm_mlp_kernel, in_specs=[ANYWHERE] * (len(slabs) + len(w...  8.88 us
    ppermute x6, waiting for transfers between devices, flipped(): return lax.ppermute(array, 'tile', [(i, i ^ bit) for i in range(8)])  6.94 us
  transfers between devices with their start and end apart: 28, of which 16 were waited for; matrix products, arithmetic and copies ran while one was open for 3% of the time, Pallas kernels for 19%

profile of v7, /device:TPU:8, one launch (start us, length us, event | category | flops | bytes accessed | tf_op | source)
XLA Modules:
  0.0 139.5 jit_solution(2087499416090892432)
XLA Ops:
  1.2 1.8 %collective-permute-start = (bf16[3,384,128]{2,1,0:T(8,128)(2,1)S(1)}, bf16[3,384,128]{2,1,0:T(8,128)(2,1)S(1)}, u32[]{:S(2)}, u32[]{:S(2)}) collective-permute-start(bf16[3,384,128]{2,1,0:T(8,128)(2,1)S(1)} %get-tuple-element.45), channel_id=1, source_target_pairs={{0,4},{4,8},{8,12},{12,16},{16,20},{20,24},{24,28},{1,5},{5,9},{9,... | collective-permute-start | bytes 884744 | tf_op jit(solution)/shard_map/ppermute | solution.py:364
  5.6 2.1 %collective-permute-done.6.refs_1_ = bf16[3,384,128]{2,1,0:T(8,128)(2,1)S(1)} collective-permute-done((bf16[3,384,128]{2,1,0:T(8,128)(2,1)S(1)}, bf16[3,384,128]{2,1,0:T(8,128)(2,1)S(1)}, u32[]{:S(2)}, u32[]{:S(2)}) %collective-permute-start.6) | collective-permute-done | bytes 294944 | tf_op jit(solution)/shard_map/ppermute | solution.py:364
  7.7 5.2 %collective-permute-start.7 = (bf16[384,1536]{1,0:T(8,128)(2,1)S(1)}, bf16[384,1536]{1,0:T(8,128)(2,1)S(1)}, u32[]{:S(2)}, u32[]{:S(2)}) collective-permute-start(bf16[384,1536]{1,0:T(8,128)(2,1)S(1)} %pad_maximum_fusion.1.refs_1_.refs_6_), channel_id=1, source_target_pairs={{0,8},{4,12},{8,0},{12,4},{16,24},{20,28},{24,16},{28,20},{1,9},{5... | collective-permute-start | bytes 3538952 | tf_op jit(solution)/shard_map/ppermute | solution.py:357
  14.0 4.4 %depthwise.2 = bf16[4,128,384]{2,1,0:T(8,128)(2,1)S(1)} custom-call(bf16[8,384,128]{2,1,0:T(8,128)(2,1)S(1)} %copy-done, bf16[3,384,128]{2,1,0:T(8,128)(2,1)S(1)} %collective-permute-done.refs_1_, f32[49,384]{1,0:T(8,128)S(1)} %bitcast.16, f32[1,384]{1,0:T(1,128)S(1)} %broadcast_in_dim.8.refs_3_), custom_call_target="tpu_custom_call" | custom-call | flops 19267584 | bytes 786432 | tf_op jit(solution)/shard_map/depthwise/pallas_call | solution.py:63
  19.0 4.6 %collective-permute-start.2 = (bf16[4,128,384]{2,1,0:T(8,128)(2,1)S(1)}, bf16[4,128,384]{2,1,0:T(8,128)(2,1)S(1)}, u32[]{:S(2)}, u32[]{:S(2)}) collective-permute-start(bf16[4,128,384]{2,1,0:T(8,128)(2,1)S(1)} %depthwise.2), channel_id=1, source_target_pairs={{1,2},{2,1},{5,6},{6,5},{9,10},{10,9},{13,14},{14,13},{17,18},{18,... | collective-permute-start | bytes 1179656 | tf_op jit(solution)/shard_map/ppermute | solution.py:337
  23.6 6.8 %collective-permute-done.1 = bf16[4,128,384]{2,1,0:T(8,128)(2,1)S(1)} collective-permute-done((bf16[4,128,384]{2,1,0:T(8,128)(2,1)S(1)}, bf16[4,128,384]{2,1,0:T(8,128)(2,1)S(1)}, u32[]{:S(2)}, u32[]{:S(2)}) %collective-permute-start.1) | collective-permute-done | bytes 393248 | tf_op jit(solution)/shard_map/ppermute | solution.py:333
  30.5 3.5 %collective-permute-start.4 = (bf16[4,128,384]{2,1,0:T(8,128)(2,1)S(1)}, bf16[4,128,384]{2,1,0:T(8,128)(2,1)S(1)}, u32[]{:S(2)}, u32[]{:S(2)}) collective-permute-start(bf16[4,128,384]{2,1,0:T(8,128)(2,1)S(1)} %collective-permute-done.1), channel_id=1, source_target_pairs={{1,2},{2,1},{5,6},{6,5},{9,10},{10,9},{13,14},{14,13},{17,18},{18,... | collective-permute-start | bytes 1179656 | tf_op jit(solution)/shard_map/ppermute | solution.py:337
  35.3 4.4 %depthwise.3 = bf16[4,128,384]{2,1,0:T(8,128)(2,1)S(1)} custom-call(bf16[8,384,128]{2,1,0:T(8,128)(2,1)S(1)} %copy-done, bf16[3,384,128]{2,1,0:T(8,128)(2,1)S(1)} %collective-permute-done.6.refs_1_, f32[49,384]{1,0:T(8,128)S(1)} %bitcast.17, f32[1,384]{1,0:T(1,128)S(1)} %broadcast_in_dim.8.refs_3_), custom_call_target="tpu_custom_call" | custom-call | flops 19267584 | bytes 786432 | tf_op jit(solution)/shard_map/depthwise/pallas_call | solution.py:63
  39.7 3.7 %collective-permute-done.4 = bf16[4,128,384]{2,1,0:T(8,128)(2,1)S(1)} collective-permute-done((bf16[4,128,384]{2,1,0:T(8,128)(2,1)S(1)}, bf16[4,128,384]{2,1,0:T(8,128)(2,1)S(1)}, u32[]{:S(2)}, u32[]{:S(2)}) %collective-permute-start.4) | collective-permute-done | bytes 393248 | tf_op jit(solution)/shard_map/ppermute | solution.py:337
  44.7 1.6 %collective-permute-start.11 = (bf16[4,128,384]{2,1,0:T(8,128)(2,1)S(1)}, bf16[4,128,384]{2,1,0:T(8,128)(2,1)S(1)}, u32[]{:S(2)}, u32[]{:S(2)}) collective-permute-start(bf16[4,128,384]{2,1,0:T(8,128)(2,1)S(1)} %depthwise.3), channel_id=1, source_target_pairs={{0,1},{1,0},{2,3},{3,2},{4,5},{5,4},{6,7},{7,6},{8,9},{9,8},{10,11... | collective-permute-start | bytes 1179656 | tf_op jit(solution)/shard_map/ppermute | solution.py:333
  46.3 3.2 %collective-permute-start.12 = (bf16[4,128,384]{2,1,0:T(8,128)(2,1)S(1)}, bf16[4,128,384]{2,1,0:T(8,128)(2,1)S(1)}, u32[]{:S(2)}, u32[]{:S(2)}) collective-permute-start(bf16[4,128,384]{2,1,0:T(8,128)(2,1)S(1)} %depthwise.3), channel_id=1, source_target_pairs={{1,2},{2,1},{5,6},{6,5},{9,10},{10,9},{13,14},{14,13},{17,18},{18,... | collective-permute-start | bytes 1179656 | tf_op jit(solution)/shard_map/ppermute | solution.py:337
  49.6 1.6 %collective-permute-start.9 = (bf16[192,1536]{1,0:T(8,128)(2,1)S(1)}, bf16[192,1536]{1,0:T(8,128)(2,1)S(1)}, u32[]{:S(2)}, u32[]{:S(2)}) collective-permute-start(bf16[192,1536]{1,0:T(8,128)(2,1)S(1)} %slice.21), channel_id=1, source_target_pairs={{0,16},{4,20},{8,24},{12,28},{16,0},{20,4},{24,8},{28,12},{1,17},{... | collective-permute-start | bytes 1769480 | tf_op jit(solution)/shard_map/ppermute | solution.py:357
  52.1 2.1 %collective-permute-done.5 = bf16[4,128,384]{2,1,0:T(8,128)(2,1)S(1)} collective-permute-done((bf16[4,128,384]{2,1,0:T(8,128)(2,1)S(1)}, bf16[4,128,384]{2,1,0:T(8,128)(2,1)S(1)}, u32[]{:S(2)}, u32[]{:S(2)}) %collective-permute-start.5) | collective-permute-done | bytes 393248 | tf_op jit(solution)/shard_map/ppermute | solution.py:341
  54.2 6.9 %collective-permute-done.11 = bf16[4,128,384]{2,1,0:T(8,128)(2,1)S(1)} collective-permute-done((bf16[4,128,384]{2,1,0:T(8,128)(2,1)S(1)}, bf16[4,128,384]{2,1,0:T(8,128)(2,1)S(1)}, u32[]{:S(2)}, u32[]{:S(2)}) %collective-permute-start.11) | collective-permute-done | bytes 393248 | tf_op jit(solution)/shard_map/ppermute | solution.py:333
  61.1 3.0 %collective-permute-done.9.refs_4_.refs_9_ = bf16[192,1536]{1,0:T(8,128)(2,1)S(1)} collective-permute-done((bf16[192,1536]{1,0:T(8,128)(2,1)S(1)}, bf16[192,1536]{1,0:T(8,128)(2,1)S(1)}, u32[]{:S(2)}, u32[]{:S(2)}) %collective-permute-start.9) | collective-permute-done | bytes 589856 | tf_op jit(solution)/shard_map/ppermute | solution.py:357
  64.0 1.6 %collective-permute-done.10.refs_5_.refs_10_ = bf16[192,1536]{1,0:T(8,128)(2,1)S(1)} collective-permute-done((bf16[192,1536]{1,0:T(8,128)(2,1)S(1)}, bf16[192,1536]{1,0:T(8,128)(2,1)S(1)}, u32[]{:S(2)}, u32[]{:S(2)}) %collective-permute-start.10) | collective-permute-done | bytes 589856 | tf_op jit(solution)/shard_map/ppermute | solution.py:357
  66.3 2.2 %collective-permute-start.17 = (bf16[4,128,384]{2,1,0:T(8,128)(2,1)S(1)}, bf16[4,128,384]{2,1,0:T(8,128)(2,1)S(1)}, u32[]{:S(2)}, u32[]{:S(2)}) collective-permute-start(bf16[4,128,384]{2,1,0:T(8,128)(2,1)S(1)} %collective-permute-done.11), channel_id=1, source_target_pairs={{1,2},{2,1},{5,6},{6,5},{9,10},{10,9},{13,14},{14,13},{17,18},{18,... | collective-permute-start | bytes 1179656 | tf_op jit(solution)/shard_map/ppermute | solution.py:337
  71.1 2.4 %collective-permute-done.14.refs_7_.refs_12_ = bf16[384,1536]{1,0:T(8,128)(2,1)S(1)} collective-permute-done((bf16[384,1536]{1,0:T(8,128)(2,1)S(1)}, bf16[384,1536]{1,0:T(8,128)(2,1)S(1)}, u32[]{:S(2)}, u32[]{:S(2)}) %collective-permute-start.14) | collective-permute-done | bytes 1179680 | tf_op jit(solution)/shard_map/ppermute | solution.py:357
  73.5 5.1 %mlp_first.1 = (bf16[512,1536]{1,0:T(8,128)(2,1)S(1)}, bf16[4,384,128]{2,1,0:T(8,128)(2,1)S(1)}) custom-call(bf16[512,1536]{1,0:T(8,128)(2,1)S(1)} %norm.1.refs_0_, bf16[384,1536]{1,0:T(8,128)(2,1)S(1)} %pad_maximum_fusion.1.refs_1_.refs_6_, bf16[384,1536]{1,0:T(8,128)(2,1)S(1)} %collective-permute-done.7.refs_2_.refs_7_, ...), custom_call_target="tpu_custom_call" | custom-call | flops 3623878656 | bytes 9437184 | tf_op jit(solution)/shard_map/mlp_first/pallas_call | solution.py:230
  81.9 2.9 %mlp_rest.1 = (bf16[4,384,128]{2,1,0:T(8,128)(2,1)S(1)}, bf16[4,384,128]{2,1,0:T(8,128)(2,1)S(1)}, bf16[4,384,128]{2,1,0:T(8,128)(2,1)S(1)}) custom-call(bf16[512,1536]{1,0:T(8,128)(2,1)S(1)} %get-tuple-element.30.refs_0_, bf16[384,1536]{1,0:T(8,128)(2,1)S(1)} %pad_maximum_fusion.1.refs_1_.refs_6_, ...), custom_call_target="tpu_custom_call" | custom-call | flops 2415919104 | bytes 4718592 | tf_op jit(solution)/shard_map/mlp_rest/pallas_call | solution.py:242
  86.1 2.7 %collective-permute-done.18 = bf16[4,128,384]{2,1,0:T(8,128)(2,1)S(1)} collective-permute-done((bf16[4,128,384]{2,1,0:T(8,128)(2,1)S(1)}, bf16[4,128,384]{2,1,0:T(8,128)(2,1)S(1)}, u32[]{:S(2)}, u32[]{:S(2)}) %collective-permute-start.18) | collective-permute-done | bytes 393248 | tf_op jit(solution)/shard_map/ppermute | solution.py:341
  88.8 8.9 %mlp.1 = (bf16[4,384,128]{2,1,0:T(8,128)(2,1)S(1)}, bf16[4,384,128]{2,1,0:T(8,128)(2,1)S(1)}, bf16[4,384,128]{2,1,0:T(8,128)(2,1)S(1)}, bf16[4,384,128]{2,1,0:T(8,128)(2,1)S(1)}) custom-call(bf16[512,384]{1,0:T(8,128)(2,1)S(1)} %bitcast.14, bf16[512,384]{1,0:T(8,128)(2,1)S(1)} %bitcast.18, bf16[512,384]{1,0:T(8,128)(2,1)S(1)} %bitcast.19, ...), custom_call_target="tpu_custom_call" | custom-call | flops 4831838208 | bytes 12582912 | tf_op jit(solution)/shard_map/mlp/pallas_call | solution.py:302
  99.1 2.9 %collective-permute-start.22 = (bf16[4,384,128]{2,1,0:T(8,128)(2,1)S(1)}, bf16[4,384,128]{2,1,0:T(8,128)(2,1)S(1)}, u32[]{:S(2)}, u32[]{:S(2)}) collective-permute-start(bf16[4,384,128]{2,1,0:T(8,128)(2,1)S(1)} %add_convert_fusion.5), channel_id=1, source_target_pairs={{1,2},{2,1},{5,6},{6,5},{9,10},{10,9},{13,14},{14,13},{17,18},{18,... | collective-permute-start | bytes 1179656 | tf_op jit(solution)/shard_map/ppermute | solution.py:337
  103.5 8.2 %collective-permute-done.19 = bf16[4,384,128]{2,1,0:T(8,128)(2,1)S(1)} collective-permute-done((bf16[4,384,128]{2,1,0:T(8,128)(2,1)S(1)}, bf16[4,384,128]{2,1,0:T(8,128)(2,1)S(1)}, u32[]{:S(2)}, u32[]{:S(2)}) %collective-permute-start.19) | collective-permute-done | bytes 393248 | tf_op jit(solution)/shard_map/ppermute | solution.py:345
  111.8 2.9 %collective-permute-start.26 = (bf16[4,384,128]{2,1,0:T(8,128)(2,1)S(1)}, bf16[4,384,128]{2,1,0:T(8,128)(2,1)S(1)}, u32[]{:S(2)}, u32[]{:S(2)}) collective-permute-start(bf16[4,384,128]{2,1,0:T(8,128)(2,1)S(1)} %add_convert_fusion.6), channel_id=1, source_target_pairs={{1,2},{2,1},{5,6},{6,5},{9,10},{10,9},{13,14},{14,13},{17,18},{18,... | collective-permute-start | bytes 1179656 | tf_op jit(solution)/shard_map/ppermute | solution.py:337
  115.5 3.0 %collective-permute-start.20 = (bf16[4,384,128]{2,1,0:T(8,128)(2,1)S(1)}, bf16[4,384,128]{2,1,0:T(8,128)(2,1)S(1)}, u32[]{:S(2)}, u32[]{:S(2)}) collective-permute-start(bf16[4,384,128]{2,1,0:T(8,128)(2,1)S(1)} %add_convert_fusion.7), channel_id=1, source_target_pairs={{1,2},{2,1},{5,6},{6,5},{9,10},{10,9},{13,14},{14,13},{17,18},{18,... | collective-permute-start | bytes 1179656 | tf_op jit(solution)/shard_map/ppermute | solution.py:337
  118.5 1.6 %collective-permute-done.24 = bf16[4,384,128]{2,1,0:T(8,128)(2,1)S(1)} collective-permute-done((bf16[4,384,128]{2,1,0:T(8,128)(2,1)S(1)}, bf16[4,384,128]{2,1,0:T(8,128)(2,1)S(1)}, u32[]{:S(2)}, u32[]{:S(2)}) %collective-permute-start.24) | collective-permute-done | bytes 393248 | tf_op jit(solution)/shard_map/ppermute | solution.py:345
  120.9 2.8 %collective-permute-start.25 = (bf16[4,384,128]{2,1,0:T(8,128)(2,1)}, bf16[4,384,128]{2,1,0:T(8,128)(2,1)S(1)}, u32[]{:S(2)}, u32[]{:S(2)}) collective-permute-start(bf16[4,384,128]{2,1,0:T(8,128)(2,1)} %add_convert_fusion.2), channel_id=1, source_target_pairs={{1,2},{2,1},{5,6},{6,5},{9,10},{10,9},{13,14},{14,13},{17,18},{18,... | collective-permute-start | bytes 1179656 | tf_op jit(solution)/shard_map/ppermute | solution.py:337
  123.8 1.9 %collective-permute-done.26 = bf16[4,384,128]{2,1,0:T(8,128)(2,1)S(1)} collective-permute-done((bf16[4,384,128]{2,1,0:T(8,128)(2,1)S(1)}, bf16[4,384,128]{2,1,0:T(8,128)(2,1)S(1)}, u32[]{:S(2)}, u32[]{:S(2)}) %collective-permute-start.26) | collective-permute-done | bytes 393248 | tf_op jit(solution)/shard_map/ppermute | solution.py:337
  126.5 2.0 %collective-permute-done.23 = bf16[4,384,128]{2,1,0:T(8,128)(2,1)S(1)} collective-permute-done((bf16[4,384,128]{2,1,0:T(8,128)(2,1)}, bf16[4,384,128]{2,1,0:T(8,128)(2,1)S(1)}, u32[]{:S(2)}, u32[]{:S(2)}) %collective-permute-start.23) | collective-permute-done | bytes 393248 | tf_op jit(solution)/shard_map/ppermute | solution.py:333
  128.5 5.3 %collective-permute-done.20 = bf16[4,384,128]{2,1,0:T(8,128)(2,1)S(1)} collective-permute-done((bf16[4,384,128]{2,1,0:T(8,128)(2,1)S(1)}, bf16[4,384,128]{2,1,0:T(8,128)(2,1)S(1)}, u32[]{:S(2)}, u32[]{:S(2)}) %collective-permute-start.20) | collective-permute-done | bytes 393248 | tf_op jit(solution)/shard_map/ppermute | solution.py:337
  133.8 4.2 %collective-permute-done.25 = bf16[4,384,128]{2,1,0:T(8,128)(2,1)S(1)} collective-permute-done((bf16[4,384,128]{2,1,0:T(8,128)(2,1)}, bf16[4,384,128]{2,1,0:T(8,128)(2,1)S(1)}, u32[]{:S(2)}, u32[]{:S(2)}) %collective-permute-start.25) | collective-permute-done | bytes 393248 | tf_op jit(solution)/shard_map/ppermute | solution.py:337
  (68 shorter events, 23.8 us)
Async XLA Ops:
  1.2 4.4 %collective-permute-start = (bf16[3,384,128]{2,1,0:T(8,128)(2,1)S(1)}, bf16[3,384,128]{2,1,0:T(8,128)(2,1)S(1)}, u32[]{:S(2)}, u32[]{:S(2)}) collective-permute-start(bf16[3,384,128]{2,1,0:T(8,128)(2,1)S(1)} %get-tuple-element.45), channel_id=1, source_target_pairs={{0,4},{4,8},{8,12},{12,16},{16,20},{20,24},{24,28},{1,5},{5,9},{9,... | collective-permute-start | bytes 884744 | tf_op jit(solution)/shard_map/ppermute | solution.py:364
  2.9 4.7 %collective-permute-start.6 = (bf16[3,384,128]{2,1,0:T(8,128)(2,1)S(1)}, bf16[3,384,128]{2,1,0:T(8,128)(2,1)S(1)}, u32[]{:S(2)}, u32[]{:S(2)}) collective-permute-start(bf16[3,384,128]{2,1,0:T(8,128)(2,1)S(1)} %get-tuple-element.46), channel_id=1, source_target_pairs={{4,0},{8,4},{12,8},{16,12},{20,16},{24,20},{28,24},{5,1},{9,5},{13... | collective-permute-start | bytes 884744 | tf_op jit(solution)/shard_map/ppermute | solution.py:364
  7.7 37.0 %collective-permute-start.7 = (bf16[384,1536]{1,0:T(8,128)(2,1)S(1)}, bf16[384,1536]{1,0:T(8,128)(2,1)S(1)}, u32[]{:S(2)}, u32[]{:S(2)}) collective-permute-start(bf16[384,1536]{1,0:T(8,128)(2,1)S(1)} %pad_maximum_fusion.1.refs_1_.refs_6_), channel_id=1, source_target_pairs={{0,8},{4,12},{8,0},{12,4},{16,24},{20,28},{24,16},{28,20},{1,9},{5... | collective-permute-start | bytes 3538952 | tf_op jit(solution)/shard_map/ppermute | solution.py:357
  12.9 31.8 %collective-permute-start.8 = (bf16[384,1536]{1,0:T(8,128)(2,1)S(1)}, bf16[384,1536]{1,0:T(8,128)(2,1)S(1)}, u32[]{:S(2)}, u32[]{:S(2)}) collective-permute-start(bf16[384,1536]{1,0:T(8,128)(2,1)S(1)} %pad_maximum_fusion.1.refs_1_.refs_6_), channel_id=1, source_target_pairs={{0,16},{4,20},{8,24},{12,28},{16,0},{20,4},{24,8},{28,12},{1,17},{... | collective-permute-start | bytes 3538952 | tf_op jit(solution)/shard_map/ppermute | solution.py:357
  14.0 37.8 %copy-start.2 = (bf16[1536,192]{0,1:T(8,128)(2,1)S(1)}, bf16[1536,192]{0,1:T(8,128)(2,1)}, u32[]{:S(2)}) copy-start(bf16[1536,192]{0,1:T(8,128)(2,1)} %param.17) | copy-start | bytes 1769476
  14.0 37.8 %copy-start.3 = (bf16[192,1536]{1,0:T(8,128)(2,1)S(1)}, bf16[192,1536]{1,0:T(8,128)(2,1)}, u32[]{:S(2)}) copy-start(bf16[192,1536]{1,0:T(8,128)(2,1)} %param.15) | copy-start | bytes 1769476
  18.5 12.0 %collective-permute-start.1 = (bf16[4,128,384]{2,1,0:T(8,128)(2,1)S(1)}, bf16[4,128,384]{2,1,0:T(8,128)(2,1)S(1)}, u32[]{:S(2)}, u32[]{:S(2)}) collective-permute-start(bf16[4,128,384]{2,1,0:T(8,128)(2,1)S(1)} %depthwise.2), channel_id=1, source_target_pairs={{0,1},{1,0},{2,3},{3,2},{4,5},{5,4},{6,7},{7,6},{8,9},{9,8},{10,11... | collective-permute-start | bytes 1179656 | tf_op jit(solution)/shard_map/ppermute | solution.py:333
  19.0 14.9 %collective-permute-start.2 = (bf16[4,128,384]{2,1,0:T(8,128)(2,1)S(1)}, bf16[4,128,384]{2,1,0:T(8,128)(2,1)S(1)}, u32[]{:S(2)}, u32[]{:S(2)}) collective-permute-start(bf16[4,128,384]{2,1,0:T(8,128)(2,1)S(1)} %depthwise.2), channel_id=1, source_target_pairs={{1,2},{2,1},{5,6},{6,5},{9,10},{10,9},{13,14},{14,13},{17,18},{18,... | collective-permute-start | bytes 1179656 | tf_op jit(solution)/shard_map/ppermute | solution.py:337
  30.5 12.9 %collective-permute-start.4 = (bf16[4,128,384]{2,1,0:T(8,128)(2,1)S(1)}, bf16[4,128,384]{2,1,0:T(8,128)(2,1)S(1)}, u32[]{:S(2)}, u32[]{:S(2)}) collective-permute-start(bf16[4,128,384]{2,1,0:T(8,128)(2,1)S(1)} %collective-permute-done.1), channel_id=1, source_target_pairs={{1,2},{2,1},{5,6},{6,5},{9,10},{10,9},{13,14},{14,13},{17,18},{18,... | collective-permute-start | bytes 1179656 | tf_op jit(solution)/shard_map/ppermute | solution.py:337
  33.9 10.8 %collective-permute-start.3 = (bf16[4,128,384]{2,1,0:T(8,128)(2,1)S(1)}, bf16[4,128,384]{2,1,0:T(8,128)(2,1)S(1)}, u32[]{:S(2)}, u32[]{:S(2)}) collective-permute-start(bf16[4,128,384]{2,1,0:T(8,128)(2,1)S(1)} %collective-permute-done.2), channel_id=1, source_target_pairs={{1,0},{2,3},{5,4},{6,7},{9,8},{10,11},{13,12},{14,15},{17,16},{18,... | collective-permute-start | bytes 1179656 | tf_op jit(solution)/shard_map/ppermute | solution.py:341
  43.4 10.8 %collective-permute-start.5 = (bf16[4,128,384]{2,1,0:T(8,128)(2,1)S(1)}, bf16[4,128,384]{2,1,0:T(8,128)(2,1)S(1)}, u32[]{:S(2)}, u32[]{:S(2)}) collective-permute-start(bf16[4,128,384]{2,1,0:T(8,128)(2,1)S(1)} %collective-permute-done.4), channel_id=1, source_target_pairs={{1,0},{2,3},{5,4},{6,7},{9,8},{10,11},{13,12},{14,15},{17,16},{18,... | collective-permute-start | bytes 1179656 | tf_op jit(solution)/shard_map/ppermute | solution.py:341
  44.7 16.4 %collective-permute-start.11 = (bf16[4,128,384]{2,1,0:T(8,128)(2,1)S(1)}, bf16[4,128,384]{2,1,0:T(8,128)(2,1)S(1)}, u32[]{:S(2)}, u32[]{:S(2)}) collective-permute-start(bf16[4,128,384]{2,1,0:T(8,128)(2,1)S(1)} %depthwise.3), channel_id=1, source_target_pairs={{0,1},{1,0},{2,3},{3,2},{4,5},{5,4},{6,7},{7,6},{8,9},{9,8},{10,11... | collective-permute-start | bytes 1179656 | tf_op jit(solution)/shard_map/ppermute | solution.py:333
  46.3 14.8 %collective-permute-start.12 = (bf16[4,128,384]{2,1,0:T(8,128)(2,1)S(1)}, bf16[4,128,384]{2,1,0:T(8,128)(2,1)S(1)}, u32[]{:S(2)}, u32[]{:S(2)}) collective-permute-start(bf16[4,128,384]{2,1,0:T(8,128)(2,1)S(1)} %depthwise.3), channel_id=1, source_target_pairs={{1,2},{2,1},{5,6},{6,5},{9,10},{10,9},{13,14},{14,13},{17,18},{18,... | collective-permute-start | bytes 1179656 | tf_op jit(solution)/shard_map/ppermute | solution.py:337
  49.6 14.5 %collective-permute-start.9 = (bf16[192,1536]{1,0:T(8,128)(2,1)S(1)}, bf16[192,1536]{1,0:T(8,128)(2,1)S(1)}, u32[]{:S(2)}, u32[]{:S(2)}) collective-permute-start(bf16[192,1536]{1,0:T(8,128)(2,1)S(1)} %slice.21), channel_id=1, source_target_pairs={{0,16},{4,20},{8,24},{12,28},{16,0},{20,4},{24,8},{28,12},{1,17},{... | collective-permute-start | bytes 1769480 | tf_op jit(solution)/shard_map/ppermute | solution.py:357
  51.2 14.4 %collective-permute-start.10 = (bf16[192,1536]{1,0:T(8,128)(2,1)S(1)}, bf16[192,1536]{1,0:T(8,128)(2,1)S(1)}, u32[]{:S(2)}, u32[]{:S(2)}) collective-permute-start(bf16[192,1536]{1,0:T(8,128)(2,1)S(1)} %slice.22), channel_id=1, source_target_pairs={{0,8},{4,12},{8,0},{12,4},{16,24},{20,28},{24,16},{28,20},{1,9},{5... | collective-permute-start | bytes 1769480 | tf_op jit(solution)/shard_map/ppermute | solution.py:357
  65.6 7.9 %collective-permute-start.13 = (bf16[1152,1536]{1,0:T(8,128)(2,1)S(1)}, bf16[1152,1536]{1,0:T(8,128)(2,1)S(1)}, u32[]{:S(2)}, u32[]{:S(2)}) collective-permute-start(bf16[1152,1536]{1,0:T(8,128)(2,1)S(1)} %pad_maximum_fusion), channel_id=1, source_target_pairs={{0,4},{4,0},{8,12},{12,8},{16,20},{20,16},{24,28},{28,24},{1,5},{5... | collective-permute-start | bytes 10616840 | tf_op jit(solution)/shard_map/ppermute | solution.py:357
  65.7 7.8 %collective-permute-start.14 = (bf16[384,1536]{1,0:T(8,128)(2,1)S(1)}, bf16[384,1536]{1,0:T(8,128)(2,1)S(1)}, u32[]{:S(2)}, u32[]{:S(2)}) collective-permute-start(bf16[384,1536]{1,0:T(8,128)(2,1)S(1)} %pad_maximum_fusion.2), channel_id=1, source_target_pairs={{0,4},{4,0},{8,12},{12,8},{16,20},{20,16},{24,28},{28,24},{1,5},{5... | collective-permute-start | bytes 3538952 | tf_op jit(solution)/shard_map/ppermute | solution.py:357
  66.3 12.9 %collective-permute-start.17 = (bf16[4,128,384]{2,1,0:T(8,128)(2,1)S(1)}, bf16[4,128,384]{2,1,0:T(8,128)(2,1)S(1)}, u32[]{:S(2)}, u32[]{:S(2)}) collective-permute-start(bf16[4,128,384]{2,1,0:T(8,128)(2,1)S(1)} %collective-permute-done.11), channel_id=1, source_target_pairs={{1,2},{2,1},{5,6},{6,5},{9,10},{10,9},{13,14},{14,13},{17,18},{18,... | collective-permute-start | bytes 1179656 | tf_op jit(solution)/shard_map/ppermute | solution.py:337
  69.8 16.3 %collective-permute-start.16 = (bf16[4,128,384]{2,1,0:T(8,128)(2,1)S(1)}, bf16[4,128,384]{2,1,0:T(8,128)(2,1)S(1)}, u32[]{:S(2)}, u32[]{:S(2)}) collective-permute-start(bf16[4,128,384]{2,1,0:T(8,128)(2,1)S(1)} %collective-permute-done.12), channel_id=1, source_target_pairs={{1,0},{2,3},{5,4},{6,7},{9,8},{10,11},{13,12},{14,15},{17,16},{18,... | collective-permute-start | bytes 1179656 | tf_op jit(solution)/shard_map/ppermute | solution.py:341
  79.3 9.6 %collective-permute-start.18 = (bf16[4,128,384]{2,1,0:T(8,128)(2,1)S(1)}, bf16[4,128,384]{2,1,0:T(8,128)(2,1)S(1)}, u32[]{:S(2)}, u32[]{:S(2)}) collective-permute-start(bf16[4,128,384]{2,1,0:T(8,128)(2,1)S(1)} %collective-permute-done.17), channel_id=1, source_target_pairs={{1,0},{2,3},{5,4},{6,7},{9,8},{10,11},{13,12},{14,15},{17,16},{18,... | collective-permute-start | bytes 1179656 | tf_op jit(solution)/shard_map/ppermute | solution.py:341
  80.6 18.4 %collective-permute-start.21 = (bf16[4,384,128]{2,1,0:T(8,128)(2,1)S(1)}, bf16[4,384,128]{2,1,0:T(8,128)(2,1)S(1)}, u32[]{:S(2)}, u32[]{:S(2)}) collective-permute-start(bf16[4,384,128]{2,1,0:T(8,128)(2,1)S(1)} %get-tuple-element.35), channel_id=1, source_target_pairs={{0,1},{3,2},{4,5},{7,6},{8,9},{11,10},{12,13},{15,14},{16,17},{19,... | collective-permute-start | bytes 1179656 | tf_op jit(solution)/shard_map/ppermute | solution.py:345
  84.8 18.5 %collective-permute-start.15 = (bf16[4,384,128]{2,1,0:T(8,128)(2,1)S(1)}, bf16[4,384,128]{2,1,0:T(8,128)(2,1)S(1)}, u32[]{:S(2)}, u32[]{:S(2)}) collective-permute-start(bf16[4,384,128]{2,1,0:T(8,128)(2,1)S(1)} %get-tuple-element.32), channel_id=1, source_target_pairs={{0,1},{3,2},{4,5},{7,6},{8,9},{11,10},{12,13},{15,14},{16,17},{19,... | collective-permute-start | bytes 1179656 | tf_op jit(solution)/shard_map/ppermute | solution.py:345
  97.7 13.9 %collective-permute-start.19 = (bf16[4,384,128]{2,1,0:T(8,128)(2,1)S(1)}, bf16[4,384,128]{2,1,0:T(8,128)(2,1)S(1)}, u32[]{:S(2)}, u32[]{:S(2)}) collective-permute-start(bf16[4,384,128]{2,1,0:T(8,128)(2,1)S(1)} %get-tuple-element.37), channel_id=1, source_target_pairs={{0,1},{3,2},{4,5},{7,6},{8,9},{11,10},{12,13},{15,14},{16,17},{19,... | collective-permute-start | bytes 1179656 | tf_op jit(solution)/shard_map/ppermute | solution.py:345
  99.1 15.5 %collective-permute-start.22 = (bf16[4,384,128]{2,1,0:T(8,128)(2,1)S(1)}, bf16[4,384,128]{2,1,0:T(8,128)(2,1)S(1)}, u32[]{:S(2)}, u32[]{:S(2)}) collective-permute-start(bf16[4,384,128]{2,1,0:T(8,128)(2,1)S(1)} %add_convert_fusion.5), channel_id=1, source_target_pairs={{1,2},{2,1},{5,6},{6,5},{9,10},{10,9},{13,14},{14,13},{17,18},{18,... | collective-permute-start | bytes 1179656 | tf_op jit(solution)/shard_map/ppermute | solution.py:337
  102.0 18.1 %collective-permute-start.24 = (bf16[4,384,128]{2,1,0:T(8,128)(2,1)S(1)}, bf16[4,384,128]{2,1,0:T(8,128)(2,1)S(1)}, u32[]{:S(2)}, u32[]{:S(2)}) collective-permute-start(bf16[4,384,128]{2,1,0:T(8,128)(2,1)S(1)} %get-tuple-element.41), channel_id=1, source_target_pairs={{0,1},{3,2},{4,5},{7,6},{8,9},{11,10},{12,13},{15,14},{16,17},{19,... | collective-permute-start | bytes 1179656 | tf_op jit(solution)/shard_map/ppermute | solution.py:345
  103.4 34.6 %copy-start.7 = (f32[384]{0:T(512)S(1)}, f32[384]{0:T(512)}, u32[]{:S(2)}) copy-start(f32[384]{0:T(512)} %param.18) | copy-start | bytes 4612
  103.4 34.6 %copy-start.8 = (f32[384]{0:T(512)S(1)}, f32[384]{0:T(512)}, u32[]{:S(2)}) copy-start(f32[384]{0:T(512)} %param.19) | copy-start | bytes 4612
  111.8 13.9 %collective-permute-start.26 = (bf16[4,384,128]{2,1,0:T(8,128)(2,1)S(1)}, bf16[4,384,128]{2,1,0:T(8,128)(2,1)S(1)}, u32[]{:S(2)}, u32[]{:S(2)}) collective-permute-start(bf16[4,384,128]{2,1,0:T(8,128)(2,1)S(1)} %add_convert_fusion.6), channel_id=1, source_target_pairs={{1,2},{2,1},{5,6},{6,5},{9,10},{10,9},{13,14},{14,13},{17,18},{18,... | collective-permute-start | bytes 1179656 | tf_op jit(solution)/shard_map/ppermute | solution.py:337
  115.5 13.0 %collective-permute-start.23 = (bf16[4,384,128]{2,1,0:T(8,128)(2,1)}, bf16[4,384,128]{2,1,0:T(8,128)(2,1)S(1)}, u32[]{:S(2)}, u32[]{:S(2)}) collective-permute-start(bf16[4,384,128]{2,1,0:T(8,128)(2,1)} %add_convert_fusion.4), channel_id=1, source_target_pairs={{0,1},{1,0},{2,3},{3,2},{4,5},{5,4},{6,7},{7,6},{8,9},{9,8},{10,11... | collective-permute-start | bytes 1179656 | tf_op jit(solution)/shard_map/ppermute | solution.py:333
  115.5 18.3 %collective-permute-start.20 = (bf16[4,384,128]{2,1,0:T(8,128)(2,1)S(1)}, bf16[4,384,128]{2,1,0:T(8,128)(2,1)S(1)}, u32[]{:S(2)}, u32[]{:S(2)}) collective-permute-start(bf16[4,384,128]{2,1,0:T(8,128)(2,1)S(1)} %add_convert_fusion.7), channel_id=1, source_target_pairs={{1,2},{2,1},{5,6},{6,5},{9,10},{10,9},{13,14},{14,13},{17,18},{18,... | collective-permute-start | bytes 1179656 | tf_op jit(solution)/shard_map/ppermute | solution.py:337
  120.9 17.1 %collective-permute-start.25 = (bf16[4,384,128]{2,1,0:T(8,128)(2,1)}, bf16[4,384,128]{2,1,0:T(8,128)(2,1)S(1)}, u32[]{:S(2)}, u32[]{:S(2)}) collective-permute-start(bf16[4,384,128]{2,1,0:T(8,128)(2,1)} %add_convert_fusion.2), channel_id=1, source_target_pairs={{1,2},{2,1},{5,6},{6,5},{9,10},{10,9},{13,14},{14,13},{17,18},{18,... | collective-permute-start | bytes 1179656 | tf_op jit(solution)/shard_map/ppermute | solution.py:337
  126.5 11.5 %collective-permute-start.27 = (bf16[4,384,128]{2,1,0:T(8,128)(2,1)}, bf16[4,384,128]{2,1,0:T(8,128)(2,1)S(1)}, u32[]{:S(2)}, u32[]{:S(2)}) collective-permute-start(bf16[4,384,128]{2,1,0:T(8,128)(2,1)} %add_convert_fusion.1), channel_id=1, source_target_pairs={{0,1},{1,0},{2,3},{3,2},{4,5},{5,4},{6,7},{7,6},{8,9},{9,8},{10,11... | collective-permute-start | bytes 1179656 | tf_op jit(solution)/shard_map/ppermute | solution.py:333
  (6 other events, 84.5 us)
